TPU v7x, 32 devices: a whole 2x2x4 slice. The times are simulated.
32 devices in a mesh: row: 8 (over y, x, core), col: 4 (over z).
Axes of the slice: x: 2, y: 2, z: 4, core: 2. Of those that a mesh axis runs over, the one named last changes fastest.
Arguments:
- row_points: bfloat16 [2048, 64], P(('row', 'col')), may hold values from -6 to 6, as said below
- col_points: bfloat16 [16384, 64], P(('col', 'row')), may hold values from -6 to 6, as said below
- row_vectors: bfloat16 [2048, 64], P(('row', 'col')), may hold values from -1 to 1
- col_vectors: bfloat16 [16384, 64], P(('col', 'row')), may hold values from -0.375 to 0.375
- weight_in: bfloat16 [64, 512], replicated, may hold values from -0.75 to 0.75
- bias_in: float32 [512], replicated, may hold values from -3 to 3
- weight_mid: bfloat16 [512, 512], replicated, may hold values from -0.75 to 0.75
- bias_mid: float32 [512], replicated, may hold values from -3 to 3
- weight_out: bfloat16 [512, 256], replicated, may hold values from -0.75 to 0.75
- ard_scales: float32 [256], replicated, may hold values from 0.002 to 0.01
- signal_scale: float32 [1], replicated, may hold values from 0.5 to 2
Outputs:
- row_result: float32 [2048, 64], P(('row', 'col'))
- col_result: float32 [16384, 64], P(('col', 'row'))
Inputs may be any that keep to these rules, and one draw needn't show every extreme that they name: `row_points`: each row point's input lies near one of 64 centres that row and column points share; which centre is not given. `col_points`: each column point's input lies near one of the same 64 centres; which centre is not given.
All inputs are finite; a program needn't handle non-finite values.
Results may differ from a plain program's by a relative error of at most 0.0041.
Values may be sent and summed in bfloat16 or wider, within the bound.
No kernel may reach another device: no remote copies, remote signals or barrier semaphores. Data moves between devices by JAX's collectives and lax.ppermute only.
A program may use at most 64 MiB of HBM per device.

v0:
```python
import math

import jax
import jax.numpy as jnp
from jax import lax
from jax.sharding import PartitionSpec as P


def from_behind(block, axis, distance):
    devices = range(lax.axis_size(axis))
    route = [((i - distance) % len(devices), i) for i in devices]
    return lax.ppermute(block, axis, route)


def embed_points(points, weight_in, bias_in, weight_mid, bias_mid, weight_out, ard_scales):
    hidden_one = jnp.tanh(
        jnp.dot(points, weight_in, preferred_element_type=jnp.float32) + bias_in
    ).astype(jnp.bfloat16)
    hidden_two = jnp.tanh(
        jnp.dot(hidden_one, weight_mid, preferred_element_type=jnp.float32) + bias_mid
    ).astype(jnp.bfloat16)
    return (
        jnp.dot(hidden_two, weight_out, preferred_element_type=jnp.float32) * jnp.sqrt(ard_scales)
    ).astype(jnp.bfloat16)


def body(
    row_points,
    col_points,
    row_vectors,
    col_vectors,
    weight_in,
    bias_in,
    weight_mid,
    bias_mid,
    weight_out,
    ard_scales,
    signal_scale,
):
    row_feats = embed_points(
        row_points, weight_in, bias_in, weight_mid, bias_mid, weight_out, ard_scales
    )
    rows_all, row_vecs_all = (
        lax.all_gather(row_feats, "col", axis=0, tiled=True),
        lax.all_gather(row_vectors, "col", axis=0, tiled=True),
    )
    row_sq = jnp.sum(jnp.square(rows_all.astype(jnp.float32)), axis=1)
    count_vecs = row_vectors.shape[1]

    def tile_block(totals, features, vectors):
        count_cols = features.shape[0]
        step_rows = math.gcd(count_cols, 512)

        def visit(number, state):
            row_acc, col_acc = state
            squares_now = jnp.sum(jnp.square(features.astype(jnp.float32)), axis=1)
            inner_prod = lax.dot_general(
                rows_all, features, (((1,), (1,)), ((), ())), preferred_element_type=jnp.float32
            )
            kernel = jnp.exp(
                inner_prod - 0.5 * row_sq[:, None] - 0.5 * squares_now[None, :]
            ).astype(jnp.bfloat16)
            row_acc = row_acc + jnp.dot(kernel, vectors, preferred_element_type=jnp.float32)
            col_part = lax.dot_general(
                kernel, row_vecs_all, (((0,), (0,)), ((), ())), preferred_element_type=jnp.float32
            )
            col_acc = col_part
            return (row_acc, col_acc)

        return lax.fori_loop(0, count_cols // step_rows, visit, totals)

    row_start = jnp.zeros((rows_all.shape[0], count_vecs), jnp.float32)
    col_feats = embed_points(
        col_points, weight_in, bias_in, weight_mid, bias_mid, weight_out, ard_scales
    )
    sums_start = jnp.zeros((col_points.shape[0], count_vecs), jnp.float32)

    def travel_step(number, state):
        row_acc, feats_here, vecs_here, sums_here = state
        row_acc, col_part = tile_block((row_acc, jnp.zeros_like(sums_here)), feats_here, vecs_here)
        sums_here = from_behind(sums_here + col_part, "row", 1)
        feats_here, vecs_here = from_behind((feats_here, vecs_here), "row", 1)
        return (row_acc, feats_here, vecs_here, sums_here)

    row_acc, unused_feats, unused_vecs, col_sums = lax.fori_loop(
        0, lax.axis_size("row"), travel_step, (row_start, col_feats, col_vectors, sums_start)
    )
    col_result = col_sums * signal_scale[0]
    row_result = lax.psum_scatter(row_acc, "col", scatter_dimension=0, tiled=True) * signal_scale[0]
    return (row_result, col_result)


def solution(mesh):
    in_specs = (
        P(("row", "col"), None),
        P(("col", "row"), None),
        P(("row", "col"), None),
        P(("col", "row"), None),
        P(),
        P(),
        P(),
        P(),
        P(),
        P(),
        P(),
    )
    out_specs = (P(("row", "col"), None), P(("col", "row"), None))
    return jax.shard_map(body, mesh=mesh, in_specs=in_specs, out_specs=out_specs, check_vma=False)
```

profile of v0, /device:TPU:0, one launch (start us, length us, event | category | flops | bytes accessed | tf_op | source)
XLA Modules:
  0.0 140.2 jit_solution(6331707783850708729)
XLA Ops:
  7.3 0.7 copy-done.8
  8.0 0.2 copy-done
  8.3 0.3 fusion.12
  8.6 0.6 copy-done.2
  9.4 15.1 %all_gather.6 = bf16[256,256]{1,0:T(8,128)(2,1)S(1)} all-gather(bf16[64,256]{1,0:T(8,128)(2,1)S(1)} %fusion.14), channel_id=1, replica_groups=mesh['row'=8,'col'=4] {'col'}, dimensions={0}, use_global_device_ids=true | all-gather | bytes 163840 | tf_op jit(solution)/shard_map/all_gather | solution.py:44
  24.5 0.7 copy-done.9
  25.3 0.3 fusion.5
  25.6 0.7 fusion.9
  26.3 13.2 %all_gather.7 = bf16[256,64]{1,0:T(8,128)(2,1)S(1)} all-gather(bf16[64,64]{1,0:T(8,128)(2,1)S(1)} %copy-done.4), channel_id=1, replica_groups=mesh['row'=8,'col'=4] {'col'}, dimensions={0}, use_global_device_ids=true | all-gather | bytes 40960 | tf_op jit(solution)/shard_map/all_gather | solution.py:45
  39.6 0.8 copy-done.1
  40.4 71.1 %while.15 = (s32[]{:T(128)}, f32[256,64]{0,1:T(8,128)S(1)}, bf16[512,256]{1,0:T(8,128)(2,1)S(1)}, bf16[512,64]{0,1:T(8,128)(2,1)S(1)}, f32[512,64]{0,1:T(8,128)S...) while((s32[]{:T(128)}, f32[256,64]{0,1:T(8,128)S(1)}, ...), condition=%wide.region_3.4_spmd.clone, body=%wide.region_1.3_spmd.clone.sunk | while | flops 101515520 | bytes 4435175 | solution.py:85
  40.6 0.3 fusion.46
  40.9 0.2 convolution_add_fusion.9
  41.1 1.6 %collective-permute-start.2 = (f32[512,64]{0,1:T(8,128)S(1)}, f32[512,64]{0,1:T(8,128)S(1)}, u32[]{:S(2)}, u32[]{:S(2)}) collective-permute-start(f32[512,64]{0,1:T(8,128)S(1)} %convolution_add_fusion.9), channel_id=1, source_target_pairs={{28,0},{0,4},{4,8},{8,12},{12,16},{16,20},{20,24},{24,28},{29,1},{... | collective-permute-start | bytes 393224 | tf_op jit(solution)/shard_map/while/body/eval_jaxpr/ppermute | solution.py:12
  42.9 0.2 convolution_add_fusion.8
  43.1 6.2 %collective-permute-done.1 = bf16[512,64]{0,1:T(8,128)(2,1)S(1)} collective-permute-done((bf16[512,64]{0,1:T(8,128)(2,1)S(1)}, bf16[512,64]{0,1:T(8,128)(2,1)S(1)}, u32[]{:S(2)}, u32[]{:S(2)}) %collective-permute-start.1) | collective-permute-done | bytes 65568 | tf_op jit(solution)/shard_map/while/body/eval_jaxpr/ppermute | solution.py:12
  49.5 0.3 fusion.46
  49.8 0.2 convolution_add_fusion.9
  50.0 0.7 collective-permute-start.2
  50.8 0.2 convolution_add_fusion.8
  51.1 7.1 %collective-permute-done.1 = bf16[512,64]{0,1:T(8,128)(2,1)S(1)} collective-permute-done((bf16[512,64]{0,1:T(8,128)(2,1)S(1)}, bf16[512,64]{0,1:T(8,128)(2,1)S(1)}, u32[]{:S(2)}, u32[]{:S(2)}) %collective-permute-start.1) | collective-permute-done | bytes 65568 | tf_op jit(solution)/shard_map/while/body/eval_jaxpr/ppermute | solution.py:12
  58.4 0.3 fusion.46
  58.7 0.2 convolution_add_fusion.9
  59.0 0.2 convolution_add_fusion.8
  59.3 7.8 %collective-permute-done.1 = bf16[512,64]{0,1:T(8,128)(2,1)S(1)} collective-permute-done((bf16[512,64]{0,1:T(8,128)(2,1)S(1)}, bf16[512,64]{0,1:T(8,128)(2,1)S(1)}, u32[]{:S(2)}, u32[]{:S(2)}) %collective-permute-start.1) | collective-permute-done | bytes 65568 | tf_op jit(solution)/shard_map/while/body/eval_jaxpr/ppermute | solution.py:12
  67.3 0.3 fusion.46
  67.9 0.2 convolution_add_fusion.8
  68.2 7.8 %collective-permute-done.1 = bf16[512,64]{0,1:T(8,128)(2,1)S(1)} collective-permute-done((bf16[512,64]{0,1:T(8,128)(2,1)S(1)}, bf16[512,64]{0,1:T(8,128)(2,1)S(1)}, u32[]{:S(2)}, u32[]{:S(2)}) %collective-permute-start.1) | collective-permute-done | bytes 65568 | tf_op jit(solution)/shard_map/while/body/eval_jaxpr/ppermute | solution.py:12
  76.2 0.3 fusion.46
  76.5 0.2 convolution_add_fusion.9
  76.8 0.2 convolution_add_fusion.8
  77.1 7.7 %collective-permute-done.1 = bf16[512,64]{0,1:T(8,128)(2,1)S(1)} collective-permute-done((bf16[512,64]{0,1:T(8,128)(2,1)S(1)}, bf16[512,64]{0,1:T(8,128)(2,1)S(1)}, u32[]{:S(2)}, u32[]{:S(2)}) %collective-permute-start.1) | collective-permute-done | bytes 65568 | tf_op jit(solution)/shard_map/while/body/eval_jaxpr/ppermute | solution.py:12
  85.1 0.3 fusion.46
  85.4 0.2 convolution_add_fusion.9
  85.7 0.2 convolution_add_fusion.8
  85.9 7.7 %collective-permute-done.1 = bf16[512,64]{0,1:T(8,128)(2,1)S(1)} collective-permute-done((bf16[512,64]{0,1:T(8,128)(2,1)S(1)}, bf16[512,64]{0,1:T(8,128)(2,1)S(1)}, u32[]{:S(2)}, u32[]{:S(2)}) %collective-permute-start.1) | collective-permute-done | bytes 65568 | tf_op jit(solution)/shard_map/while/body/eval_jaxpr/ppermute | solution.py:12
  94.0 0.3 fusion.46
  94.2 0.2 convolution_add_fusion.9
  94.6 0.2 convolution_add_fusion.8
  94.8 7.7 %collective-permute-done.1 = bf16[512,64]{0,1:T(8,128)(2,1)S(1)} collective-permute-done((bf16[512,64]{0,1:T(8,128)(2,1)S(1)}, bf16[512,64]{0,1:T(8,128)(2,1)S(1)}, u32[]{:S(2)}, u32[]{:S(2)}) %collective-permute-start.1) | collective-permute-done | bytes 65568 | tf_op jit(solution)/shard_map/while/body/eval_jaxpr/ppermute | solution.py:12
  102.8 0.3 fusion.46
  103.1 0.2 convolution_add_fusion.9
  103.5 0.2 convolution_add_fusion.8
  103.7 7.7 %collective-permute-done.1 = bf16[512,64]{0,1:T(8,128)(2,1)S(1)} collective-permute-done((bf16[512,64]{0,1:T(8,128)(2,1)S(1)}, bf16[512,64]{0,1:T(8,128)(2,1)S(1)}, u32[]{:S(2)}, u32[]{:S(2)}) %collective-permute-start.1) | collective-permute-done | bytes 65568 | tf_op jit(solution)/shard_map/while/body/eval_jaxpr/ppermute | solution.py:12
  111.5 0.8 copy.13
  112.9 0.7 broadcast_multiply_fusion.2
  113.6 18.4 %reduce-scatter.2.cloned.1.call-done = f32[64,64]{1,0:T(8,128)} async-done(((f32[256,64]{1,0:T(8,128)}), f32[64,64]{1,0:T(8,128)}) %reduce-scatter.2.cloned.1.call-update) | async-done | bytes 16400 | tf_op jit(solution)/shard_map/reduce_scatter | solution.py:89
  131.9 1.4 broadcast_multiply_fusion.3
  (101 shorter events, 3.4 us)
Async XLA Ops:
  7.2 1.1 copy-start
  7.2 1.1 copy-start.5
  7.2 1.0 copy-start.3
  7.2 124.7 %reduce-scatter.2.cloned.1.call-start = ((), (), s32[]{:S(2)}) async-start(), calls=%async_computation.1 | async-start | bytes 163840 | tf_op jit(solution)/shard_map/reduce_scatter | solution.py:89
  7.2 0.7 copy-start.8
  7.3 1.0 copy-start.7
  7.3 1.0 copy-start.6
  8.2 1.0 copy-start.2
  24.4 0.8 copy-start.9
  25.6 0.7 copy-start.4
  39.5 0.8 copy-start.1
  40.4 8.9 %collective-permute-start = (bf16[512,256]{1,0:T(8,128)(2,1)S(1)}, bf16[512,256]{1,0:T(8,128)(2,1)S(1)}, u32[]{:S(2)}, u32[]{:S(2)}) collective-permute-start(bf16[512,256]{1,0:T(8,128)(2,1)S(1)} %copy.21), channel_id=1, source_target_pairs={{28,0},{0,4},{4,8},{8,12},{12,16},{16,20},{20,24},{24,28},{29,1},{... | collective-permute-start | bytes 786440 | tf_op jit(solution)/shard_map/while/body/eval_jaxpr/ppermute | solution.py:12
  41.1 8.1 %collective-permute-start.2 = (f32[512,64]{0,1:T(8,128)S(1)}, f32[512,64]{0,1:T(8,128)S(1)}, u32[]{:S(2)}, u32[]{:S(2)}) collective-permute-start(f32[512,64]{0,1:T(8,128)S(1)} %convolution_add_fusion.9), channel_id=1, source_target_pairs={{28,0},{0,4},{4,8},{8,12},{12,16},{16,20},{20,24},{24,28},{29,1},{... | collective-permute-start | bytes 393224 | tf_op jit(solution)/shard_map/while/body/eval_jaxpr/ppermute | solution.py:12
  42.8 6.5 %collective-permute-start.1 = (bf16[512,64]{0,1:T(8,128)(2,1)S(1)}, bf16[512,64]{0,1:T(8,128)(2,1)S(1)}, u32[]{:S(2)}, u32[]{:S(2)}) collective-permute-start(bf16[512,64]{0,1:T(8,128)(2,1)S(1)} %copy.22), channel_id=1, source_target_pairs={{28,0},{0,4},{4,8},{8,12},{12,16},{16,20},{20,24},{24,28},{29,1},{... | collective-permute-start | bytes 196616 | tf_op jit(solution)/shard_map/while/body/eval_jaxpr/ppermute | solution.py:12
  49.3 8.9 %collective-permute-start = (bf16[512,256]{1,0:T(8,128)(2,1)S(1)}, bf16[512,256]{1,0:T(8,128)(2,1)S(1)}, u32[]{:S(2)}, u32[]{:S(2)}) collective-permute-start(bf16[512,256]{1,0:T(8,128)(2,1)S(1)} %copy.21), channel_id=1, source_target_pairs={{28,0},{0,4},{4,8},{8,12},{12,16},{16,20},{20,24},{24,28},{29,1},{... | collective-permute-start | bytes 786440 | tf_op jit(solution)/shard_map/while/body/eval_jaxpr/ppermute | solution.py:12
  50.0 8.1 %collective-permute-start.2 = (f32[512,64]{0,1:T(8,128)S(1)}, f32[512,64]{0,1:T(8,128)S(1)}, u32[]{:S(2)}, u32[]{:S(2)}) collective-permute-start(f32[512,64]{0,1:T(8,128)S(1)} %convolution_add_fusion.9), channel_id=1, source_target_pairs={{28,0},{0,4},{4,8},{8,12},{12,16},{16,20},{20,24},{24,28},{29,1},{... | collective-permute-start | bytes 393224 | tf_op jit(solution)/shard_map/while/body/eval_jaxpr/ppermute | solution.py:12
  50.8 7.4 %collective-permute-start.1 = (bf16[512,64]{0,1:T(8,128)(2,1)S(1)}, bf16[512,64]{0,1:T(8,128)(2,1)S(1)}, u32[]{:S(2)}, u32[]{:S(2)}) collective-permute-start(bf16[512,64]{0,1:T(8,128)(2,1)S(1)} %copy.22), channel_id=1, source_target_pairs={{28,0},{0,4},{4,8},{8,12},{12,16},{16,20},{20,24},{24,28},{29,1},{... | collective-permute-start | bytes 196616 | tf_op jit(solution)/shard_map/while/body/eval_jaxpr/ppermute | solution.py:12
  58.2 8.9 %collective-permute-start = (bf16[512,256]{1,0:T(8,128)(2,1)S(1)}, bf16[512,256]{1,0:T(8,128)(2,1)S(1)}, u32[]{:S(2)}, u32[]{:S(2)}) collective-permute-start(bf16[512,256]{1,0:T(8,128)(2,1)S(1)} %copy.21), channel_id=1, source_target_pairs={{28,0},{0,4},{4,8},{8,12},{12,16},{16,20},{20,24},{24,28},{29,1},{... | collective-permute-start | bytes 786440 | tf_op jit(solution)/shard_map/while/body/eval_jaxpr/ppermute | solution.py:12
  58.9 8.1 %collective-permute-start.2 = (f32[512,64]{0,1:T(8,128)S(1)}, f32[512,64]{0,1:T(8,128)S(1)}, u32[]{:S(2)}, u32[]{:S(2)}) collective-permute-start(f32[512,64]{0,1:T(8,128)S(1)} %convolution_add_fusion.9), channel_id=1, source_target_pairs={{28,0},{0,4},{4,8},{8,12},{12,16},{16,20},{20,24},{24,28},{29,1},{... | collective-permute-start | bytes 393224 | tf_op jit(solution)/shard_map/while/body/eval_jaxpr/ppermute | solution.py:12
  59.0 8.0 %collective-permute-start.1 = (bf16[512,64]{0,1:T(8,128)(2,1)S(1)}, bf16[512,64]{0,1:T(8,128)(2,1)S(1)}, u32[]{:S(2)}, u32[]{:S(2)}) collective-permute-start(bf16[512,64]{0,1:T(8,128)(2,1)S(1)} %copy.22), channel_id=1, source_target_pairs={{28,0},{0,4},{4,8},{8,12},{12,16},{16,20},{20,24},{24,28},{29,1},{... | collective-permute-start | bytes 196616 | tf_op jit(solution)/shard_map/while/body/eval_jaxpr/ppermute | solution.py:12
  67.1 8.9 %collective-permute-start = (bf16[512,256]{1,0:T(8,128)(2,1)S(1)}, bf16[512,256]{1,0:T(8,128)(2,1)S(1)}, u32[]{:S(2)}, u32[]{:S(2)}) collective-permute-start(bf16[512,256]{1,0:T(8,128)(2,1)S(1)} %copy.21), channel_id=1, source_target_pairs={{28,0},{0,4},{4,8},{8,12},{12,16},{16,20},{20,24},{24,28},{29,1},{... | collective-permute-start | bytes 786440 | tf_op jit(solution)/shard_map/while/body/eval_jaxpr/ppermute | solution.py:12
  67.8 8.1 %collective-permute-start.2 = (f32[512,64]{0,1:T(8,128)S(1)}, f32[512,64]{0,1:T(8,128)S(1)}, u32[]{:S(2)}, u32[]{:S(2)}) collective-permute-start(f32[512,64]{0,1:T(8,128)S(1)} %convolution_add_fusion.9), channel_id=1, source_target_pairs={{28,0},{0,4},{4,8},{8,12},{12,16},{16,20},{20,24},{24,28},{29,1},{... | collective-permute-start | bytes 393224 | tf_op jit(solution)/shard_map/while/body/eval_jaxpr/ppermute | solution.py:12
  67.9 8.0 %collective-permute-start.1 = (bf16[512,64]{0,1:T(8,128)(2,1)S(1)}, bf16[512,64]{0,1:T(8,128)(2,1)S(1)}, u32[]{:S(2)}, u32[]{:S(2)}) collective-permute-start(bf16[512,64]{0,1:T(8,128)(2,1)S(1)} %copy.22), channel_id=1, source_target_pairs={{28,0},{0,4},{4,8},{8,12},{12,16},{16,20},{20,24},{24,28},{29,1},{... | collective-permute-start | bytes 196616 | tf_op jit(solution)/shard_map/while/body/eval_jaxpr/ppermute | solution.py:12
  75.9 8.9 %collective-permute-start = (bf16[512,256]{1,0:T(8,128)(2,1)S(1)}, bf16[512,256]{1,0:T(8,128)(2,1)S(1)}, u32[]{:S(2)}, u32[]{:S(2)}) collective-permute-start(bf16[512,256]{1,0:T(8,128)(2,1)S(1)} %copy.21), channel_id=1, source_target_pairs={{28,0},{0,4},{4,8},{8,12},{12,16},{16,20},{20,24},{24,28},{29,1},{... | collective-permute-start | bytes 786440 | tf_op jit(solution)/shard_map/while/body/eval_jaxpr/ppermute | solution.py:12
  76.7 8.1 %collective-permute-start.2 = (f32[512,64]{0,1:T(8,128)S(1)}, f32[512,64]{0,1:T(8,128)S(1)}, u32[]{:S(2)}, u32[]{:S(2)}) collective-permute-start(f32[512,64]{0,1:T(8,128)S(1)} %convolution_add_fusion.9), channel_id=1, source_target_pairs={{28,0},{0,4},{4,8},{8,12},{12,16},{16,20},{20,24},{24,28},{29,1},{... | collective-permute-start | bytes 393224 | tf_op jit(solution)/shard_map/while/body/eval_jaxpr/ppermute | solution.py:12
  76.8 8.0 %collective-permute-start.1 = (bf16[512,64]{0,1:T(8,128)(2,1)S(1)}, bf16[512,64]{0,1:T(8,128)(2,1)S(1)}, u32[]{:S(2)}, u32[]{:S(2)}) collective-permute-start(bf16[512,64]{0,1:T(8,128)(2,1)S(1)} %copy.22), channel_id=1, source_target_pairs={{28,0},{0,4},{4,8},{8,12},{12,16},{16,20},{20,24},{24,28},{29,1},{... | collective-permute-start | bytes 196616 | tf_op jit(solution)/shard_map/while/body/eval_jaxpr/ppermute | solution.py:12
  84.8 8.9 %collective-permute-start = (bf16[512,256]{1,0:T(8,128)(2,1)S(1)}, bf16[512,256]{1,0:T(8,128)(2,1)S(1)}, u32[]{:S(2)}, u32[]{:S(2)}) collective-permute-start(bf16[512,256]{1,0:T(8,128)(2,1)S(1)} %copy.21), channel_id=1, source_target_pairs={{28,0},{0,4},{4,8},{8,12},{12,16},{16,20},{20,24},{24,28},{29,1},{... | collective-permute-start | bytes 786440 | tf_op jit(solution)/shard_map/while/body/eval_jaxpr/ppermute | solution.py:12
  85.6 8.1 %collective-permute-start.2 = (f32[512,64]{0,1:T(8,128)S(1)}, f32[512,64]{0,1:T(8,128)S(1)}, u32[]{:S(2)}, u32[]{:S(2)}) collective-permute-start(f32[512,64]{0,1:T(8,128)S(1)} %convolution_add_fusion.9), channel_id=1, source_target_pairs={{28,0},{0,4},{4,8},{8,12},{12,16},{16,20},{20,24},{24,28},{29,1},{... | collective-permute-start | bytes 393224 | tf_op jit(solution)/shard_map/while/body/eval_jaxpr/ppermute | solution.py:12
  85.6 8.0 %collective-permute-start.1 = (bf16[512,64]{0,1:T(8,128)(2,1)S(1)}, bf16[512,64]{0,1:T(8,128)(2,1)S(1)}, u32[]{:S(2)}, u32[]{:S(2)}) collective-permute-start(bf16[512,64]{0,1:T(8,128)(2,1)S(1)} %copy.22), channel_id=1, source_target_pairs={{28,0},{0,4},{4,8},{8,12},{12,16},{16,20},{20,24},{24,28},{29,1},{... | collective-permute-start | bytes 196616 | tf_op jit(solution)/shard_map/while/body/eval_jaxpr/ppermute | solution.py:12
  93.7 8.9 %collective-permute-start = (bf16[512,256]{1,0:T(8,128)(2,1)S(1)}, bf16[512,256]{1,0:T(8,128)(2,1)S(1)}, u32[]{:S(2)}, u32[]{:S(2)}) collective-permute-start(bf16[512,256]{1,0:T(8,128)(2,1)S(1)} %copy.21), channel_id=1, source_target_pairs={{28,0},{0,4},{4,8},{8,12},{12,16},{16,20},{20,24},{24,28},{29,1},{... | collective-permute-start | bytes 786440 | tf_op jit(solution)/shard_map/while/body/eval_jaxpr/ppermute | solution.py:12
  94.5 8.1 %collective-permute-start.2 = (f32[512,64]{0,1:T(8,128)S(1)}, f32[512,64]{0,1:T(8,128)S(1)}, u32[]{:S(2)}, u32[]{:S(2)}) collective-permute-start(f32[512,64]{0,1:T(8,128)S(1)} %convolution_add_fusion.9), channel_id=1, source_target_pairs={{28,0},{0,4},{4,8},{8,12},{12,16},{16,20},{20,24},{24,28},{29,1},{... | collective-permute-start | bytes 393224 | tf_op jit(solution)/shard_map/while/body/eval_jaxpr/ppermute | solution.py:12
  94.5 8.0 %collective-permute-start.1 = (bf16[512,64]{0,1:T(8,128)(2,1)S(1)}, bf16[512,64]{0,1:T(8,128)(2,1)S(1)}, u32[]{:S(2)}, u32[]{:S(2)}) collective-permute-start(bf16[512,64]{0,1:T(8,128)(2,1)S(1)} %copy.22), channel_id=1, source_target_pairs={{28,0},{0,4},{4,8},{8,12},{12,16},{16,20},{20,24},{24,28},{29,1},{... | collective-permute-start | bytes 196616 | tf_op jit(solution)/shard_map/while/body/eval_jaxpr/ppermute | solution.py:12
  102.6 8.9 %collective-permute-start = (bf16[512,256]{1,0:T(8,128)(2,1)S(1)}, bf16[512,256]{1,0:T(8,128)(2,1)S(1)}, u32[]{:S(2)}, u32[]{:S(2)}) collective-permute-start(bf16[512,256]{1,0:T(8,128)(2,1)S(1)} %copy.21), channel_id=1, source_target_pairs={{28,0},{0,4},{4,8},{8,12},{12,16},{16,20},{20,24},{24,28},{29,1},{... | collective-permute-start | bytes 786440 | tf_op jit(solution)/shard_map/while/body/eval_jaxpr/ppermute | solution.py:12
  103.3 8.1 %collective-permute-start.2 = (f32[512,64]{0,1:T(8,128)S(1)}, f32[512,64]{0,1:T(8,128)S(1)}, u32[]{:S(2)}, u32[]{:S(2)}) collective-permute-start(f32[512,64]{0,1:T(8,128)S(1)} %convolution_add_fusion.9), channel_id=1, source_target_pairs={{28,0},{0,4},{4,8},{8,12},{12,16},{16,20},{20,24},{24,28},{29,1},{... | collective-permute-start | bytes 393224 | tf_op jit(solution)/shard_map/while/body/eval_jaxpr/ppermute | solution.py:12
  103.4 8.0 %collective-permute-start.1 = (bf16[512,64]{0,1:T(8,128)(2,1)S(1)}, bf16[512,64]{0,1:T(8,128)(2,1)S(1)}, u32[]{:S(2)}, u32[]{:S(2)}) collective-permute-start(bf16[512,64]{0,1:T(8,128)(2,1)S(1)} %copy.22), channel_id=1, source_target_pairs={{28,0},{0,4},{4,8},{8,12},{12,16},{16,20},{20,24},{24,28},{29,1},{... | collective-permute-start | bytes 196616 | tf_op jit(solution)/shard_map/while/body/eval_jaxpr/ppermute | solution.py:12
Sparse Core Ops, SparseCore 0:
  112.4 19.5 reduce-scatter.1
where the time goes:
time: 141 us; the launch traced here: 140 us
  waiting for transfers between devices  78.2 us (55%)
  blocking collectives  28.3 us (20%)
  between operations  14.8 us (10%)
  matrix products  7.15 us (5%)
  local copies, waits for them, and re-layouts  4.1 us (3%)
  starting transfers between devices  3.7 us (3%)
  other arithmetic  3.4 us (2%)
    ppermute x24, waiting for transfers between devices, from_behind(): return lax.ppermute(block, axis, route)  59.8 us
    reduce_scatter x1, waiting for transfers between devices, body(): lax.psum_scatter(row_acc, 'col', scatter_dimension=0, tiled=True)  18.4 us
    all_gather x1, blocking collectives, body(): lax.all_gather(row_feats, 'col', axis=0, tiled=True)  15.1 us
    all_gather x1, blocking collectives, body(): lax.all_gather(row_vectors, 'col', axis=0, tiled=True)  13.2 us
    ppermute x24, starting transfers between devices, from_behind(): return lax.ppermute(block, axis, route)  3.67 us
    unnamed x20, local copies, waits for them, and re-layouts  3.14 us
  transfers between devices with their start and end apart: 25, of which 9 were waited for; matrix products, arithmetic and copies ran while one was open for 5% of the time, Pallas kernels for 0%

commit v1 on v0

v1 whole, which is shorter than its diff:
```python
import functools

import jax
import jax.numpy as jnp
from jax import lax
from jax.experimental import pallas as pl
from jax.experimental.pallas import tpu as pltpu
from jax.sharding import PartitionSpec as P

AXES = ("row", "col")
F32, BF16 = jnp.float32, jnp.bfloat16


def dot(a, b, over):
    return lax.dot_general(a, b, (over, ((), ())), preferred_element_type=F32)


def embed(points, over, w_in, b_in, w_mid, b_mid, w_out, ard):
    one = jnp.tanh(dot(points, w_in[...], ((over,), (0,))) + b_in[...]).astype(BF16)
    two = jnp.tanh(dot(one, w_mid[...], ((1,), (0,))) + b_mid[...]).astype(BF16)
    return (dot(two, w_out[...], ((1,), (0,))) * jnp.sqrt(ard[...])).astype(BF16)


def col_kernel(chunk, points, w_in, b_in, w_mid, b_mid, w_out, ard, feats, half_sq):
    for start in range(0, points.shape[1], chunk):
        part = pl.ds(start, chunk)
        turned = embed(points[:, part], 0, w_in, b_in, w_mid, b_mid, w_out, ard).T
        feats[:, part] = turned
        half_sq[:, part] = 0.5 * jnp.sum(jnp.square(turned.astype(F32)), axis=0, keepdims=True)


def panel_kernel(chunk_rows, chunk_cols, rows, feats, half_sq, col_vecs, w_in, b_in, w_mid, b_mid, w_out, ard, *rest):
    row_out, near, far = rest[-3:]
    before = rest[:-3]
    width = w_in.shape[0]
    count_rows, count_cols = rows.shape[0], feats.shape[1]
    for at in range(0, count_rows, chunk_rows):
        block = rows[at : at + chunk_rows, :]
        row_feats = embed(block[:, :width], 1, w_in, b_in, w_mid, b_mid, w_out, ard)
        row_half = 0.5 * jnp.sum(jnp.square(row_feats.astype(F32)), axis=1, keepdims=True)
        vecs = block[:, width:]
        row_acc = None
        for start in range(0, count_cols, chunk_cols):
            part = pl.ds(start, chunk_cols)
            inner = dot(row_feats, feats[:, part], ((1,), (0,)))
            kernel = jnp.exp(inner - row_half - half_sq[:, part]).astype(BF16)
            term = dot(kernel, col_vecs[:, part], ((1,), (1,)))
            row_acc = term if row_acc is None else row_acc + term
            col_term = dot(vecs, kernel, ((0,), (0,)))
            side = 0 if start < count_cols // 2 else 1
            out = (near, far)[side]
            here = pl.ds(start - side * (count_cols // 2), chunk_cols)
            if at > 0:
                col_term = col_term + out[:, here]
            elif before:
                col_term = col_term + before[side][:, here]
            out[:, here] = col_term
        row_out[at : at + chunk_rows, :] = row_acc


def call(kernel, outs, args, flops):
    return pl.pallas_call(
        kernel,
        out_shape=outs,
        in_specs=[pl.BlockSpec(memory_space=pltpu.VMEM)] * len(args),
        out_specs=[pl.BlockSpec(memory_space=pltpu.VMEM)] * len(outs),
        compiler_params=pltpu.CompilerParams(vmem_limit_bytes=40 * 2**20),
        cost_estimate=pl.CostEstimate(flops=flops, bytes_accessed=2**20, transcendentals=0),
    )(*args)


def body(
    row_points,
    col_points,
    row_vectors,
    col_vectors,
    weight_in,
    bias_in,
    weight_mid,
    bias_mid,
    weight_out,
    ard_scales,
    signal_scale,
):
    count_row, count_col = lax.axis_size("row"), lax.axis_size("col")
    devices = count_row * count_col
    row_masks = [1 << b for b in reversed(range(count_col.bit_length() - 1))] + [devices // 2]
    col_masks = [count_col << b for b in reversed(range(count_row.bit_length() - 2))]

    def swap(block, mask):
        return lax.ppermute(block, AXES, [(i, i ^ mask) for i in range(devices)])

    weights = (
        weight_in,
        bias_in.reshape(1, -1),
        weight_mid,
        bias_mid.reshape(1, -1),
        weight_out,
        ard_scales.reshape(1, -1),
    )
    rows = jnp.concatenate([row_points, row_vectors], axis=1)
    points, vectors = col_points.T, col_vectors.T
    for mask in col_masks:
        points = jnp.concatenate([points, swap(points, mask)], axis=1)
        vectors = jnp.concatenate([vectors, swap(vectors, mask)], axis=1)
    for mask in row_masks[:-1]:
        rows = jnp.concatenate([rows, swap(rows, mask)], axis=0)
    far_rows = swap(rows, row_masks[-1])

    count_rows, count_cols = rows.shape[0], points.shape[1]
    nvec, emb = vectors.shape[0], weight_out.shape[1]
    chunk_cols, chunk_rows = min(512, count_cols // 2), min(256, count_rows)
    layers = sum(w.shape[0] * w.shape[1] for w in (weight_in, weight_mid, weight_out))
    feats, half_sq = call(
        functools.partial(col_kernel, chunk_cols),
        [jax.ShapeDtypeStruct((emb, count_cols), BF16), jax.ShapeDtypeStruct((1, count_cols), F32)],
        (points, *weights),
        2 * count_cols * layers,
    )
    half = jax.ShapeDtypeStruct((nvec, count_cols // 2), F32)
    panel = functools.partial(
        call,
        functools.partial(panel_kernel, chunk_rows, chunk_cols),
        [jax.ShapeDtypeStruct((count_rows, nvec), F32), half, half],
        flops=2 * count_rows * (layers + count_cols * (emb + 8 * nvec)),
    )
    row_near, near, far = panel((rows, feats, half_sq, vectors, *weights))
    row_far, near, far = panel((far_rows, feats, half_sq, vectors, *weights, near, far))

    row_sum = row_near + swap(row_far, row_masks[-1])
    for mask in reversed(row_masks[:-1]):
        keep, give = jnp.split(row_sum, 2, axis=0)
        row_sum = keep + swap(give, mask)
    col_sum = near + swap(far, col_masks[-1])
    for mask in reversed(col_masks[:-1]):
        keep, give = jnp.split(col_sum, 2, axis=1)
        col_sum = keep + swap(give, mask)
    return (row_sum * signal_scale[0], col_sum.T * signal_scale[0])


def solution(mesh):
    in_specs = (
        P(("row", "col"), None),
        P(("col", "row"), None),
        P(("row", "col"), None),
        P(("col", "row"), None),
        P(),
        P(),
        P(),
        P(),
        P(),
        P(),
        P(),
    )
    out_specs = (P(("row", "col"), None), P(("col", "row"), None))
    return jax.shard_map(body, mesh=mesh, in_specs=in_specs, out_specs=out_specs, check_vma=False)
```

time: 141 us -> 40.1 us (0.28)
  waiting for transfers between devices: 78.2 us -> 13.1 us
  blocking collectives: 28.3 us -> 0 us
  between operations: 14.8 us -> 1.51 us
  starting transfers between devices: 3.7 us -> 15.7 us
  matrix products: 7.15 us -> 0 us
  Pallas kernels: 0 us -> 6.26 us
  local copies, waits for them, and re-layouts: 4.1 us -> 0.84 us
    ppermute x24 -> x12, waiting for transfers between devices: 59.8 us -> 13.1 us  [swap(): return lax.ppermute(block, AXES, [(i, i ^ mask) for i in range(devices)])]
    all_gather x2 -> x0, blocking collectives: 28.3 us -> none  [the longest x1 15.1 us: body(): lax.all_gather(row_feats, 'col', axis=0, tiled=True)]
    reduce_scatter x1 -> x0, waiting for transfers between devices: 18.4 us -> none  [body(): lax.psum_scatter(row_acc, 'col', scatter_dimension=0, tiled=True)]
    ppermute x24 -> x12, starting transfers between devices: 3.67 us -> 15.7 us  [swap(): return lax.ppermute(block, AXES, [(i, i ^ mask) for i in range(devices)])]
    dot_general x28 -> x0, matrix products: 7.15 us -> none  [the longest x8 2.23 us: visit(): lax.dot_general(rows_all, features, (((1,), (1,)), ((), ())), preferred_e...]
    pallas_call x0 -> x3, Pallas kernels: none -> 6.26 us  [call(): pl.pallas_call(kernel, out_shape=outs, in_specs=[pl.BlockSpec(memory_spac...]
    unnamed x20, local copies, waits for them, and re-layouts: 3.14 us -> 0.82 us
  transfers between devices with their start and end apart: 25 -> 12, of which waited for: 9 -> 5; matrix products, arithmetic and copies ran while one was open for 5% -> 2% of each run, Pallas kernels for 0% -> 11%
where the time goes in v1:
time: 40.1 us; the launch traced here: 39.8 us
  starting transfers between devices  15.7 us (39%)
  waiting for transfers between devices  13.1 us (33%)
  Pallas kernels  6.26 us (16%)
  other arithmetic  2.42 us (6%)
  between operations  1.51 us (4%)
  local copies, waits for them, and re-layouts  0.84 us (2%)
    ppermute x12, starting transfers between devices, swap(): return lax.ppermute(block, AXES, [(i, i ^ mask) for i in range(devices)])  15.7 us
    ppermute x12, waiting for transfers between devices, swap(): return lax.ppermute(block, AXES, [(i, i ^ mask) for i in range(devices)])  13.1 us
    pallas_call x3, Pallas kernels, call(): pl.pallas_call(kernel, out_shape=outs, in_specs=[pl.BlockSpec(memory_spac...  6.26 us
    mul x2, other arithmetic, body(): return (row_sum * signal_scale[0], col_sum.T * signal_scale[0])  1.3 us
    concatenate x1, other arithmetic, body(): rows = jnp.concatenate([row_points, row_vectors], axis=1)  0.85 us
    unnamed x20, local copies, waits for them, and re-layouts  0.82 us
  transfers between devices with their start and end apart: 12, of which 5 were waited for; matrix products, arithmetic and copies ran while one was open for 2% of the time, Pallas kernels for 11%

profile of v1, /device:TPU:0, one launch (start us, length us, event | category | flops | bytes accessed | tf_op | source)
XLA Modules:
  0.0 39.8 jit_solution(14044103731669160881)
XLA Ops:
  0.6 0.0 copy-start.8
  0.6 0.0 copy-start.9
  0.6 0.0 copy-start.6
  0.7 0.8 %pad_maximum_fusion.6 = bf16[64,128]{1,0:T(8,128)(2,1)S(1)} fusion(bf16[64,64]{1,0:T(8,128)(2,1)} %param.13, bf16[64,64]{1,0:T(8,128)(2,1)} %param.11), kind=kLoop, calls=%fused_computation.12 | loop fusion | flops 32768 | bytes 32768 | tf_op jit(solution)/shard_map/concatenate | solution.py:101
  1.5 4.1 %collective-permute-start = (bf16[64,128]{1,0:T(8,128)(2,1)S(1)}, bf16[64,128]{1,0:T(8,128)(2,1)S(1)}, u32[]{:S(2)}, u32[]{:S(2)}) collective-permute-start(bf16[64,128]{1,0:T(8,128)(2,1)S(1)} %pad_maximum_fusion.6), channel_id=1, source_target_pairs={{0,2},{1,3},{2,0},{3,1},{4,6},{5,7},{6,4},{7,5},{8,10},{9,11},{10,... | collective-permute-start | bytes 49160 | tf_op jit(solution)/shard_map/ppermute | solution.py:91
  5.6 1.5 %collective-permute-start.2 = (bf16[64,512]{1,0:T(8,128)(2,1)}, bf16[64,512]{1,0:T(8,128)(2,1)S(1)}, u32[]{:S(2)}, u32[]{:S(2)}) collective-permute-start(bf16[64,512]{1,0:T(8,128)(2,1)} %bitcast.19), channel_id=1, source_target_pairs={{0,8},{1,9},{2,10},{3,11},{4,12},{5,13},{6,14},{7,15},{8,0},{9,1},... | collective-permute-start | bytes 196616 | tf_op jit(solution)/shard_map/ppermute | solution.py:91
  7.1 0.5 %collective-permute-start.4 = (bf16[64,512]{1,0:T(8,128)(2,1)}, bf16[64,512]{1,0:T(8,128)(2,1)S(1)}, u32[]{:S(2)}, u32[]{:S(2)}) collective-permute-start(bf16[64,512]{1,0:T(8,128)(2,1)} %bitcast.22), channel_id=1, source_target_pairs={{0,8},{1,9},{2,10},{3,11},{4,12},{5,13},{6,14},{7,15},{8,0},{9,1},... | collective-permute-start | bytes 196616 | tf_op jit(solution)/shard_map/ppermute | solution.py:91
  7.6 0.0 collective-permute-done
  7.6 0.0 copy-done.8
  7.6 0.0 copy-done.9
  7.6 0.1 pad_maximum_fusion.5
  7.7 1.6 %collective-permute-start.1 = (bf16[128,128]{1,0:T(8,128)(2,1)S(1)}, bf16[128,128]{1,0:T(8,128)(2,1)S(1)}, u32[]{:S(2)}, u32[]{:S(2)}) collective-permute-start(bf16[128,128]{1,0:T(8,128)(2,1)S(1)} %pad_maximum_fusion.5), channel_id=1, source_target_pairs={{0,1},{1,0},{2,3},{3,2},{4,5},{5,4},{6,7},{7,6},{8,9},{9,8},{10,11... | collective-permute-start | bytes 98312 | tf_op jit(solution)/shard_map/ppermute | solution.py:91
  9.3 1.3 %collective-permute-done.2 = bf16[64,512]{1,0:T(8,128)(2,1)S(1)} collective-permute-done((bf16[64,512]{1,0:T(8,128)(2,1)}, bf16[64,512]{1,0:T(8,128)(2,1)S(1)}, u32[]{:S(2)}, u32[]{:S(2)}) %collective-permute-start.2) | collective-permute-done | bytes 65568 | tf_op jit(solution)/shard_map/ppermute | solution.py:91
  10.5 0.0 copy-done.6
  10.6 0.0 copy-start
  10.6 0.1 collective-permute-start.3
  10.7 1.0 %collective-permute-done.1 = bf16[128,128]{1,0:T(8,128)(2,1)S(1)} collective-permute-done((bf16[128,128]{1,0:T(8,128)(2,1)S(1)}, bf16[128,128]{1,0:T(8,128)(2,1)S(1)}, u32[]{:S(2)}, u32[]{:S(2)}) %collective-permute-start.1) | collective-permute-done | bytes 32800 | tf_op jit(solution)/shard_map/ppermute | solution.py:91
  11.6 0.1 pad_maximum_fusion.4.rows
  11.7 1.6 %collective-permute-start.6 = (bf16[256,128]{1,0:T(8,128)(2,1)S(1)}, bf16[256,128]{1,0:T(8,128)(2,1)S(1)}, u32[]{:S(2)}, u32[]{:S(2)}) collective-permute-start(bf16[256,128]{1,0:T(8,128)(2,1)S(1)} %pad_maximum_fusion.4.rows), channel_id=1, source_target_pairs={{0,16},{1,17},{2,18},{3,19},{4,20},{5,21},{6,22},{7,23},{8,24},{9,... | collective-permute-start | bytes 196616 | tf_op jit(solution)/shard_map/ppermute | solution.py:91
  13.3 0.0 collective-permute-done.4
  13.3 0.0 copy-done.7
  13.3 0.0 copy-start.1
  13.3 0.0 copy-start.2
  13.3 0.1 collective-permute-start.5
  13.4 0.0 collective-permute-done.3
  13.4 0.0 copy-start.4
  13.5 0.0 copy-start.3
  13.5 0.0 copy-start.5
  13.5 0.0 copy-done
  13.5 0.8 %copy-done.1 = bf16[512,256]{1,0:T(8,128)(2,1)S(1)} copy-done((bf16[512,256]{1,0:T(8,128)(2,1)S(1)}, bf16[512,256]{1,0:T(8,128)(2,1)}, u32[]{:S(2)}) %copy-start.1) | copy-done | bytes 262168
  14.3 0.0 copy-done.2
  14.3 2.6 %shard_map.122 = (bf16[256,2048]{1,0:T(8,128)(2,1)S(1)}, f32[1,2048]{1,0:T(1,128)S(1)}) custom-call(bf16[64,2048]{1,0:T(8,128)(2,1)S(1)} %pad_maximum_fusion.points, bf16[64,512]{1,0:T(8,128)(2,1)S(1)} %copy-done.2, f32[1,512]{1,0:T(1,128)S(1)} %bitcast.10, bf16[512,512]{1,0:T(8,128)(2,1)S(1)} %copy-done, f32[1,512]{1,0:T(1,128)S(1)} %bitcast.13, ...), custom_call_target="tpu_custom_call" | custom-call | flops 1744830464 | bytes 1048576 | tf_op jit(solution)/shard_map/pallas_call | solution.py:62
  16.9 0.0 collective-permute-done.5
  16.9 1.8 %shard_map.123 = (f32[256,64]{1,0:T(8,128)S(1)}, f32[64,1024]{1,0:T(8,128)S(1)}, f32[64,1024]{1,0:T(8,128)S(1)}) custom-call(bf16[256,128]{1,0:T(8,128)(2,1)S(1)} %pad_maximum_fusion.4.rows, bf16[256,2048]{1,0:T(8,128)(2,1)S(1)} %get-tuple-element.10.feats, f32[1,2048]{1,0:T(1,128)S(1)} %get-tuple-element.11.half_sq, ...), custom_call_target="tpu_custom_call" | custom-call | flops 1023410176 | bytes 1048576 | tf_op jit(solution)/shard_map/pallas_call | solution.py:62
  18.7 0.0 collective-permute-done.6.rows
  18.8 1.8 %shard_map.124 = (f32[256,64]{1,0:T(8,128)S(1)}, f32[64,1024]{1,0:T(8,128)S(1)}, f32[64,1024]{1,0:T(8,128)S(1)}) custom-call(bf16[256,128]{1,0:T(8,128)(2,1)S(1)} %collective-permute-done.6.rows, bf16[256,2048]{1,0:T(8,128)(2,1)S(1)} %get-tuple-element.10.feats, f32[1,2048]{1,0:T(1,128)S(1)} %get-tuple-element.11.half_sq, ...), custom_call_target="tpu_custom_call" | custom-call | flops 1023410176 | bytes 1048576 | tf_op jit(solution)/shard_map/pallas_call | solution.py:62
  20.6 0.5 %collective-permute-start.7 = (f32[256,64]{1,0:T(8,128)S(1)}, f32[256,64]{1,0:T(8,128)S(1)}, u32[]{:S(2)}, u32[]{:S(2)}) collective-permute-start(f32[256,64]{1,0:T(8,128)S(1)} %get-tuple-element.15), channel_id=1, source_target_pairs={{0,16},{1,17},{2,18},{3,19},{4,20},{5,21},{6,22},{7,23},{8,24},{9,... | collective-permute-start | bytes 196616 | tf_op jit(solution)/shard_map/ppermute | solution.py:91
  21.1 5.3 %collective-permute-done.7 = f32[256,64]{1,0:T(8,128)S(1)} collective-permute-done((f32[256,64]{1,0:T(8,128)S(1)}, f32[256,64]{1,0:T(8,128)S(1)}, u32[]{:S(2)}, u32[]{:S(2)}) %collective-permute-start.7) | collective-permute-done | bytes 65568 | tf_op jit(solution)/shard_map/ppermute | solution.py:91
  26.4 1.6 %collective-permute-start.8 = (f32[128,64]{1,0:T(8,128)S(1)}, f32[128,64]{1,0:T(8,128)S(1)}, u32[]{:S(2)}, u32[]{:S(2)}) collective-permute-start(f32[128,64]{1,0:T(8,128)S(1)} %split.25), channel_id=1, source_target_pairs={{0,1},{1,0},{2,3},{3,2},{4,5},{5,4},{6,7},{7,6},{8,9},{9,8},{10,11... | collective-permute-start | bytes 98312 | tf_op jit(solution)/shard_map/ppermute | solution.py:91
  28.0 0.0 collective-permute-start.10
  28.0 2.7 %collective-permute-done.8 = f32[128,64]{1,0:T(8,128)S(1)} collective-permute-done((f32[128,64]{1,0:T(8,128)S(1)}, f32[128,64]{1,0:T(8,128)S(1)}, u32[]{:S(2)}, u32[]{:S(2)}) %collective-permute-start.8) | collective-permute-done | bytes 32800 | tf_op jit(solution)/shard_map/ppermute | solution.py:91
  30.8 2.6 %collective-permute-start.9 = (f32[64,64]{1,0:T(8,128)S(1)}, f32[64,64]{1,0:T(8,128)S(1)}, u32[]{:S(2)}, u32[]{:S(2)}) collective-permute-start(f32[64,64]{1,0:T(8,128)S(1)} %split.27), channel_id=1, source_target_pairs={{0,2},{1,3},{2,0},{3,1},{4,6},{5,7},{6,4},{7,5},{8,10},{9,11},{10,... | collective-permute-start | bytes 49160 | tf_op jit(solution)/shard_map/ppermute | solution.py:91
  34.1 0.0 collective-permute-done.10
  34.1 1.6 %collective-permute-start.11 = (f32[64,512]{1,0:T(8,128)S(1)}, f32[64,512]{1,0:T(8,128)S(1)}, u32[]{:S(2)}, u32[]{:S(2)}) collective-permute-start(f32[64,512]{1,0:T(8,128)S(1)} %split.29), channel_id=1, source_target_pairs={{0,8},{1,9},{2,10},{3,11},{4,12},{5,13},{6,14},{7,15},{8,0},{9,1},... | collective-permute-start | bytes 393224 | tf_op jit(solution)/shard_map/ppermute | solution.py:91
  35.7 0.0 collective-permute-done.9
  35.7 0.6 %fusion.2 = f32[64,64]{1,0:T(8,128)} fusion(f32[64,64]{1,0:T(8,128)S(1)} %collective-permute-done.9, f32[128,64]{1,0:T(8,128)S(1)} %slice_add_fusion.1, f32[]{:T(128)} %bitcast.8), kind=kLoop, calls=%fused_computation.10 | loop fusion | flops 8192 | bytes 49156 | tf_op jit(solution)/shard_map/mul | solution.py:138
  36.3 2.9 %collective-permute-done.11 = f32[64,512]{1,0:T(8,128)S(1)} collective-permute-done((f32[64,512]{1,0:T(8,128)S(1)}, f32[64,512]{1,0:T(8,128)S(1)}, u32[]{:S(2)}, u32[]{:S(2)}) %collective-permute-start.11) | collective-permute-done | bytes 131104 | tf_op jit(solution)/shard_map/ppermute | solution.py:91
  39.2 0.7 %fusion.1 = f32[512,64]{0,1:T(8,128)} fusion(f32[64,512]{1,0:T(8,128)S(1)} %collective-permute-done.11, f32[64,1024]{1,0:T(8,128)S(1)} %add.18, f32[]{:T(128)} %bitcast.9), kind=kLoop, calls=%fused_computation.4 | loop fusion | flops 65536 | bytes 393220 | tf_op jit(solution)/shard_map/mul | solution.py:138
  (14 shorter events, 0.1 us)
Async XLA Ops:
  0.6 7.0 %copy-start.8 = (bf16[64,64]{1,0:T(8,128)(2,1)S(1)}, bf16[64,64]{1,0:T(8,128)(2,1)}, u32[]{:S(2)}) copy-start(bf16[64,64]{1,0:T(8,128)(2,1)} %param.13) | copy-start | bytes 24580
  0.6 7.0 %copy-start.9 = (bf16[64,64]{1,0:T(8,128)(2,1)S(1)}, bf16[64,64]{1,0:T(8,128)(2,1)}, u32[]{:S(2)}) copy-start(bf16[64,64]{1,0:T(8,128)(2,1)} %param.11) | copy-start | bytes 24580
  0.6 9.9 %copy-start.6 = (bf16[512,64]{0,1:T(8,128)(2,1)S(1)}, bf16[512,64]{0,1:T(8,128)(2,1)}, u32[]{:S(2)}) copy-start(bf16[512,64]{0,1:T(8,128)(2,1)} %param.12) | copy-start | bytes 196612
  1.5 6.1 %collective-permute-start = (bf16[64,128]{1,0:T(8,128)(2,1)S(1)}, bf16[64,128]{1,0:T(8,128)(2,1)S(1)}, u32[]{:S(2)}, u32[]{:S(2)}) collective-permute-start(bf16[64,128]{1,0:T(8,128)(2,1)S(1)} %pad_maximum_fusion.6), channel_id=1, source_target_pairs={{0,2},{1,3},{2,0},{3,1},{4,6},{5,7},{6,4},{7,5},{8,10},{9,11},{10,... | collective-permute-start | bytes 49160 | tf_op jit(solution)/shard_map/ppermute | solution.py:91
  5.6 5.0 %collective-permute-start.2 = (bf16[64,512]{1,0:T(8,128)(2,1)}, bf16[64,512]{1,0:T(8,128)(2,1)S(1)}, u32[]{:S(2)}, u32[]{:S(2)}) collective-permute-start(bf16[64,512]{1,0:T(8,128)(2,1)} %bitcast.19), channel_id=1, source_target_pairs={{0,8},{1,9},{2,10},{3,11},{4,12},{5,13},{6,14},{7,15},{8,0},{9,1},... | collective-permute-start | bytes 196616 | tf_op jit(solution)/shard_map/ppermute | solution.py:91
  7.1 6.2 %collective-permute-start.4 = (bf16[64,512]{1,0:T(8,128)(2,1)}, bf16[64,512]{1,0:T(8,128)(2,1)S(1)}, u32[]{:S(2)}, u32[]{:S(2)}) collective-permute-start(bf16[64,512]{1,0:T(8,128)(2,1)} %bitcast.22), channel_id=1, source_target_pairs={{0,8},{1,9},{2,10},{3,11},{4,12},{5,13},{6,14},{7,15},{8,0},{9,1},... | collective-permute-start | bytes 196616 | tf_op jit(solution)/shard_map/ppermute | solution.py:91
  7.7 3.9 %collective-permute-start.1 = (bf16[128,128]{1,0:T(8,128)(2,1)S(1)}, bf16[128,128]{1,0:T(8,128)(2,1)S(1)}, u32[]{:S(2)}, u32[]{:S(2)}) collective-permute-start(bf16[128,128]{1,0:T(8,128)(2,1)S(1)} %pad_maximum_fusion.5), channel_id=1, source_target_pairs={{0,1},{1,0},{2,3},{3,2},{4,5},{5,4},{6,7},{7,6},{8,9},{9,8},{10,11... | collective-permute-start | bytes 98312 | tf_op jit(solution)/shard_map/ppermute | solution.py:91
  10.5 2.7 %copy-start.7 = (bf16[512,64]{0,1:T(8,128)(2,1)S(1)}, bf16[512,64]{0,1:T(8,128)(2,1)}, u32[]{:S(2)}) copy-start(bf16[512,64]{0,1:T(8,128)(2,1)} %param.14) | copy-start | bytes 196612
  10.6 2.9 %copy-start = (bf16[512,512]{1,0:T(8,128)(2,1)S(1)}, bf16[512,512]{1,0:T(8,128)(2,1)}, u32[]{:S(2)}) copy-start(bf16[512,512]{1,0:T(8,128)(2,1)} %w_mid.5) | copy-start | bytes 1572868
  10.6 2.8 %collective-permute-start.3 = (bf16[64,1024]{1,0:T(8,128)(2,1)S(1)}, bf16[64,1024]{1,0:T(8,128)(2,1)S(1)}, u32[]{:S(2)}, u32[]{:S(2)}) collective-permute-start(bf16[64,1024]{1,0:T(8,128)(2,1)S(1)} %pad_maximum_fusion.2), channel_id=1, source_target_pairs={{0,4},{1,5},{2,6},{3,7},{4,0},{5,1},{6,2},{7,3},{8,12},{9,13},{10,... | collective-permute-start | bytes 393224 | tf_op jit(solution)/shard_map/ppermute | solution.py:91
  11.7 7.1 %collective-permute-start.6 = (bf16[256,128]{1,0:T(8,128)(2,1)S(1)}, bf16[256,128]{1,0:T(8,128)(2,1)S(1)}, u32[]{:S(2)}, u32[]{:S(2)}) collective-permute-start(bf16[256,128]{1,0:T(8,128)(2,1)S(1)} %pad_maximum_fusion.4.rows), channel_id=1, source_target_pairs={{0,16},{1,17},{2,18},{3,19},{4,20},{5,21},{6,22},{7,23},{8,24},{9,... | collective-permute-start | bytes 196616 | tf_op jit(solution)/shard_map/ppermute | solution.py:91
  13.3 1.0 %copy-start.1 = (bf16[512,256]{1,0:T(8,128)(2,1)S(1)}, bf16[512,256]{1,0:T(8,128)(2,1)}, u32[]{:S(2)}) copy-start(bf16[512,256]{1,0:T(8,128)(2,1)} %w_out.5) | copy-start | bytes 786436
  13.3 0.9 %copy-start.2 = (bf16[64,512]{1,0:T(8,128)(2,1)S(1)}, bf16[64,512]{1,0:T(8,128)(2,1)}, u32[]{:S(2)}) copy-start(bf16[64,512]{1,0:T(8,128)(2,1)} %w_in.5) | copy-start | bytes 196612
  13.3 3.5 %collective-permute-start.5 = (bf16[64,1024]{1,0:T(8,128)(2,1)S(1)}, bf16[64,1024]{1,0:T(8,128)(2,1)S(1)}, u32[]{:S(2)}, u32[]{:S(2)}) collective-permute-start(bf16[64,1024]{1,0:T(8,128)(2,1)S(1)} %pad_maximum_fusion.3), channel_id=1, source_target_pairs={{0,4},{1,5},{2,6},{3,7},{4,0},{5,1},{6,2},{7,3},{8,12},{9,13},{10,... | collective-permute-start | bytes 393224 | tf_op jit(solution)/shard_map/ppermute | solution.py:91
  13.4 0.8 %copy-start.4 = (f32[512]{0:T(512)S(1)}, f32[512]{0:T(512)}, u32[]{:S(2)}) copy-start(f32[512]{0:T(512)} %param.18) | copy-start | bytes 6148
  13.5 0.8 %copy-start.3 = (f32[512]{0:T(512)S(1)}, f32[512]{0:T(512)}, u32[]{:S(2)}) copy-start(f32[512]{0:T(512)} %param.16) | copy-start | bytes 6148
  13.5 0.8 %copy-start.5 = (f32[256]{0:T(256)S(1)}, f32[256]{0:T(256)}, u32[]{:S(2)}) copy-start(f32[256]{0:T(256)} %param.20) | copy-start | bytes 3076
  20.6 5.8 %collective-permute-start.7 = (f32[256,64]{1,0:T(8,128)S(1)}, f32[256,64]{1,0:T(8,128)S(1)}, u32[]{:S(2)}, u32[]{:S(2)}) collective-permute-start(f32[256,64]{1,0:T(8,128)S(1)} %get-tuple-element.15), channel_id=1, source_target_pairs={{0,16},{1,17},{2,18},{3,19},{4,20},{5,21},{6,22},{7,23},{8,24},{9,... | collective-permute-start | bytes 196616 | tf_op jit(solution)/shard_map/ppermute | solution.py:91
  26.4 4.3 %collective-permute-start.8 = (f32[128,64]{1,0:T(8,128)S(1)}, f32[128,64]{1,0:T(8,128)S(1)}, u32[]{:S(2)}, u32[]{:S(2)}) collective-permute-start(f32[128,64]{1,0:T(8,128)S(1)} %split.25), channel_id=1, source_target_pairs={{0,1},{1,0},{2,3},{3,2},{4,5},{5,4},{6,7},{7,6},{8,9},{9,8},{10,11... | collective-permute-start | bytes 98312 | tf_op jit(solution)/shard_map/ppermute | solution.py:91
  28.0 6.0 %collective-permute-start.10 = (f32[64,1024]{1,0:T(8,128)S(1)}, f32[64,1024]{1,0:T(8,128)S(1)}, u32[]{:S(2)}, u32[]{:S(2)}) collective-permute-start(f32[64,1024]{1,0:T(8,128)S(1)} %get-tuple-element.17), channel_id=1, source_target_pairs={{0,4},{1,5},{2,6},{3,7},{4,0},{5,1},{6,2},{7,3},{8,12},{9,13},{10,... | collective-permute-start | bytes 786440 | tf_op jit(solution)/shard_map/ppermute | solution.py:91
  30.8 4.9 %collective-permute-start.9 = (f32[64,64]{1,0:T(8,128)S(1)}, f32[64,64]{1,0:T(8,128)S(1)}, u32[]{:S(2)}, u32[]{:S(2)}) collective-permute-start(f32[64,64]{1,0:T(8,128)S(1)} %split.27), channel_id=1, source_target_pairs={{0,2},{1,3},{2,0},{3,1},{4,6},{5,7},{6,4},{7,5},{8,10},{9,11},{10,... | collective-permute-start | bytes 49160 | tf_op jit(solution)/shard_map/ppermute | solution.py:91
  34.1 5.0 %collective-permute-start.11 = (f32[64,512]{1,0:T(8,128)S(1)}, f32[64,512]{1,0:T(8,128)S(1)}, u32[]{:S(2)}, u32[]{:S(2)}) collective-permute-start(f32[64,512]{1,0:T(8,128)S(1)} %split.29), channel_id=1, source_target_pairs={{0,8},{1,9},{2,10},{3,11},{4,12},{5,13},{6,14},{7,15},{8,0},{9,1},... | collective-permute-start | bytes 393224 | tf_op jit(solution)/shard_map/ppermute | solution.py:91

commit v2 on v1

v2 whole, which is shorter than its diff:
```python
import functools

import jax
import jax.numpy as jnp
from jax import lax
from jax.experimental import pallas as pl
from jax.experimental.pallas import tpu as pltpu
from jax.sharding import PartitionSpec as P

AXES = ("row", "col")
F32, BF16 = jnp.float32, jnp.bfloat16


def dot(a, b, over):
    return lax.dot_general(a, b, (over, ((), ())), preferred_element_type=F32)


def embed(points, over, w_in, b_in, w_mid, b_mid, w_out, ard):
    one = jnp.tanh(dot(points, w_in[...], ((over,), (0,))) + b_in[...]).astype(BF16)
    two = jnp.tanh(dot(one, w_mid[...], ((1,), (0,))) + b_mid[...]).astype(BF16)
    return (dot(two, w_out[...], ((1,), (0,))) * jnp.sqrt(ard[...])).astype(BF16)


def col_kernel(chunk, points, w_in, b_in, w_mid, b_mid, w_out, ard, feats, half_sq):
    for start in range(0, points.shape[1], chunk):
        part = pl.ds(start, chunk)
        turned = embed(points[:, part], 0, w_in, b_in, w_mid, b_mid, w_out, ard).T
        feats[:, part] = turned
        half_sq[:, part] = 0.5 * jnp.sum(jnp.square(turned.astype(F32)), axis=0, keepdims=True)


def panel_kernel(chunk_rows, chunk_cols, tall, sides, rows, *rest):
    columns = [rest[3 * side : 3 * side + 3] for side in range(sides)]
    weights, rest = rest[3 * sides : 3 * sides + 6], rest[3 * sides + 6 :]
    before, row_out, col_outs = rest[: -sides - 1], rest[-sides - 1], rest[-sides:]
    width = weights[0].shape[0]
    own = rows.shape[1] - width
    for at in range(0, rows.shape[0], chunk_rows):
        block = rows[at : at + chunk_rows, :]
        row_feats = embed(block[:, :width], 1, *weights)
        row_half = 0.5 * jnp.sum(jnp.square(row_feats.astype(F32)), axis=1, keepdims=True)
        vecs = block[:, width:]
        row_acc = None
        for side, (feats, half_sq, col_vecs) in enumerate(columns):
            for start in range(0, feats.shape[1], chunk_cols):
                part = pl.ds(start, chunk_cols)
                inner = dot(row_feats, feats[:, part], ((1,), (0,)))
                kernel = jnp.exp(inner - row_half - half_sq[:, part]).astype(BF16)
                term = dot(kernel, col_vecs[:, part], ((1,), (1,)))
                row_acc = term if row_acc is None else row_acc + term
                col_term = dot(vecs, kernel, ((0,), (0,)))
                if at > 0:
                    col_term = col_term + col_outs[side][:, part]
                elif before:
                    col_term = col_term + before[side][:, part]
                col_outs[side][:, part] = col_term
        for pair in range(0, chunk_rows, 2 * tall):
            to = pl.ds((at + pair) // 2, tall)
            row_out[to, :own] = row_acc[pair : pair + tall]
            row_out[to, own:] = row_acc[pair + tall : pair + 2 * tall]


def call(kernel, outs, args, flops):
    return pl.pallas_call(
        kernel,
        out_shape=outs,
        in_specs=[pl.BlockSpec(memory_space=pltpu.VMEM)] * len(args),
        out_specs=[pl.BlockSpec(memory_space=pltpu.VMEM)] * len(outs),
        compiler_params=pltpu.CompilerParams(vmem_limit_bytes=40 * 2**20),
        cost_estimate=pl.CostEstimate(flops=flops, bytes_accessed=2**20, transcendentals=0),
    )(*args)


def body(
    row_points,
    col_points,
    row_vectors,
    col_vectors,
    weight_in,
    bias_in,
    weight_mid,
    bias_mid,
    weight_out,
    ard_scales,
    signal_scale,
):
    count_row, count_col = lax.axis_size("row"), lax.axis_size("col")
    devices = count_row * count_col
    row_masks = [1 << b for b in reversed(range(count_col.bit_length() - 1))] + [devices // 2]
    col_masks = [count_col << b for b in reversed(range(count_row.bit_length() - 2))]

    def swap(block, mask):
        return lax.ppermute(block, AXES, [(i, i ^ mask) for i in range(devices)])

    weights = (
        weight_in,
        bias_in.reshape(1, -1),
        weight_mid,
        bias_mid.reshape(1, -1),
        weight_out,
        ard_scales.reshape(1, -1),
    )
    block, nvec = row_vectors.shape
    emb = weight_out.shape[1]
    layers = sum(w.shape[0] * w.shape[1] for w in (weight_in, weight_mid, weight_out))
    chunk_cols = min(512, col_points.shape[0])

    def col_feats(points):
        count = points.shape[1]
        return call(
            functools.partial(col_kernel, chunk_cols),
            [jax.ShapeDtypeStruct((emb, count), BF16), jax.ShapeDtypeStruct((1, count), F32)],
            (points, *weights),
            2 * count * layers,
        )

    rows = jnp.concatenate([row_points, row_vectors], axis=1)
    rows = jnp.concatenate([rows, swap(rows, row_masks[0])], axis=0)
    points, vectors = [col_points.T], [col_vectors.T]
    feats = [col_feats(points[0])]
    for mask in col_masks:
        points.append(swap(jnp.concatenate(points, axis=1), mask))
        vectors.append(swap(jnp.concatenate(vectors, axis=1), mask))
        if mask == col_masks[0]:
            rows, points[1], feats[0] = lax.optimization_barrier((rows, points[1], feats[0]))
        feats.append(col_feats(points[-1]))
    for mask in row_masks[1:-1]:
        rows = jnp.concatenate([rows, swap(rows, mask)], axis=0)
    rows, feats = lax.optimization_barrier((rows, feats))
    far_rows = swap(rows, row_masks[-1])

    count_rows = rows.shape[0]
    sides = [v.shape[1] for v in vectors]
    panel = functools.partial(
        call,
        functools.partial(panel_kernel, min(4 * block, count_rows), chunk_cols, block, len(sides)),
        [jax.ShapeDtypeStruct((count_rows // 2, 2 * nvec), F32)]
        + [jax.ShapeDtypeStruct((nvec, count), F32) for count in sides],
        flops=2 * count_rows * (layers + sum(sides) * (emb + 8 * nvec)),
    )
    columns = [a for f, v in zip(feats, vectors, strict=True) for a in (*f, v)]
    row_near, *near = panel((rows, *columns, *weights))
    row_far, *col_sums = panel((far_rows, *columns, *weights, *near))

    row_sum = row_near + swap(row_far, row_masks[-1])
    for number, mask in reversed(list(enumerate(col_masks))):
        got, start = swap(col_sums[number + 1], mask), 0
        for side in range(number + 1):
            col_sums[side] = col_sums[side] + got[:, start : start + sides[side]]
            start += sides[side]
    for mask in reversed(row_masks[1:-1]):
        keep, give = jnp.split(row_sum, 2, axis=0)
        row_sum = keep + swap(give, mask)
    row_sum, col_sum = lax.optimization_barrier((row_sum, col_sums[0]))
    row_sum = row_sum[:, :nvec] + swap(row_sum, row_masks[0])[:, nvec:]
    return (row_sum * signal_scale[0], col_sum.T * signal_scale[0])


def solution(mesh):
    in_specs = (
        P(("row", "col"), None),
        P(("col", "row"), None),
        P(("row", "col"), None),
        P(("col", "row"), None),
        P(),
        P(),
        P(),
        P(),
        P(),
        P(),
        P(),
    )
    out_specs = (P(("row", "col"), None), P(("col", "row"), None))
    return jax.shard_map(body, mesh=mesh, in_specs=in_specs, out_specs=out_specs, check_vma=False)
```

time: 40.1 us -> 42.3 us (1.055)
  local copies, waits for them, and re-layouts: 0.84 us -> 5.1 us
  waiting for transfers between devices: 13.1 us -> 11.1 us
  starting transfers between devices: 15.7 us -> 14.7 us
  Pallas kernels: 6.26 us -> 7.14 us
    unnamed x20 -> x26, local copies, waits for them, and re-layouts: 0.82 us -> 5.1 us
    ppermute x12, waiting for transfers between devices: 13.1 us -> 11.1 us  [swap(): return lax.ppermute(block, AXES, [(i, i ^ mask) for i in range(devices)])]
    ppermute x12, starting transfers between devices: 15.7 us -> 14.7 us  [swap(): return lax.ppermute(block, AXES, [(i, i ^ mask) for i in range(devices)])]
    pallas_call x3 -> x5, Pallas kernels: 6.26 us -> 7.14 us  [call(): pl.pallas_call(kernel, out_shape=outs, in_specs=[pl.BlockSpec(memory_spac...]
  transfers between devices with their start and end apart: 12 -> 12, of which waited for: 5 -> 6; matrix products, arithmetic and copies ran while one was open for 2% -> 2% of each run, Pallas kernels for 11% -> 13%
where the time goes in v2:
time: 42.3 us; the launch traced here: 41.9 us
  starting transfers between devices  14.7 us (35%)
  waiting for transfers between devices  11.1 us (26%)
  Pallas kernels  7.14 us (17%)
  local copies, waits for them, and re-layouts  5.1 us (12%)
  other arithmetic  2.35 us (6%)
  between operations  1.45 us (3%)
    ppermute x12, starting transfers between devices, swap(): return lax.ppermute(block, AXES, [(i, i ^ mask) for i in range(devices)])  14.7 us
    ppermute x12, waiting for transfers between devices, swap(): return lax.ppermute(block, AXES, [(i, i ^ mask) for i in range(devices)])  11.1 us
    pallas_call x5, Pallas kernels, call(): pl.pallas_call(kernel, out_shape=outs, in_specs=[pl.BlockSpec(memory_spac...  7.14 us
    unnamed x26, local copies, waits for them, and re-layouts  5.1 us
    mul x2, other arithmetic, body(): return (row_sum * signal_scale[0], col_sum.T * signal_scale[0])  1.36 us
  transfers between devices with their start and end apart: 12, of which 6 were waited for; matrix products, arithmetic and copies ran while one was open for 2% of the time, Pallas kernels for 13%

profile of v2, /device:TPU:0, one launch (start us, length us, event | category | flops | bytes accessed | tf_op | source)
XLA Modules:
  0.0 41.9 jit_solution(8185131720873573258)
XLA Ops:
  0.6 0.8 %pad_maximum_fusion.4 = bf16[64,128]{1,0:T(8,128)(2,1)S(1)} fusion(bf16[64,64]{1,0:T(8,128)(2,1)} %param.13, bf16[64,64]{1,0:T(8,128)(2,1)} %param.11), kind=kLoop, calls=%fused_computation.11 | loop fusion | flops 32768 | bytes 32768 | tf_op jit(solution)/shard_map/concatenate | solution.py:117
  1.4 4.1 %collective-permute-start = (bf16[64,128]{1,0:T(8,128)(2,1)S(1)}, bf16[64,128]{1,0:T(8,128)(2,1)S(1)}, u32[]{:S(2)}, u32[]{:S(2)}) collective-permute-start(bf16[64,128]{1,0:T(8,128)(2,1)S(1)} %pad_maximum_fusion.4), channel_id=1, source_target_pairs={{0,2},{1,3},{2,0},{3,1},{4,6},{5,7},{6,4},{7,5},{8,10},{9,11},{10,... | collective-permute-start | bytes 49160 | tf_op jit(solution)/shard_map/ppermute | solution.py:93
  5.5 1.5 %collective-permute-start.1 = (bf16[64,512]{1,0:T(8,128)(2,1)}, bf16[64,512]{1,0:T(8,128)(2,1)S(1)}, u32[]{:S(2)}, u32[]{:S(2)}) collective-permute-start(bf16[64,512]{1,0:T(8,128)(2,1)} %bitcast.10), channel_id=1, source_target_pairs={{0,8},{1,9},{2,10},{3,11},{4,12},{5,13},{6,14},{7,15},{8,0},{9,1},... | collective-permute-start | bytes 196616 | tf_op jit(solution)/shard_map/ppermute | solution.py:93
  7.0 0.5 %collective-permute-start.4 = (bf16[64,512]{1,0:T(8,128)(2,1)}, bf16[64,512]{1,0:T(8,128)(2,1)S(1)}, u32[]{:S(2)}, u32[]{:S(2)}) collective-permute-start(bf16[64,512]{1,0:T(8,128)(2,1)} %bitcast.13), channel_id=1, source_target_pairs={{0,8},{1,9},{2,10},{3,11},{4,12},{5,13},{6,14},{7,15},{8,0},{9,1},... | collective-permute-start | bytes 196616 | tf_op jit(solution)/shard_map/ppermute | solution.py:93
  7.5 0.7 %copy-done.9 = f32[512]{0:T(512)S(1)} copy-done((f32[512]{0:T(512)S(1)}, f32[512]{0:T(512)}, u32[]{:S(2)}) %copy-start.9) | copy-done | bytes 2072
  8.2 0.0 copy-done.8
  8.2 0.0 copy-done.10
  8.2 0.8 %copy-done = bf16[512,64]{0,1:T(8,128)(2,1)S(1)} copy-done((bf16[512,64]{0,1:T(8,128)(2,1)S(1)}, bf16[512,64]{0,1:T(8,128)(2,1)}, u32[]{:S(2)}) %copy-start) | copy-done | bytes 65560
  9.1 1.0 %copy-done.2 = bf16[512,512]{1,0:T(8,128)(2,1)S(1)} copy-done((bf16[512,512]{1,0:T(8,128)(2,1)S(1)}, bf16[512,512]{1,0:T(8,128)(2,1)}, u32[]{:S(2)}) %copy-start.2) | copy-done | bytes 524312
  10.1 0.9 %copy-done.4 = bf16[512,256]{1,0:T(8,128)(2,1)S(1)} copy-done((bf16[512,256]{1,0:T(8,128)(2,1)S(1)}, bf16[512,256]{1,0:T(8,128)(2,1)}, u32[]{:S(2)}) %copy-start.4) | copy-done | bytes 262168
  11.1 0.8 %copy-done.6 = bf16[64,512]{1,0:T(8,128)(2,1)S(1)} copy-done((bf16[64,512]{1,0:T(8,128)(2,1)S(1)}, bf16[64,512]{1,0:T(8,128)(2,1)}, u32[]{:S(2)}) %copy-start.6) | copy-done | bytes 65560
  11.9 0.9 %shard_map.122 = (bf16[256,512]{1,0:T(8,128)(2,1)S(1)}, f32[1,512]{1,0:T(1,128)S(1)}) custom-call(bf16[64,512]{1,0:T(8,128)(2,1)S(1)} %bitcast.11, bf16[64,512]{1,0:T(8,128)(2,1)S(1)} %copy-done.6, f32[1,512]{1,0:T(1,128)S(1)} %bitcast.17, bf16[512,512]{1,0:T(8,128)(2,1)S(1)} %copy-done.2, f32[1,512]{1,0:T(1,128)S(1)} %bitcast.22, ...), custom_call_target="tpu_custom_call" | custom-call | flops 436207616 | bytes 1048576 | tf_op jit(solution)/shard_map/pallas_call | solution.py:64
  12.9 0.0 collective-permute-done
  12.9 0.0 copy-done.11
  12.9 0.0 copy-done.12
  12.9 0.1 pad_maximum_fusion.3
  13.0 0.0 collective-permute-done.1.points
  13.0 0.0 copy-start.1
  13.0 0.0 copy-start.5
  13.0 1.6 %collective-permute-start.2 = (bf16[128,128]{1,0:T(8,128)(2,1)S(1)}, bf16[128,128]{1,0:T(8,128)(2,1)S(1)}, u32[]{:S(2)}, u32[]{:S(2)}) collective-permute-start(bf16[128,128]{1,0:T(8,128)(2,1)S(1)} %pad_maximum_fusion.3), channel_id=1, source_target_pairs={{0,1},{1,0},{2,3},{3,2},{4,5},{5,4},{6,7},{7,6},{8,9},{9,8},{10,11... | collective-permute-start | bytes 98312 | tf_op jit(solution)/shard_map/ppermute | solution.py:93
  14.7 0.0 copy-start.7
  14.7 0.1 collective-permute-start.3
  14.8 0.0 collective-permute-done.4.rest_5_
  14.8 0.0 copy-done.3
  14.8 0.0 copy-done.5
  14.8 0.7 %copy-done.7 = bf16[64,512]{1,0:T(8,128)(2,1)S(1)} copy-done((bf16[64,512]{1,0:T(8,128)(2,1)S(1)}, bf16[64,512]{1,0:T(8,128)(2,1)}, u32[]{:S(2)}) %copy-start.7) | copy-done | bytes 65560
  15.5 0.9 %shard_map.123 = (bf16[256,512]{1,0:T(8,128)(2,1)S(1)}, f32[1,512]{1,0:T(1,128)S(1)}) custom-call(bf16[64,512]{1,0:T(8,128)(2,1)S(1)} %collective-permute-done.1.points, bf16[64,512]{1,0:T(8,128)(2,1)S(1)} %copy-done.7, f32[1,512]{1,0:T(1,128)S(1)} %bitcast.18, bf16[512,512]{1,0:T(8,128)(2,1)S(1)} %copy-done.3, f32[1,512]{1,0:T(1,128)S(1)} %bitcast.23, ...), custom_call_target="tpu_custom_call" | custom-call | flops 436207616 | bytes 1048576 | tf_op jit(solution)/shard_map/pallas_call | solution.py:64
  16.4 0.1 collective-permute-start.5
  16.5 0.5 %collective-permute-done.2 = bf16[128,128]{1,0:T(8,128)(2,1)S(1)} collective-permute-done((bf16[128,128]{1,0:T(8,128)(2,1)S(1)}, bf16[128,128]{1,0:T(8,128)(2,1)S(1)}, u32[]{:S(2)}, u32[]{:S(2)}) %collective-permute-start.2) | collective-permute-done | bytes 32800 | tf_op jit(solution)/shard_map/ppermute | solution.py:93
  17.0 0.0 collective-permute-done.3.points
  17.0 1.5 %shard_map.124 = (bf16[256,1024]{1,0:T(8,128)(2,1)S(1)}, f32[1,1024]{1,0:T(1,128)S(1)}) custom-call(bf16[64,1024]{1,0:T(8,128)(2,1)S(1)} %collective-permute-done.3.points, bf16[64,512]{1,0:T(8,128)(2,1)S(1)} %copy-done.7, f32[1,512]{1,0:T(1,128)S(1)} %bitcast.19, bf16[512,512]{1,0:T(8,128)(2,1)S(1)} %copy-done.3, f32[1,512]{1,0:T(1,128)S(1)} %bitcast.24, ...), custom_call_target="tpu_custom_call" | custom-call | flops 872415232 | bytes 1048576 | tf_op jit(solution)/shard_map/pallas_call | solution.py:64
  18.5 1.6 %collective-permute-start.6 = (bf16[256,128]{1,0:T(8,128)(2,1)S(1)}, bf16[256,128]{1,0:T(8,128)(2,1)S(1)}, u32[]{:S(2)}, u32[]{:S(2)}) collective-permute-start(bf16[256,128]{1,0:T(8,128)(2,1)S(1)} %pad_maximum_fusion.2.rows), channel_id=1, source_target_pairs={{0,16},{1,17},{2,18},{3,19},{4,20},{5,21},{6,22},{7,23},{8,24},{9,... | collective-permute-start | bytes 196616 | tf_op jit(solution)/shard_map/ppermute | solution.py:93
  20.1 0.0 collective-permute-done.5.rest_8_
  20.1 1.9 %shard_map.125 = (f32[128,128]{1,0:T(8,128)S(1)}, f32[64,512]{1,0:T(8,128)S(1)}, f32[64,512]{1,0:T(8,128)S(1)}, f32[64,1024]{1,0:T(8,128)S(1)}) custom-call(bf16[256,128]{1,0:T(8,128)(2,1)S(1)} %pad_maximum_fusion.2.rows, bf16[256,512]{1,0:T(8,128)(2,1)S(1)} %get-tuple-element.40.rest_0_, f32[1,512]{1,0:T(1,128)S(1)} %get-tuple-element.41.rest_1_, ...), custom_call_target="tpu_custom_call" | custom-call | flops 1023410176 | bytes 1048576 | tf_op jit(solution)/shard_map/pallas_call | solution.py:64
  22.0 0.9 %collective-permute-done.6.rows = bf16[256,128]{1,0:T(8,128)(2,1)S(1)} collective-permute-done((bf16[256,128]{1,0:T(8,128)(2,1)S(1)}, bf16[256,128]{1,0:T(8,128)(2,1)S(1)}, u32[]{:S(2)}, u32[]{:S(2)}) %collective-permute-start.6) | collective-permute-done | bytes 65568 | tf_op jit(solution)/shard_map/ppermute | solution.py:93
  22.8 1.9 %shard_map.126 = (f32[128,128]{1,0:T(8,128)S(1)}, f32[64,512]{1,0:T(8,128)S(1)}, f32[64,512]{1,0:T(8,128)S(1)}, f32[64,1024]{1,0:T(8,128)S(1)}) custom-call(bf16[256,128]{1,0:T(8,128)(2,1)S(1)} %collective-permute-done.6.rows, bf16[256,512]{1,0:T(8,128)(2,1)S(1)} %get-tuple-element.40.rest_0_, f32[1,512]{1,0:T(1,128)S(1)} %get-tuple-element.41.rest_1_, ...), custom_call_target="tpu_custom_call" | custom-call | flops 1023410176 | bytes 1048576 | tf_op jit(solution)/shard_map/pallas_call | solution.py:64
  24.7 0.1 collective-permute-start.9
  24.8 1.6 %collective-permute-start.7 = (f32[128,128]{1,0:T(8,128)S(1)}, f32[128,128]{1,0:T(8,128)S(1)}, u32[]{:S(2)}, u32[]{:S(2)}) collective-permute-start(f32[128,128]{1,0:T(8,128)S(1)} %get-tuple-element.50), channel_id=1, source_target_pairs={{0,16},{1,17},{2,18},{3,19},{4,20},{5,21},{6,22},{7,23},{8,24},{9,... | collective-permute-start | bytes 196616 | tf_op jit(solution)/shard_map/ppermute | solution.py:93
  27.0 2.3 %collective-permute-done.7 = f32[128,128]{1,0:T(8,128)S(1)} collective-permute-done((f32[128,128]{1,0:T(8,128)S(1)}, f32[128,128]{1,0:T(8,128)S(1)}, u32[]{:S(2)}, u32[]{:S(2)}) %collective-permute-start.7) | collective-permute-done | bytes 65568 | tf_op jit(solution)/shard_map/ppermute | solution.py:93
  29.3 1.6 %collective-permute-start.8 = (f32[64,128]{1,0:T(8,128)S(1)}, f32[64,128]{1,0:T(8,128)S(1)}, u32[]{:S(2)}, u32[]{:S(2)}) collective-permute-start(f32[64,128]{1,0:T(8,128)S(1)} %split.9), channel_id=1, source_target_pairs={{0,1},{1,0},{2,3},{3,2},{4,5},{5,4},{6,7},{7,6},{8,9},{9,8},{10,11... | collective-permute-start | bytes 98312 | tf_op jit(solution)/shard_map/ppermute | solution.py:93
  31.0 0.0 collective-permute-done.9
  31.0 1.6 %collective-permute-start.10 = (f32[64,512]{1,0:T(8,128)S(1)}, f32[64,512]{1,0:T(8,128)S(1)}, u32[]{:S(2)}, u32[]{:S(2)}) collective-permute-start(f32[64,512]{1,0:T(8,128)S(1)} %slice_add_fusion), channel_id=1, source_target_pairs={{0,8},{1,9},{2,10},{3,11},{4,12},{5,13},{6,14},{7,15},{8,0},{9,1},... | collective-permute-start | bytes 393224 | tf_op jit(solution)/shard_map/ppermute | solution.py:93
  32.5 0.8 %collective-permute-done.8 = f32[64,128]{1,0:T(8,128)S(1)} collective-permute-done((f32[64,128]{1,0:T(8,128)S(1)}, f32[64,128]{1,0:T(8,128)S(1)}, u32[]{:S(2)}, u32[]{:S(2)}) %collective-permute-start.8) | collective-permute-done | bytes 32800 | tf_op jit(solution)/shard_map/ppermute | solution.py:93
  33.3 2.7 %collective-permute-done.10 = f32[64,512]{1,0:T(8,128)S(1)} collective-permute-done((f32[64,512]{1,0:T(8,128)S(1)}, f32[64,512]{1,0:T(8,128)S(1)}, u32[]{:S(2)}, u32[]{:S(2)}) %collective-permute-start.10) | collective-permute-done | bytes 131104 | tf_op jit(solution)/shard_map/ppermute | solution.py:93
  36.0 0.4 collective-permute-start.11
  36.4 0.7 %multiply_bitcast_fusion = f32[512,64]{0,1:T(8,128)} fusion(f32[64,512]{1,0:T(8,128)S(1)} %fusion, f32[]{:T(128)} %bitcast.9), kind=kLoop, calls=%fused_computation.5 | loop fusion | flops 32768 | bytes 262148 | tf_op jit(solution)/shard_map/mul | solution.py:156
  37.1 4.0 %collective-permute-done.11 = f32[64,128]{1,0:T(8,128)S(1)} collective-permute-done((f32[64,128]{1,0:T(8,128)S(1)}, f32[64,128]{1,0:T(8,128)S(1)}, u32[]{:S(2)}, u32[]{:S(2)}) %collective-permute-start.11) | collective-permute-done | bytes 32800 | tf_op jit(solution)/shard_map/ppermute | solution.py:93
  41.2 0.7 %fusion.1 = f32[64,64]{1,0:T(8,128)} fusion(f32[64,128]{1,0:T(8,128)S(1)} %collective-permute-done.11, f32[64,128]{1,0:T(8,128)S(1)} %slice_add_fusion.3, f32[]{:T(128)} %bitcast.8), kind=kLoop, calls=%fused_computation.8 | loop fusion | flops 8192 | bytes 49156 | tf_op jit(solution)/shard_map/mul | solution.py:156
  (19 shorter events, 0.1 us)
Async XLA Ops:
  1.4 11.4 %collective-permute-start = (bf16[64,128]{1,0:T(8,128)(2,1)S(1)}, bf16[64,128]{1,0:T(8,128)(2,1)S(1)}, u32[]{:S(2)}, u32[]{:S(2)}) collective-permute-start(bf16[64,128]{1,0:T(8,128)(2,1)S(1)} %pad_maximum_fusion.4), channel_id=1, source_target_pairs={{0,2},{1,3},{2,0},{3,1},{4,6},{5,7},{6,4},{7,5},{8,10},{9,11},{10,... | collective-permute-start | bytes 49160 | tf_op jit(solution)/shard_map/ppermute | solution.py:93
  5.5 7.5 %collective-permute-start.1 = (bf16[64,512]{1,0:T(8,128)(2,1)}, bf16[64,512]{1,0:T(8,128)(2,1)S(1)}, u32[]{:S(2)}, u32[]{:S(2)}) collective-permute-start(bf16[64,512]{1,0:T(8,128)(2,1)} %bitcast.10), channel_id=1, source_target_pairs={{0,8},{1,9},{2,10},{3,11},{4,12},{5,13},{6,14},{7,15},{8,0},{9,1},... | collective-permute-start | bytes 196616 | tf_op jit(solution)/shard_map/ppermute | solution.py:93
  7.0 7.8 %collective-permute-start.4 = (bf16[64,512]{1,0:T(8,128)(2,1)}, bf16[64,512]{1,0:T(8,128)(2,1)S(1)}, u32[]{:S(2)}, u32[]{:S(2)}) collective-permute-start(bf16[64,512]{1,0:T(8,128)(2,1)} %bitcast.13), channel_id=1, source_target_pairs={{0,8},{1,9},{2,10},{3,11},{4,12},{5,13},{6,14},{7,15},{8,0},{9,1},... | collective-permute-start | bytes 196616 | tf_op jit(solution)/shard_map/ppermute | solution.py:93
  7.5 0.7 %copy-start.9 = (f32[512]{0:T(512)S(1)}, f32[512]{0:T(512)}, u32[]{:S(2)}) copy-start(f32[512]{0:T(512)} %param.18) | copy-start | bytes 6148
  7.5 0.7 %copy-start.8 = (f32[512]{0:T(512)S(1)}, f32[512]{0:T(512)}, u32[]{:S(2)}) copy-start(f32[512]{0:T(512)} %param.16) | copy-start | bytes 6148
  7.5 0.7 %copy-start.10 = (f32[256]{0:T(256)S(1)}, f32[256]{0:T(256)}, u32[]{:S(2)}) copy-start(f32[256]{0:T(256)} %param.20) | copy-start | bytes 3076
  8.2 0.8 %copy-start = (bf16[512,64]{0,1:T(8,128)(2,1)S(1)}, bf16[512,64]{0,1:T(8,128)(2,1)}, u32[]{:S(2)}) copy-start(bf16[512,64]{0,1:T(8,128)(2,1)} %param.12) | copy-start | bytes 196612
  9.1 1.0 %copy-start.2 = (bf16[512,512]{1,0:T(8,128)(2,1)S(1)}, bf16[512,512]{1,0:T(8,128)(2,1)}, u32[]{:S(2)}) copy-start(bf16[512,512]{1,0:T(8,128)(2,1)} %rest_11_.3) | copy-start | bytes 1572868
  10.1 0.9 %copy-start.4 = (bf16[512,256]{1,0:T(8,128)(2,1)S(1)}, bf16[512,256]{1,0:T(8,128)(2,1)}, u32[]{:S(2)}) copy-start(bf16[512,256]{1,0:T(8,128)(2,1)} %rest_13_.3) | copy-start | bytes 786436
  11.1 0.8 %copy-start.6 = (bf16[64,512]{1,0:T(8,128)(2,1)S(1)}, bf16[64,512]{1,0:T(8,128)(2,1)}, u32[]{:S(2)}) copy-start(bf16[64,512]{1,0:T(8,128)(2,1)} %rest_9_.3) | copy-start | bytes 196612
  11.9 1.0 %copy-start.11 = (bf16[64,64]{1,0:T(8,128)(2,1)S(1)}, bf16[64,64]{1,0:T(8,128)(2,1)}, u32[]{:S(2)}) copy-start(bf16[64,64]{1,0:T(8,128)(2,1)} %param.13) | copy-start | bytes 24580
  11.9 1.0 %copy-start.12 = (bf16[64,64]{1,0:T(8,128)(2,1)S(1)}, bf16[64,64]{1,0:T(8,128)(2,1)}, u32[]{:S(2)}) copy-start(bf16[64,64]{1,0:T(8,128)(2,1)} %param.11) | copy-start | bytes 24580
  11.9 2.9 %copy-start.3 = (bf16[512,512]{1,0:T(8,128)(2,1)S(1)}, bf16[512,512]{1,0:T(8,128)(2,1)}, u32[]{:S(2)}) copy-start(bf16[512,512]{1,0:T(8,128)(2,1)} %rest_11_.3) | copy-start | bytes 1572868
  13.0 1.8 %copy-start.1 = (bf16[512,64]{0,1:T(8,128)(2,1)S(1)}, bf16[512,64]{0,1:T(8,128)(2,1)}, u32[]{:S(2)}) copy-start(bf16[512,64]{0,1:T(8,128)(2,1)} %param.14) | copy-start | bytes 196612
  13.0 1.8 %copy-start.5 = (bf16[512,256]{1,0:T(8,128)(2,1)S(1)}, bf16[512,256]{1,0:T(8,128)(2,1)}, u32[]{:S(2)}) copy-start(bf16[512,256]{1,0:T(8,128)(2,1)} %rest_13_.3) | copy-start | bytes 786436
  13.0 4.0 %collective-permute-start.2 = (bf16[128,128]{1,0:T(8,128)(2,1)S(1)}, bf16[128,128]{1,0:T(8,128)(2,1)S(1)}, u32[]{:S(2)}, u32[]{:S(2)}) collective-permute-start(bf16[128,128]{1,0:T(8,128)(2,1)S(1)} %pad_maximum_fusion.3), channel_id=1, source_target_pairs={{0,1},{1,0},{2,3},{3,2},{4,5},{5,4},{6,7},{7,6},{8,9},{9,8},{10,11... | collective-permute-start | bytes 98312 | tf_op jit(solution)/shard_map/ppermute | solution.py:93
  14.7 0.8 %copy-start.7 = (bf16[64,512]{1,0:T(8,128)(2,1)S(1)}, bf16[64,512]{1,0:T(8,128)(2,1)}, u32[]{:S(2)}) copy-start(bf16[64,512]{1,0:T(8,128)(2,1)} %rest_9_.3) | copy-start | bytes 196612
  14.7 2.3 %collective-permute-start.3 = (bf16[64,1024]{1,0:T(8,128)(2,1)S(1)}, bf16[64,1024]{1,0:T(8,128)(2,1)S(1)}, u32[]{:S(2)}, u32[]{:S(2)}) collective-permute-start(bf16[64,1024]{1,0:T(8,128)(2,1)S(1)} %pad_maximum_fusion), channel_id=1, source_target_pairs={{0,4},{1,5},{2,6},{3,7},{4,0},{5,1},{6,2},{7,3},{8,12},{9,13},{10,... | collective-permute-start | bytes 393224 | tf_op jit(solution)/shard_map/ppermute | solution.py:93
  16.4 3.6 %collective-permute-start.5 = (bf16[64,1024]{1,0:T(8,128)(2,1)S(1)}, bf16[64,1024]{1,0:T(8,128)(2,1)S(1)}, u32[]{:S(2)}, u32[]{:S(2)}) collective-permute-start(bf16[64,1024]{1,0:T(8,128)(2,1)S(1)} %pad_maximum_fusion.1), channel_id=1, source_target_pairs={{0,4},{1,5},{2,6},{3,7},{4,0},{5,1},{6,2},{7,3},{8,12},{9,13},{10,... | collective-permute-start | bytes 393224 | tf_op jit(solution)/shard_map/ppermute | solution.py:93
  18.5 4.3 %collective-permute-start.6 = (bf16[256,128]{1,0:T(8,128)(2,1)S(1)}, bf16[256,128]{1,0:T(8,128)(2,1)S(1)}, u32[]{:S(2)}, u32[]{:S(2)}) collective-permute-start(bf16[256,128]{1,0:T(8,128)(2,1)S(1)} %pad_maximum_fusion.2.rows), channel_id=1, source_target_pairs={{0,16},{1,17},{2,18},{3,19},{4,20},{5,21},{6,22},{7,23},{8,24},{9,... | collective-permute-start | bytes 196616 | tf_op jit(solution)/shard_map/ppermute | solution.py:93
  24.7 6.2 %collective-permute-start.9 = (f32[64,1024]{1,0:T(8,128)S(1)}, f32[64,1024]{1,0:T(8,128)S(1)}, u32[]{:S(2)}, u32[]{:S(2)}) collective-permute-start(f32[64,1024]{1,0:T(8,128)S(1)} %get-tuple-element.52), channel_id=1, source_target_pairs={{0,4},{1,5},{2,6},{3,7},{4,0},{5,1},{6,2},{7,3},{8,12},{9,13},{10,... | collective-permute-start | bytes 786440 | tf_op jit(solution)/shard_map/ppermute | solution.py:93
  24.8 4.5 %collective-permute-start.7 = (f32[128,128]{1,0:T(8,128)S(1)}, f32[128,128]{1,0:T(8,128)S(1)}, u32[]{:S(2)}, u32[]{:S(2)}) collective-permute-start(f32[128,128]{1,0:T(8,128)S(1)} %get-tuple-element.50), channel_id=1, source_target_pairs={{0,16},{1,17},{2,18},{3,19},{4,20},{5,21},{6,22},{7,23},{8,24},{9,... | collective-permute-start | bytes 196616 | tf_op jit(solution)/shard_map/ppermute | solution.py:93
  29.3 4.0 %collective-permute-start.8 = (f32[64,128]{1,0:T(8,128)S(1)}, f32[64,128]{1,0:T(8,128)S(1)}, u32[]{:S(2)}, u32[]{:S(2)}) collective-permute-start(f32[64,128]{1,0:T(8,128)S(1)} %split.9), channel_id=1, source_target_pairs={{0,1},{1,0},{2,3},{3,2},{4,5},{5,4},{6,7},{7,6},{8,9},{9,8},{10,11... | collective-permute-start | bytes 98312 | tf_op jit(solution)/shard_map/ppermute | solution.py:93
  31.0 5.0 %collective-permute-start.10 = (f32[64,512]{1,0:T(8,128)S(1)}, f32[64,512]{1,0:T(8,128)S(1)}, u32[]{:S(2)}, u32[]{:S(2)}) collective-permute-start(f32[64,512]{1,0:T(8,128)S(1)} %slice_add_fusion), channel_id=1, source_target_pairs={{0,8},{1,9},{2,10},{3,11},{4,12},{5,13},{6,14},{7,15},{8,0},{9,1},... | collective-permute-start | bytes 393224 | tf_op jit(solution)/shard_map/ppermute | solution.py:93
  36.0 5.1 %collective-permute-start.11 = (f32[64,128]{1,0:T(8,128)S(1)}, f32[64,128]{1,0:T(8,128)S(1)}, u32[]{:S(2)}, u32[]{:S(2)}) collective-permute-start(f32[64,128]{1,0:T(8,128)S(1)} %slice_add_fusion.3), channel_id=1, source_target_pairs={{0,2},{1,3},{2,0},{3,1},{4,6},{5,7},{6,4},{7,5},{8,10},{9,11},{10,... | collective-permute-start | bytes 98312 | tf_op jit(solution)/shard_map/ppermute | solution.py:93

commit v3 on v2

--- a/solution.py
+++ b/solution.py
@@ -9,6 +9,8 @@
 
 AXES = ("row", "col")
 F32, BF16 = jnp.float32, jnp.bfloat16
+HOLD_FLOPS = 2 * 10**10
+FINISH_FLOPS = 10**6
 
 
 def dot(a, b, over):
@@ -66,9 +68,17 @@
         out_shape=outs,
         in_specs=[pl.BlockSpec(memory_space=pltpu.VMEM)] * len(args),
         out_specs=[pl.BlockSpec(memory_space=pltpu.VMEM)] * len(outs),
-        compiler_params=pltpu.CompilerParams(vmem_limit_bytes=40 * 2**20),
+        compiler_params=pltpu.CompilerParams(vmem_limit_bytes=16 * 2**20),
         cost_estimate=pl.CostEstimate(flops=flops, bytes_accessed=2**20, transcendentals=0),
     )(*args)
+
+
+def hold_kernel(rows, out):
+    out[...] = rows[...]
+
+
+def finish_kernel(scale, own, got, result):
+    result[...] = (own[...] + got[...]) * scale[...]
 
 
 def body(
@@ -99,6 +109,7 @@
         bias_mid.reshape(1, -1),
         weight_out,
         ard_scales.reshape(1, -1),
+        signal_scale.reshape(1, 1),
     )
     block, nvec = row_vectors.shape
     emb = weight_out.shape[1]
@@ -115,19 +126,20 @@
         )
 
     rows = jnp.concatenate([row_points, row_vectors], axis=1)
-    rows = jnp.concatenate([rows, swap(rows, row_masks[0])], axis=0)
+    (rows,) = call(hold_kernel, [jax.ShapeDtypeStruct(rows.shape, BF16)], (rows,), HOLD_FLOPS)
+    *weights, scale = weights
+    for mask in row_masks[:-2]:
+        rows = jnp.concatenate([rows, swap(rows, mask)], axis=0)
     points, vectors = [col_points.T], [col_vectors.T]
-    feats = [col_feats(points[0])]
     for mask in col_masks:
         points.append(swap(jnp.concatenate(points, axis=1), mask))
         vectors.append(swap(jnp.concatenate(vectors, axis=1), mask))
-        if mask == col_masks[0]:
-            rows, points[1], feats[0] = lax.optimization_barrier((rows, points[1], feats[0]))
-        feats.append(col_feats(points[-1]))
-    for mask in row_masks[1:-1]:
-        rows = jnp.concatenate([rows, swap(rows, mask)], axis=0)
+    feats = [col_feats(p) for p in points[:-1]]
+    rows = jnp.concatenate([rows, swap(rows, row_masks[-2])], axis=0)
     rows, feats = lax.optimization_barrier((rows, feats))
     far_rows = swap(rows, row_masks[-1])
+    feats.append(col_feats(points[-1]))
+    far_rows, feats = lax.optimization_barrier((far_rows, feats))
 
     count_rows = rows.shape[0]
     sides = [v.shape[1] for v in vectors]
@@ -139,21 +151,26 @@
         flops=2 * count_rows * (layers + sum(sides) * (emb + 8 * nvec)),
     )
     columns = [a for f, v in zip(feats, vectors, strict=True) for a in (*f, v)]
-    row_near, *near = panel((rows, *columns, *weights))
-    row_far, *col_sums = panel((far_rows, *columns, *weights, *near))
+    row_far, *far = panel((far_rows, *columns, *weights))
+    row_near, *col_sums = panel((rows, *columns, *weights, *far))
 
-    row_sum = row_near + swap(row_far, row_masks[-1])
-    for number, mask in reversed(list(enumerate(col_masks))):
+    got, col_sums = lax.optimization_barrier((swap(row_far, row_masks[-1]), col_sums))
+    row_sum = row_near + got
+    for number, mask in reversed(list(enumerate(col_masks))[1:]):
         got, start = swap(col_sums[number + 1], mask), 0
         for side in range(number + 1):
             col_sums[side] = col_sums[side] + got[:, start : start + sides[side]]
             start += sides[side]
+    got = swap(col_sums[1], col_masks[0])
+    (col_result,) = call(
+        finish_kernel, [jax.ShapeDtypeStruct(got.shape, F32)], (scale, col_sums[0], got), FINISH_FLOPS
+    )
     for mask in reversed(row_masks[1:-1]):
         keep, give = jnp.split(row_sum, 2, axis=0)
         row_sum = keep + swap(give, mask)
-    row_sum, col_sum = lax.optimization_barrier((row_sum, col_sums[0]))
-    row_sum = row_sum[:, :nvec] + swap(row_sum, row_masks[0])[:, nvec:]
-    return (row_sum * signal_scale[0], col_sum.T * signal_scale[0])
+    got, col_result = lax.optimization_barrier((swap(row_sum, row_masks[0]), col_result))
+    row_sum = row_sum[:, :nvec] + got[:, nvec:]
+    return (row_sum * scale, col_result.T)
 
 
 def solution(mesh):

time: 42.3 us -> 34.7 us (0.82)
  waiting for transfers between devices: 11.1 us -> 5.88 us
  local copies, waits for them, and re-layouts: 5.1 us -> 0.69 us
  starting transfers between devices: 14.7 us -> 16.9 us
  other arithmetic: 2.35 us -> 1.59 us
  Pallas kernels: 7.14 us -> 7.88 us
    ppermute x12, waiting for transfers between devices: 11.1 us -> 5.88 us  [swap(): return lax.ppermute(block, AXES, [(i, i ^ mask) for i in range(devices)])]
    unnamed x26 -> x16, local copies, waits for them, and re-layouts: 5.1 us -> 0.69 us
    ppermute x12, starting transfers between devices: 14.7 us -> 16.9 us  [swap(): return lax.ppermute(block, AXES, [(i, i ^ mask) for i in range(devices)])]
    pallas_call x5 -> x7, Pallas kernels: 7.14 us -> 7.88 us  [call(): pl.pallas_call(kernel, out_shape=outs, in_specs=[pl.BlockSpec(memory_spac...]
    mul x2 -> x1, other arithmetic: 1.36 us -> 0.69 us  [body(): return (row_sum * scale, col_result.T)]
  transfers between devices with their start and end apart: 12 -> 12, of which waited for: 6 -> 7; matrix products, arithmetic and copies ran while one was open for 2% -> 3% of each run, Pallas kernels for 13% -> 17%
where the time goes in v3:
time: 34.7 us; the launch traced here: 34.4 us
  starting transfers between devices  16.9 us (49%)
  Pallas kernels  7.88 us (23%)
  waiting for transfers between devices  5.88 us (17%)
  other arithmetic  1.59 us (5%)
  between operations  1.43 us (4%)
  local copies, waits for them, and re-layouts  0.69 us (2%)
    ppermute x12, starting transfers between devices, swap(): return lax.ppermute(block, AXES, [(i, i ^ mask) for i in range(devices)])  16.9 us
    pallas_call x7, Pallas kernels, call(): pl.pallas_call(kernel, out_shape=outs, in_specs=[pl.BlockSpec(memory_spac...  7.88 us
    ppermute x12, waiting for transfers between devices, swap(): return lax.ppermute(block, AXES, [(i, i ^ mask) for i in range(devices)])  5.88 us
    concatenate x1, other arithmetic, body(): rows = jnp.concatenate([row_points, row_vectors], axis=1)  0.81 us
    mul x1, other arithmetic, body(): return (row_sum * scale, col_result.T)  0.69 us
  transfers between devices with their start and end apart: 12, of which 7 were waited for; matrix products, arithmetic and copies ran while one was open for 3% of the time, Pallas kernels for 17%

profile of v3, /device:TPU:0, one launch (start us, length us, event | category | flops | bytes accessed | tf_op | source)
XLA Modules:
  0.0 34.4 jit_solution(13778555513869334543)
XLA Ops:
  0.6 3.0 %collective-permute-start.2 = (bf16[64,512]{1,0:T(8,128)(2,1)}, bf16[64,512]{1,0:T(8,128)(2,1)S(1)}, u32[]{:S(2)}, u32[]{:S(2)}) collective-permute-start(bf16[64,512]{1,0:T(8,128)(2,1)} %bitcast.10), channel_id=1, source_target_pairs={{0,8},{1,9},{2,10},{3,11},{4,12},{5,13},{6,14},{7,15},{8,0},{9,1},... | collective-permute-start | bytes 196616 | tf_op jit(solution)/shard_map/ppermute | solution.py:103
  3.6 0.8 %pad_maximum_fusion.4.rows = bf16[64,128]{1,0:T(8,128)(2,1)S(1)} fusion(bf16[64,64]{1,0:T(8,128)(2,1)} %param.13, bf16[64,64]{1,0:T(8,128)(2,1)} %param.11), kind=kLoop, calls=%fused_computation.9 | loop fusion | flops 32768 | bytes 32768 | tf_op jit(solution)/shard_map/concatenate | solution.py:128
  4.4 0.0 copy-start.1
  4.5 0.0 copy-start
  4.5 0.0 copy-start.2
  4.5 0.0 copy-start.3
  4.5 0.0 copy-start.4
  4.5 0.0 copy-start.6
  4.5 2.7 %collective-permute-start = (bf16[64,128]{1,0:T(8,128)(2,1)S(1)}, bf16[64,128]{1,0:T(8,128)(2,1)S(1)}, u32[]{:S(2)}, u32[]{:S(2)}) collective-permute-start(bf16[64,128]{1,0:T(8,128)(2,1)S(1)} %shard_map.122), channel_id=1, source_target_pairs={{0,2},{1,3},{2,0},{3,1},{4,6},{5,7},{6,4},{7,5},{8,10},{9,11},{10,... | collective-permute-start | bytes 49160 | tf_op jit(solution)/shard_map/ppermute | solution.py:103
  7.2 0.0 copy-done.1
  7.2 0.5 %collective-permute-start.5 = (bf16[64,512]{1,0:T(8,128)(2,1)S(1)}, bf16[64,512]{1,0:T(8,128)(2,1)S(1)}, u32[]{:S(2)}, u32[]{:S(2)}) collective-permute-start(bf16[64,512]{1,0:T(8,128)(2,1)S(1)} %bitcast.13), channel_id=1, source_target_pairs={{0,8},{1,9},{2,10},{3,11},{4,12},{5,13},{6,14},{7,15},{8,0},{9,1},... | collective-permute-start | bytes 196616 | tf_op jit(solution)/shard_map/ppermute | solution.py:103
  7.7 0.0 copy-start.5
  7.7 0.0 copy-start.7
  7.7 0.0 copy-done
  7.7 0.0 copy-done.2
  7.7 0.0 copy-done.3
  7.7 0.0 copy-done.4
  7.7 0.0 copy-done.6
  7.8 0.6 %copy-done.5 = f32[512]{0:T(512)S(1)} copy-done((f32[512]{0:T(512)S(1)}, f32[512]{0:T(512)}, u32[]{:S(2)}) %copy-start.5) | copy-done | bytes 2072
  8.4 0.0 copy-done.7
  8.4 0.9 %shard_map.123 = (bf16[256,512]{1,0:T(8,128)(2,1)S(1)}, f32[1,512]{1,0:T(1,128)S(1)}) custom-call(bf16[64,512]{1,0:T(8,128)(2,1)S(1)} %bitcast.11, bf16[64,512]{1,0:T(8,128)(2,1)S(1)} %copy-done.4, f32[1,512]{1,0:T(1,128)S(1)} %bitcast.17, bf16[512,512]{1,0:T(8,128)(2,1)S(1)} %copy-done.2, f32[1,512]{1,0:T(1,128)S(1)} %bitcast.22, ...), custom_call_target="tpu_custom_call" | custom-call | flops 436207616 | bytes 1048576 | tf_op jit(solution)/shard_map/pallas_call | solution.py:66
  9.4 0.0 collective-permute-done
  9.4 1.6 %collective-permute-start.1 = (bf16[128,128]{1,0:T(8,128)(2,1)S(1)}, bf16[128,128]{1,0:T(8,128)(2,1)S(1)}, u32[]{:S(2)}, u32[]{:S(2)}) collective-permute-start(bf16[128,128]{1,0:T(8,128)(2,1)S(1)} %pad_maximum_fusion.3), channel_id=1, source_target_pairs={{0,1},{1,0},{2,3},{3,2},{4,5},{5,4},{6,7},{7,6},{8,9},{9,8},{10,11... | collective-permute-start | bytes 98312 | tf_op jit(solution)/shard_map/ppermute | solution.py:103
  11.0 0.0 collective-permute-done.2.points
  11.0 0.1 collective-permute-start.4
  11.1 0.3 collective-permute-done.5.rest_5_
  11.5 0.2 collective-permute-start.6
  11.7 1.7 %collective-permute-done.1 = bf16[128,128]{1,0:T(8,128)(2,1)S(1)} collective-permute-done((bf16[128,128]{1,0:T(8,128)(2,1)S(1)}, bf16[128,128]{1,0:T(8,128)(2,1)S(1)}, u32[]{:S(2)}, u32[]{:S(2)}) %collective-permute-start.1) | collective-permute-done | bytes 32800 | tf_op jit(solution)/shard_map/ppermute | solution.py:103
  13.4 0.9 %shard_map.124 = (bf16[256,512]{1,0:T(8,128)(2,1)S(1)}, f32[1,512]{1,0:T(1,128)S(1)}) custom-call(bf16[64,512]{1,0:T(8,128)(2,1)S(1)} %collective-permute-done.2.points, bf16[64,512]{1,0:T(8,128)(2,1)S(1)} %copy-done.4, f32[1,512]{1,0:T(1,128)S(1)} %bitcast.18, bf16[512,512]{1,0:T(8,128)(2,1)S(1)} %copy-done.2, f32[1,512]{1,0:T(1,128)S(1)} %bitcast.23, ...), custom_call_target="tpu_custom_call" | custom-call | flops 436207616 | bytes 1048576 | tf_op jit(solution)/shard_map/pallas_call | solution.py:66
  14.3 1.6 %collective-permute-start.3 = (bf16[256,128]{1,0:T(8,128)(2,1)S(1)}, bf16[256,128]{1,0:T(8,128)(2,1)S(1)}, u32[]{:S(2)}, u32[]{:S(2)}) collective-permute-start(bf16[256,128]{1,0:T(8,128)(2,1)S(1)} %pad_maximum_fusion.2.rows), channel_id=1, source_target_pairs={{0,16},{1,17},{2,18},{3,19},{4,20},{5,21},{6,22},{7,23},{8,24},{9,... | collective-permute-start | bytes 196616 | tf_op jit(solution)/shard_map/ppermute | solution.py:103
  15.9 0.0 collective-permute-done.4.points
  15.9 1.5 %shard_map.125 = (bf16[256,1024]{1,0:T(8,128)(2,1)S(1)}, f32[1,1024]{1,0:T(1,128)S(1)}) custom-call(bf16[64,1024]{1,0:T(8,128)(2,1)S(1)} %collective-permute-done.4.points, bf16[64,512]{1,0:T(8,128)(2,1)S(1)} %copy-done.4, f32[1,512]{1,0:T(1,128)S(1)} %bitcast.19, bf16[512,512]{1,0:T(8,128)(2,1)S(1)} %copy-done.2, f32[1,512]{1,0:T(1,128)S(1)} %bitcast.24, ...), custom_call_target="tpu_custom_call" | custom-call | flops 872415232 | bytes 1048576 | tf_op jit(solution)/shard_map/pallas_call | solution.py:66
  17.4 1.2 %collective-permute-done.3.rows = bf16[256,128]{1,0:T(8,128)(2,1)S(1)} collective-permute-done((bf16[256,128]{1,0:T(8,128)(2,1)S(1)}, bf16[256,128]{1,0:T(8,128)(2,1)S(1)}, u32[]{:S(2)}, u32[]{:S(2)}) %collective-permute-start.3) | collective-permute-done | bytes 65568 | tf_op jit(solution)/shard_map/ppermute | solution.py:103
  18.6 0.0 collective-permute-done.6.rest_8_
  18.6 1.9 %shard_map.126 = (f32[128,128]{1,0:T(8,128)S(1)}, f32[64,512]{1,0:T(8,128)S(1)}, f32[64,512]{1,0:T(8,128)S(1)}, f32[64,1024]{1,0:T(8,128)S(1)}) custom-call(bf16[256,128]{1,0:T(8,128)(2,1)S(1)} %collective-permute-done.3.rows, bf16[256,512]{1,0:T(8,128)(2,1)S(1)} %get-tuple-element.45.rest_0_, f32[1,512]{1,0:T(1,128)S(1)} %get-tuple-element.46.rest_1_, ...), custom_call_target="tpu_custom_call" | custom-call | flops 1023410176 | bytes 1048576 | tf_op jit(solution)/shard_map/pallas_call | solution.py:66
  20.5 1.6 %collective-permute-start.7 = (f32[128,128]{1,0:T(8,128)S(1)}, f32[128,128]{1,0:T(8,128)S(1)}, u32[]{:S(2)}, u32[]{:S(2)}) collective-permute-start(f32[128,128]{1,0:T(8,128)S(1)} %get-tuple-element.56), channel_id=1, source_target_pairs={{0,16},{1,17},{2,18},{3,19},{4,20},{5,21},{6,22},{7,23},{8,24},{9,... | collective-permute-start | bytes 196616 | tf_op jit(solution)/shard_map/ppermute | solution.py:103
  22.1 1.9 %shard_map.127 = (f32[128,128]{1,0:T(8,128)S(1)}, f32[64,512]{1,0:T(8,128)S(1)}, f32[64,512]{1,0:T(8,128)S(1)}, f32[64,1024]{1,0:T(8,128)S(1)}) custom-call(bf16[256,128]{1,0:T(8,128)(2,1)S(1)} %pad_maximum_fusion.2.rows, bf16[256,512]{1,0:T(8,128)(2,1)S(1)} %get-tuple-element.45.rest_0_, f32[1,512]{1,0:T(1,128)S(1)} %get-tuple-element.46.rest_1_, ...), custom_call_target="tpu_custom_call" | custom-call | flops 1023410176 | bytes 1048576 | tf_op jit(solution)/shard_map/pallas_call | solution.py:66
  24.0 0.9 %collective-permute-done.7 = f32[128,128]{1,0:T(8,128)S(1)} collective-permute-done((f32[128,128]{1,0:T(8,128)S(1)}, f32[128,128]{1,0:T(8,128)S(1)}, u32[]{:S(2)}, u32[]{:S(2)}) %collective-permute-start.7) | collective-permute-done | bytes 65568 | tf_op jit(solution)/shard_map/ppermute | solution.py:103
  24.8 0.0 collective-permute-start.10
  24.9 1.6 %collective-permute-start.8 = (f32[64,128]{1,0:T(8,128)S(1)}, f32[64,128]{1,0:T(8,128)S(1)}, u32[]{:S(2)}, u32[]{:S(2)}) collective-permute-start(f32[64,128]{1,0:T(8,128)S(1)} %split.9), channel_id=1, source_target_pairs={{0,1},{1,0},{2,3},{3,2},{4,5},{5,4},{6,7},{7,6},{8,9},{9,8},{10,11... | collective-permute-start | bytes 98312 | tf_op jit(solution)/shard_map/ppermute | solution.py:103
  26.5 0.0 collective-permute-done.10
  26.6 1.5 %collective-permute-start.11 = (f32[64,512]{1,0:T(8,128)S(1)}, f32[64,512]{1,0:T(8,128)S(1)}, u32[]{:S(2)}, u32[]{:S(2)}) collective-permute-start(f32[64,512]{1,0:T(8,128)S(1)} %get-tuple-element.66), channel_id=1, source_target_pairs={{0,8},{1,9},{2,10},{3,11},{4,12},{5,13},{6,14},{7,15},{8,0},{9,1},... | collective-permute-start | bytes 393224 | tf_op jit(solution)/shard_map/ppermute | solution.py:103
  28.1 0.7 %collective-permute-done.8 = f32[64,128]{1,0:T(8,128)S(1)} collective-permute-done((f32[64,128]{1,0:T(8,128)S(1)}, f32[64,128]{1,0:T(8,128)S(1)}, u32[]{:S(2)}, u32[]{:S(2)}) %collective-permute-start.8) | collective-permute-done | bytes 32800 | tf_op jit(solution)/shard_map/ppermute | solution.py:103
  28.9 2.4 %collective-permute-start.9 = (f32[64,128]{1,0:T(8,128)S(1)}, f32[64,128]{1,0:T(8,128)S(1)}, u32[]{:S(2)}, u32[]{:S(2)}) collective-permute-start(f32[64,128]{1,0:T(8,128)S(1)} %slice_add_fusion.3), channel_id=1, source_target_pairs={{0,2},{1,3},{2,0},{3,1},{4,6},{5,7},{6,4},{7,5},{8,10},{9,11},{10,... | collective-permute-start | bytes 98312 | tf_op jit(solution)/shard_map/ppermute | solution.py:103
  31.9 0.4 %collective-permute-done.11.got = f32[64,512]{1,0:T(8,128)S(1)} collective-permute-done((f32[64,512]{1,0:T(8,128)S(1)}, f32[64,512]{1,0:T(8,128)S(1)}, u32[]{:S(2)}, u32[]{:S(2)}) %collective-permute-start.11) | collective-permute-done | bytes 131104 | tf_op jit(solution)/shard_map/ppermute | solution.py:103
  32.3 0.7 %shard_map.128 = f32[64,512]{1,0:T(8,128)} custom-call(f32[1,1]{1,0:T(1,128)} %bitcast.8.scale, f32[64,512]{1,0:T(8,128)S(1)} %get-tuple-element.67.own, f32[64,512]{1,0:T(8,128)S(1)} %collective-permute-done.11.got), custom_call_target="tpu_custom_call" | custom-call | flops 1000000 | bytes 1048576 | tf_op jit(solution)/shard_map/pallas_call | solution.py:66
  33.0 0.7 %collective-permute-done.9 = f32[64,128]{1,0:T(8,128)S(1)} collective-permute-done((f32[64,128]{1,0:T(8,128)S(1)}, f32[64,128]{1,0:T(8,128)S(1)}, u32[]{:S(2)}, u32[]{:S(2)}) %collective-permute-start.9) | collective-permute-done | bytes 32800 | tf_op jit(solution)/shard_map/ppermute | solution.py:103
  33.7 0.7 %fusion = f32[64,64]{1,0:T(8,128)} fusion(f32[64,128]{1,0:T(8,128)S(1)} %slice_add_fusion.3, f32[64,128]{1,0:T(8,128)S(1)} %collective-permute-done.9, f32[]{:T(128)} %bitcast.9), kind=kLoop, calls=%fused_computation.6 | loop fusion | flops 8192 | bytes 49156 | tf_op jit(solution)/shard_map/mul | solution.py:173
  (9 shorter events, 0.1 us)
Async XLA Ops:
  0.6 10.4 %collective-permute-start.2 = (bf16[64,512]{1,0:T(8,128)(2,1)}, bf16[64,512]{1,0:T(8,128)(2,1)S(1)}, u32[]{:S(2)}, u32[]{:S(2)}) collective-permute-start(bf16[64,512]{1,0:T(8,128)(2,1)} %bitcast.10), channel_id=1, source_target_pairs={{0,8},{1,9},{2,10},{3,11},{4,12},{5,13},{6,14},{7,15},{8,0},{9,1},... | collective-permute-start | bytes 196616 | tf_op jit(solution)/shard_map/ppermute | solution.py:103
  4.4 2.7 %copy-start.1 = (bf16[512,64]{0,1:T(8,128)(2,1)S(1)}, bf16[512,64]{0,1:T(8,128)(2,1)}, u32[]{:S(2)}) copy-start(bf16[512,64]{0,1:T(8,128)(2,1)} %param.14) | copy-start | bytes 196612
  4.5 3.3 %copy-start = (bf16[512,64]{0,1:T(8,128)(2,1)S(1)}, bf16[512,64]{0,1:T(8,128)(2,1)}, u32[]{:S(2)}) copy-start(bf16[512,64]{0,1:T(8,128)(2,1)} %param.12) | copy-start | bytes 196612
  4.5 3.3 %copy-start.2 = (bf16[512,512]{1,0:T(8,128)(2,1)S(1)}, bf16[512,512]{1,0:T(8,128)(2,1)}, u32[]{:S(2)}) copy-start(bf16[512,512]{1,0:T(8,128)(2,1)} %rest_11_.3) | copy-start | bytes 1572868
  4.5 3.3 %copy-start.3 = (bf16[512,256]{1,0:T(8,128)(2,1)S(1)}, bf16[512,256]{1,0:T(8,128)(2,1)}, u32[]{:S(2)}) copy-start(bf16[512,256]{1,0:T(8,128)(2,1)} %rest_13_.3) | copy-start | bytes 786436
  4.5 3.3 %copy-start.4 = (bf16[64,512]{1,0:T(8,128)(2,1)S(1)}, bf16[64,512]{1,0:T(8,128)(2,1)}, u32[]{:S(2)}) copy-start(bf16[64,512]{1,0:T(8,128)(2,1)} %rest_9_.3) | copy-start | bytes 196612
  4.5 3.2 %copy-start.6 = (f32[512]{0:T(512)S(1)}, f32[512]{0:T(512)}, u32[]{:S(2)}) copy-start(f32[512]{0:T(512)} %param.18) | copy-start | bytes 6148
  4.5 4.8 %collective-permute-start = (bf16[64,128]{1,0:T(8,128)(2,1)S(1)}, bf16[64,128]{1,0:T(8,128)(2,1)S(1)}, u32[]{:S(2)}, u32[]{:S(2)}) collective-permute-start(bf16[64,128]{1,0:T(8,128)(2,1)S(1)} %shard_map.122), channel_id=1, source_target_pairs={{0,2},{1,3},{2,0},{3,1},{4,6},{5,7},{6,4},{7,5},{8,10},{9,11},{10,... | collective-permute-start | bytes 49160 | tf_op jit(solution)/shard_map/ppermute | solution.py:103
  7.2 4.3 %collective-permute-start.5 = (bf16[64,512]{1,0:T(8,128)(2,1)S(1)}, bf16[64,512]{1,0:T(8,128)(2,1)S(1)}, u32[]{:S(2)}, u32[]{:S(2)}) collective-permute-start(bf16[64,512]{1,0:T(8,128)(2,1)S(1)} %bitcast.13), channel_id=1, source_target_pairs={{0,8},{1,9},{2,10},{3,11},{4,12},{5,13},{6,14},{7,15},{8,0},{9,1},... | collective-permute-start | bytes 196616 | tf_op jit(solution)/shard_map/ppermute | solution.py:103
  7.7 0.7 %copy-start.5 = (f32[512]{0:T(512)S(1)}, f32[512]{0:T(512)}, u32[]{:S(2)}) copy-start(f32[512]{0:T(512)} %param.16) | copy-start | bytes 6148
  7.7 0.7 %copy-start.7 = (f32[256]{0:T(256)S(1)}, f32[256]{0:T(256)}, u32[]{:S(2)}) copy-start(f32[256]{0:T(256)} %param.20) | copy-start | bytes 3076
  9.4 4.0 %collective-permute-start.1 = (bf16[128,128]{1,0:T(8,128)(2,1)S(1)}, bf16[128,128]{1,0:T(8,128)(2,1)S(1)}, u32[]{:S(2)}, u32[]{:S(2)}) collective-permute-start(bf16[128,128]{1,0:T(8,128)(2,1)S(1)} %pad_maximum_fusion.3), channel_id=1, source_target_pairs={{0,1},{1,0},{2,3},{3,2},{4,5},{5,4},{6,7},{7,6},{8,9},{9,8},{10,11... | collective-permute-start | bytes 98312 | tf_op jit(solution)/shard_map/ppermute | solution.py:103
  11.0 4.9 %collective-permute-start.4 = (bf16[64,1024]{1,0:T(8,128)(2,1)S(1)}, bf16[64,1024]{1,0:T(8,128)(2,1)S(1)}, u32[]{:S(2)}, u32[]{:S(2)}) collective-permute-start(bf16[64,1024]{1,0:T(8,128)(2,1)S(1)} %pad_maximum_fusion), channel_id=1, source_target_pairs={{0,4},{1,5},{2,6},{3,7},{4,0},{5,1},{6,2},{7,3},{8,12},{9,13},{10,... | collective-permute-start | bytes 393224 | tf_op jit(solution)/shard_map/ppermute | solution.py:103
  11.5 7.2 %collective-permute-start.6 = (bf16[64,1024]{1,0:T(8,128)(2,1)S(1)}, bf16[64,1024]{1,0:T(8,128)(2,1)S(1)}, u32[]{:S(2)}, u32[]{:S(2)}) collective-permute-start(bf16[64,1024]{1,0:T(8,128)(2,1)S(1)} %pad_maximum_fusion.1), channel_id=1, source_target_pairs={{0,4},{1,5},{2,6},{3,7},{4,0},{5,1},{6,2},{7,3},{8,12},{9,13},{10,... | collective-permute-start | bytes 393224 | tf_op jit(solution)/shard_map/ppermute | solution.py:103
  14.3 4.3 %collective-permute-start.3 = (bf16[256,128]{1,0:T(8,128)(2,1)S(1)}, bf16[256,128]{1,0:T(8,128)(2,1)S(1)}, u32[]{:S(2)}, u32[]{:S(2)}) collective-permute-start(bf16[256,128]{1,0:T(8,128)(2,1)S(1)} %pad_maximum_fusion.2.rows), channel_id=1, source_target_pairs={{0,16},{1,17},{2,18},{3,19},{4,20},{5,21},{6,22},{7,23},{8,24},{9,... | collective-permute-start | bytes 196616 | tf_op jit(solution)/shard_map/ppermute | solution.py:103
  20.5 4.3 %collective-permute-start.7 = (f32[128,128]{1,0:T(8,128)S(1)}, f32[128,128]{1,0:T(8,128)S(1)}, u32[]{:S(2)}, u32[]{:S(2)}) collective-permute-start(f32[128,128]{1,0:T(8,128)S(1)} %get-tuple-element.56), channel_id=1, source_target_pairs={{0,16},{1,17},{2,18},{3,19},{4,20},{5,21},{6,22},{7,23},{8,24},{9,... | collective-permute-start | bytes 196616 | tf_op jit(solution)/shard_map/ppermute | solution.py:103
  24.8 1.7 %collective-permute-start.10 = (f32[64,1024]{1,0:T(8,128)S(1)}, f32[64,1024]{1,0:T(8,128)S(1)}, u32[]{:S(2)}, u32[]{:S(2)}) collective-permute-start(f32[64,1024]{1,0:T(8,128)S(1)} %get-tuple-element.62), channel_id=1, source_target_pairs={{0,4},{1,5},{2,6},{3,7},{4,0},{5,1},{6,2},{7,3},{8,12},{9,13},{10,... | collective-permute-start | bytes 786440 | tf_op jit(solution)/shard_map/ppermute | solution.py:103
  24.9 4.0 %collective-permute-start.8 = (f32[64,128]{1,0:T(8,128)S(1)}, f32[64,128]{1,0:T(8,128)S(1)}, u32[]{:S(2)}, u32[]{:S(2)}) collective-permute-start(f32[64,128]{1,0:T(8,128)S(1)} %split.9), channel_id=1, source_target_pairs={{0,1},{1,0},{2,3},{3,2},{4,5},{5,4},{6,7},{7,6},{8,9},{9,8},{10,11... | collective-permute-start | bytes 98312 | tf_op jit(solution)/shard_map/ppermute | solution.py:103
  26.6 5.7 %collective-permute-start.11 = (f32[64,512]{1,0:T(8,128)S(1)}, f32[64,512]{1,0:T(8,128)S(1)}, u32[]{:S(2)}, u32[]{:S(2)}) collective-permute-start(f32[64,512]{1,0:T(8,128)S(1)} %get-tuple-element.66), channel_id=1, source_target_pairs={{0,8},{1,9},{2,10},{3,11},{4,12},{5,13},{6,14},{7,15},{8,0},{9,1},... | collective-permute-start | bytes 393224 | tf_op jit(solution)/shard_map/ppermute | solution.py:103
  28.9 4.8 %collective-permute-start.9 = (f32[64,128]{1,0:T(8,128)S(1)}, f32[64,128]{1,0:T(8,128)S(1)}, u32[]{:S(2)}, u32[]{:S(2)}) collective-permute-start(f32[64,128]{1,0:T(8,128)S(1)} %slice_add_fusion.3), channel_id=1, source_target_pairs={{0,2},{1,3},{2,0},{3,1},{4,6},{5,7},{6,4},{7,5},{8,10},{9,11},{10,... | collective-permute-start | bytes 98312 | tf_op jit(solution)/shard_map/ppermute | solution.py:103

commit v4 on v3

--- a/solution.py
+++ b/solution.py
@@ -23,10 +23,11 @@
     return (dot(two, w_out[...], ((1,), (0,))) * jnp.sqrt(ard[...])).astype(BF16)
 
 
-def col_kernel(chunk, points, w_in, b_in, w_mid, b_mid, w_out, ard, feats, half_sq):
+def col_kernel(chunk, points, *rest):
+    weights, (feats, half_sq) = rest[:6], rest[-2:]
     for start in range(0, points.shape[1], chunk):
         part = pl.ds(start, chunk)
-        turned = embed(points[:, part], 0, w_in, b_in, w_mid, b_mid, w_out, ard).T
+        turned = embed(points[:, part], 0, *weights).T
         feats[:, part] = turned
         half_sq[:, part] = 0.5 * jnp.sum(jnp.square(turned.astype(F32)), axis=0, keepdims=True)
 
@@ -34,14 +35,18 @@
 def panel_kernel(chunk_rows, chunk_cols, tall, sides, rows, *rest):
     columns = [rest[3 * side : 3 * side + 3] for side in range(sides)]
     weights, rest = rest[3 * sides : 3 * sides + 6], rest[3 * sides + 6 :]
-    before, row_out, col_outs = rest[: -sides - 1], rest[-sides - 1], rest[-sides:]
+    keep = len(rest) == 1 + sides
+    if keep:
+        row_out, *panels = rest
+    else:
+        others, panels, row_out, col_outs = rest[0], rest[1 : 1 + sides], rest[1 + sides], rest[2 + sides :]
     width = weights[0].shape[0]
     own = rows.shape[1] - width
     for at in range(0, rows.shape[0], chunk_rows):
-        block = rows[at : at + chunk_rows, :]
+        here = pl.ds(at, chunk_rows)
+        block = rows[here, :]
         row_feats = embed(block[:, :width], 1, *weights)
         row_half = 0.5 * jnp.sum(jnp.square(row_feats.astype(F32)), axis=1, keepdims=True)
-        vecs = block[:, width:]
         row_acc = None
         for side, (feats, half_sq, col_vecs) in enumerate(columns):
             for start in range(0, feats.shape[1], chunk_cols):
@@ -50,16 +55,18 @@
                 kernel = jnp.exp(inner - row_half - half_sq[:, part]).astype(BF16)
                 term = dot(kernel, col_vecs[:, part], ((1,), (1,)))
                 row_acc = term if row_acc is None else row_acc + term
-                col_term = dot(vecs, kernel, ((0,), (0,)))
-                if at > 0:
-                    col_term = col_term + col_outs[side][:, part]
-                elif before:
-                    col_term = col_term + before[side][:, part]
-                col_outs[side][:, part] = col_term
-        for pair in range(0, chunk_rows, 2 * tall):
-            to = pl.ds((at + pair) // 2, tall)
-            row_out[to, :own] = row_acc[pair : pair + tall]
-            row_out[to, own:] = row_acc[pair + tall : pair + 2 * tall]
+                if keep:
+                    panels[side][here, part] = kernel
+                else:
+                    col_term = dot(block[:, width:], kernel, ((0,), (0,)))
+                    col_term += dot(others[here, width:], panels[side][here, part], ((0,), (0,)))
+                    if at > 0:
+                        col_term += col_outs[side][:, part]
+                    col_outs[side][:, part] = col_term
+        for start in range(0, chunk_rows, 2 * tall):
+            to = pl.ds((at + start) // 2, tall)
+            row_out[to, :own] = row_acc[start : start + tall]
+            row_out[to, own:] = row_acc[start + tall : start + 2 * tall]
 
 
 def call(kernel, outs, args, flops):
@@ -68,7 +75,7 @@
         out_shape=outs,
         in_specs=[pl.BlockSpec(memory_space=pltpu.VMEM)] * len(args),
         out_specs=[pl.BlockSpec(memory_space=pltpu.VMEM)] * len(outs),
-        compiler_params=pltpu.CompilerParams(vmem_limit_bytes=16 * 2**20),
+        compiler_params=pltpu.CompilerParams(vmem_limit_bytes=20 * 2**20),
         cost_estimate=pl.CostEstimate(flops=flops, bytes_accessed=2**20, transcendentals=0),
     )(*args)
 
@@ -79,6 +86,13 @@
 
 def finish_kernel(scale, own, got, result):
     result[...] = (own[...] + got[...]) * scale[...]
+
+
+def finish_rows_kernel(scale, own, got, result):
+    tall, width = got.shape[0], result.shape[1]
+    total = (own[:tall, :] + got[...]) * scale[...]
+    result[:tall, :] = total[:, :width]
+    result[tall:, :] = total[:, width:]
 
 
 def body(
@@ -125,34 +139,35 @@
             2 * count * layers,
         )
 
+    *weights, scale = weights
     rows = jnp.concatenate([row_points, row_vectors], axis=1)
-    (rows,) = call(hold_kernel, [jax.ShapeDtypeStruct(rows.shape, BF16)], (rows,), HOLD_FLOPS)
-    *weights, scale = weights
-    for mask in row_masks[:-2]:
+    (got,) = call(hold_kernel, [jax.ShapeDtypeStruct(rows.shape, BF16)], (swap(rows, row_masks[0]),), HOLD_FLOPS)
+    rows = jnp.concatenate([rows, got], axis=0)
+    for mask in row_masks[1:-2]:
         rows = jnp.concatenate([rows, swap(rows, mask)], axis=0)
     points, vectors = [col_points.T], [col_vectors.T]
     for mask in col_masks:
         points.append(swap(jnp.concatenate(points, axis=1), mask))
-        vectors.append(swap(jnp.concatenate(vectors, axis=1), mask))
-    feats = [col_feats(p) for p in points[:-1]]
-    rows = jnp.concatenate([rows, swap(rows, row_masks[-2])], axis=0)
-    rows, feats = lax.optimization_barrier((rows, feats))
+    feats = [col_feats(points[0])]
+    got, feats = lax.optimization_barrier((swap(rows, row_masks[-2]), feats))
+    rows = jnp.concatenate([rows, got], axis=0)
     far_rows = swap(rows, row_masks[-1])
-    feats.append(col_feats(points[-1]))
+    feats += [col_feats(p) for p in points[1:]]
+    for mask in col_masks:
+        vectors.append(jnp.concatenate([swap(v, mask) for v in vectors], axis=1))
     far_rows, feats = lax.optimization_barrier((far_rows, feats))
 
     count_rows = rows.shape[0]
     sides = [v.shape[1] for v in vectors]
-    panel = functools.partial(
-        call,
-        functools.partial(panel_kernel, min(4 * block, count_rows), chunk_cols, block, len(sides)),
-        [jax.ShapeDtypeStruct((count_rows // 2, 2 * nvec), F32)]
-        + [jax.ShapeDtypeStruct((nvec, count), F32) for count in sides],
-        flops=2 * count_rows * (layers + sum(sides) * (emb + 8 * nvec)),
-    )
+    panel = functools.partial(panel_kernel, min(4 * block, count_rows), chunk_cols, block // 2, len(sides))
     columns = [a for f, v in zip(feats, vectors, strict=True) for a in (*f, v)]
-    row_far, *far = panel((far_rows, *columns, *weights))
-    row_near, *col_sums = panel((rows, *columns, *weights, *far))
+    flops = 2 * count_rows * (layers + sum(sides) * (emb + 4 * nvec))
+    sums = jax.ShapeDtypeStruct((count_rows // 2, 2 * nvec), F32)
+    far_panels = [jax.ShapeDtypeStruct((count_rows, count), BF16) for count in sides]
+    row_far, *far_panels = call(panel, [sums, *far_panels], (far_rows, *columns, *weights), flops)
+    col_sums = [jax.ShapeDtypeStruct((nvec, count), F32) for count in sides]
+    args = (rows, *columns, *weights, far_rows, *far_panels)
+    row_near, *col_sums = call(panel, [sums, *col_sums], args, flops)
 
     got, col_sums = lax.optimization_barrier((swap(row_far, row_masks[-1]), col_sums))
     row_sum = row_near + got
@@ -168,9 +183,11 @@
     for mask in reversed(row_masks[1:-1]):
         keep, give = jnp.split(row_sum, 2, axis=0)
         row_sum = keep + swap(give, mask)
-    got, col_result = lax.optimization_barrier((swap(row_sum, row_masks[0]), col_result))
-    row_sum = row_sum[:, :nvec] + got[:, nvec:]
-    return (row_sum * scale, col_result.T)
+    got, col_result = lax.optimization_barrier((swap(row_sum[block // 2 :], row_masks[0]), col_result))
+    (row_result,) = call(
+        finish_rows_kernel, [jax.ShapeDtypeStruct((block, nvec), F32)], (scale, row_sum, got), FINISH_FLOPS
+    )
+    return (row_result, col_result.T)
 
 
 def solution(mesh):

time: 34.7 us -> 32.3 us (0.931)
  waiting for transfers between devices: 5.88 us -> 3.61 us
  other arithmetic: 1.59 us -> 1.04 us
  Pallas kernels: 7.88 us -> 8.34 us
    ppermute x12 -> x13, waiting for transfers between devices: 5.88 us -> 3.61 us  [swap(): return lax.ppermute(block, AXES, [(i, i ^ mask) for i in range(devices)])]
    mul x1 -> x0, other arithmetic: 0.69 us -> none  [body(): return (row_sum * scale, col_result.T)]
    pallas_call x7 -> x8, Pallas kernels: 7.88 us -> 8.34 us  [call(): pl.pallas_call(kernel, out_shape=outs, in_specs=[pl.BlockSpec(memory_spac...]
    ppermute x12 -> x13, starting transfers between devices: 16.9 us -> 16.6 us  [swap(): return lax.ppermute(block, AXES, [(i, i ^ mask) for i in range(devices)])]
    unnamed x16 -> x21, local copies, waits for them, and re-layouts: 0.69 us -> 0.79 us
  transfers between devices with their start and end apart: 12 -> 13, of which waited for: 7 -> 5; matrix products, arithmetic and copies ran while one was open for 3% -> 1% of each run, Pallas kernels for 17% -> 19%
where the time goes in v4:
time: 32.3 us; the launch traced here: 31.9 us
  starting transfers between devices  16.6 us (51%)
  Pallas kernels  8.34 us (26%)
  waiting for transfers between devices  3.61 us (11%)
  between operations  1.44 us (4%)
  other arithmetic  1.04 us (3%)
  local copies, waits for them, and re-layouts  0.81 us (3%)
    ppermute x13, starting transfers between devices, swap(): return lax.ppermute(block, AXES, [(i, i ^ mask) for i in range(devices)])  16.6 us
    pallas_call x8, Pallas kernels, call(): pl.pallas_call(kernel, out_shape=outs, in_specs=[pl.BlockSpec(memory_spac...  8.34 us
    ppermute x13, waiting for transfers between devices, swap(): return lax.ppermute(block, AXES, [(i, i ^ mask) for i in range(devices)])  3.61 us
    concatenate x1, other arithmetic, body(): rows = jnp.concatenate([row_points, row_vectors], axis=1)  0.82 us
    unnamed x21, local copies, waits for them, and re-layouts  0.79 us
  transfers between devices with their start and end apart: 13, of which 5 were waited for; matrix products, arithmetic and copies ran while one was open for 1% of the time, Pallas kernels for 19%

profile of v4, /device:TPU:0, one launch (start us, length us, event | category | flops | bytes accessed | tf_op | source)
XLA Modules:
  0.0 31.9 jit_solution(7661221828252415370)
XLA Ops:
  0.6 0.8 %pad_maximum_fusion.3 = bf16[64,128]{1,0:T(8,128)(2,1)S(1)} fusion(bf16[64,64]{1,0:T(8,128)(2,1)} %param.13, bf16[64,64]{1,0:T(8,128)(2,1)} %param.11), kind=kLoop, calls=%fused_computation.6 | loop fusion | flops 32768 | bytes 32768 | tf_op jit(solution)/shard_map/concatenate | solution.py:143
  1.4 4.1 %collective-permute-start = (bf16[64,128]{1,0:T(8,128)(2,1)S(1)}, bf16[64,128]{1,0:T(8,128)(2,1)S(1)}, u32[]{:S(2)}, u32[]{:S(2)}) collective-permute-start(bf16[64,128]{1,0:T(8,128)(2,1)S(1)} %pad_maximum_fusion.3), channel_id=1, source_target_pairs={{0,2},{1,3},{2,0},{3,1},{4,6},{5,7},{6,4},{7,5},{8,10},{9,11},{10,... | collective-permute-start | bytes 49160 | tf_op jit(solution)/shard_map/ppermute | solution.py:117
  5.5 1.5 %collective-permute-start.5 = (bf16[64,512]{1,0:T(8,128)(2,1)}, bf16[64,512]{1,0:T(8,128)(2,1)S(1)}, u32[]{:S(2)}, u32[]{:S(2)}) collective-permute-start(bf16[64,512]{1,0:T(8,128)(2,1)} %bitcast.9), channel_id=1, source_target_pairs={{0,8},{1,9},{2,10},{3,11},{4,12},{5,13},{6,14},{7,15},{8,0},{9,1},... | collective-permute-start | bytes 196616 | tf_op jit(solution)/shard_map/ppermute | solution.py:117
  7.0 0.0 collective-permute-start.6
  7.0 0.0 copy-start.1
  7.0 0.6 %collective-permute-start.3 = (bf16[64,512]{1,0:T(8,128)(2,1)}, bf16[64,512]{1,0:T(8,128)(2,1)S(1)}, u32[]{:S(2)}, u32[]{:S(2)}) collective-permute-start(bf16[64,512]{1,0:T(8,128)(2,1)} %bitcast.13), channel_id=1, source_target_pairs={{0,8},{1,9},{2,10},{3,11},{4,12},{5,13},{6,14},{7,15},{8,0},{9,1},... | collective-permute-start | bytes 196616 | tf_op jit(solution)/shard_map/ppermute | solution.py:117
  7.6 0.0 collective-permute-done.rows
  7.6 0.1 copy-done.8
  7.7 0.0 copy-done.9
  7.7 0.1 pad_maximum_fusion.2
  7.8 1.6 %collective-permute-start.1 = (bf16[128,128]{1,0:T(8,128)(2,1)S(1)}, bf16[128,128]{1,0:T(8,128)(2,1)S(1)}, u32[]{:S(2)}, u32[]{:S(2)}) collective-permute-start(bf16[128,128]{1,0:T(8,128)(2,1)S(1)} %pad_maximum_fusion.2), channel_id=1, source_target_pairs={{0,1},{1,0},{2,3},{3,2},{4,5},{5,4},{6,7},{7,6},{8,9},{9,8},{10,11... | collective-permute-start | bytes 98312 | tf_op jit(solution)/shard_map/ppermute | solution.py:117
  9.4 0.0 copy-done
  9.4 0.0 copy-done.1
  9.4 0.0 copy-done.4
  9.4 0.0 copy-done.6
  9.4 0.0 copy-done.2
  9.4 0.6 %copy-done.5 = f32[512]{0:T(512)S(1)} copy-done((f32[512]{0:T(512)S(1)}, f32[512]{0:T(512)}, u32[]{:S(2)}) %copy-start.5) | copy-done | bytes 2072
  10.1 0.0 copy-done.7
  10.1 0.9 %shard_map.123 = (bf16[256,512]{1,0:T(8,128)(2,1)S(1)}, f32[1,512]{1,0:T(1,128)S(1)}) custom-call(bf16[64,512]{1,0:T(8,128)(2,1)S(1)} %bitcast.14, bf16[64,512]{1,0:T(8,128)(2,1)S(1)} %copy-done.2, f32[1,512]{1,0:T(1,128)S(1)} %bitcast.16, bf16[512,512]{1,0:T(8,128)(2,1)S(1)} %copy-done, f32[1,512]{1,0:T(1,128)S(1)} %bitcast.21, ...), custom_call_target="tpu_custom_call" | custom-call | flops 436207616 | bytes 1048576 | tf_op jit(solution)/shard_map/pallas_call | solution.py:73
  11.0 0.7 %collective-permute-done.1 = bf16[128,128]{1,0:T(8,128)(2,1)S(1)} collective-permute-done((bf16[128,128]{1,0:T(8,128)(2,1)S(1)}, bf16[128,128]{1,0:T(8,128)(2,1)S(1)}, u32[]{:S(2)}, u32[]{:S(2)}) %collective-permute-start.1) | collective-permute-done | bytes 32800 | tf_op jit(solution)/shard_map/ppermute | solution.py:117
  11.7 0.1 pad_maximum_fusion.1.rows
  11.8 1.5 %collective-permute-start.2 = (bf16[256,128]{1,0:T(8,128)(2,1)S(1)}, bf16[256,128]{1,0:T(8,128)(2,1)S(1)}, u32[]{:S(2)}, u32[]{:S(2)}) collective-permute-start(bf16[256,128]{1,0:T(8,128)(2,1)S(1)} %pad_maximum_fusion.1.rows), channel_id=1, source_target_pairs={{0,16},{1,17},{2,18},{3,19},{4,20},{5,21},{6,22},{7,23},{8,24},{9,... | collective-permute-start | bytes 196616 | tf_op jit(solution)/shard_map/ppermute | solution.py:117
  13.3 0.0 collective-permute-done.3.points
  13.4 0.1 collective-permute-start.4
  13.4 0.0 collective-permute-done.5.rest_5_
  13.4 0.5 %collective-permute-start.7 = (bf16[64,512]{1,0:T(8,128)(2,1)S(1)}, bf16[64,512]{1,0:T(8,128)(2,1)S(1)}, u32[]{:S(2)}, u32[]{:S(2)}) collective-permute-start(bf16[64,512]{1,0:T(8,128)(2,1)S(1)} %collective-permute-done.5.rest_5_), channel_id=1, source_target_pairs={{0,4},{1,5},{2,6},{3,7},{4,0},{5,1},{6,2},{7,3},{8,12},{9,13},{10,... | collective-permute-start | bytes 196616 | tf_op jit(solution)/shard_map/ppermute | solution.py:117
  13.9 0.0 collective-permute-done.6
  13.9 0.9 %shard_map.124 = (bf16[256,512]{1,0:T(8,128)(2,1)S(1)}, f32[1,512]{1,0:T(1,128)S(1)}) custom-call(bf16[64,512]{1,0:T(8,128)(2,1)S(1)} %collective-permute-done.3.points, bf16[64,512]{1,0:T(8,128)(2,1)S(1)} %copy-done.2, f32[1,512]{1,0:T(1,128)S(1)} %bitcast.17, bf16[512,512]{1,0:T(8,128)(2,1)S(1)} %copy-done, f32[1,512]{1,0:T(1,128)S(1)} %bitcast.22, ...), custom_call_target="tpu_custom_call" | custom-call | flops 436207616 | bytes 1048576 | tf_op jit(solution)/shard_map/pallas_call | solution.py:73
  14.9 0.0 collective-permute-done.7
  14.9 0.0 copy-start.3
  14.9 0.0 collective-permute-done.4.points
  14.9 1.5 %shard_map.125 = (bf16[256,1024]{1,0:T(8,128)(2,1)S(1)}, f32[1,1024]{1,0:T(1,128)S(1)}) custom-call(bf16[64,1024]{1,0:T(8,128)(2,1)S(1)} %collective-permute-done.4.points, bf16[64,512]{1,0:T(8,128)(2,1)S(1)} %copy-done.2, f32[1,512]{1,0:T(1,128)S(1)} %bitcast.18, bf16[512,512]{1,0:T(8,128)(2,1)S(1)} %copy-done, f32[1,512]{1,0:T(1,128)S(1)} %bitcast.23, ...), custom_call_target="tpu_custom_call" | custom-call | flops 872415232 | bytes 1048576 | tf_op jit(solution)/shard_map/pallas_call | solution.py:73
  16.5 0.0 collective-permute-done.2.rows.rest_15_
  16.5 0.0 copy-done.3
  16.5 1.6 %shard_map.126 = (f32[128,128]{1,0:T(8,128)S(1)}, bf16[256,512]{1,0:T(8,128)(2,1)S(1)}, bf16[256,512]{1,0:T(8,128)(2,1)S(1)}, bf16[256,1024]{1,0:T(8,128)(2,1)S(1)}) custom-call(bf16[256,128]{1,0:T(8,128)(2,1)S(1)} %collective-permute-done.2.rows.rest_15_, bf16[256,512]{1,0:T(8,128)(2,1)S(1)} %get-tuple-element.41.rest_0_, ...), custom_call_target="tpu_custom_call" | custom-call | flops 754974720 | bytes 1048576 | tf_op jit(solution)/shard_map/pallas_call | solution.py:73
  18.1 1.2 %collective-permute-start.8 = (f32[128,128]{1,0:T(8,128)S(1)}, f32[128,128]{1,0:T(8,128)S(1)}, u32[]{:S(2)}, u32[]{:S(2)}) collective-permute-start(f32[128,128]{1,0:T(8,128)S(1)} %get-tuple-element.52), channel_id=1, source_target_pairs={{0,16},{1,17},{2,18},{3,19},{4,20},{5,21},{6,22},{7,23},{8,24},{9,... | collective-permute-start | bytes 196616 | tf_op jit(solution)/shard_map/ppermute | solution.py:117
  19.2 1.9 %shard_map.127 = (f32[128,128]{1,0:T(8,128)S(1)}, f32[64,512]{1,0:T(8,128)S(1)}, f32[64,512]{1,0:T(8,128)S(1)}, f32[64,1024]{1,0:T(8,128)S(1)}) custom-call(bf16[256,128]{1,0:T(8,128)(2,1)S(1)} %pad_maximum_fusion.1.rows, bf16[256,512]{1,0:T(8,128)(2,1)S(1)} %get-tuple-element.41.rest_0_, f32[1,512]{1,0:T(1,128)S(1)} %get-tuple-element.42.rest_1_, ...), custom_call_target="tpu_custom_call" | custom-call | flops 754974720 | bytes 1048576 | tf_op jit(solution)/shard_map/pallas_call | solution.py:73
  21.1 1.3 %collective-permute-done.8 = f32[128,128]{1,0:T(8,128)S(1)} collective-permute-done((f32[128,128]{1,0:T(8,128)S(1)}, f32[128,128]{1,0:T(8,128)S(1)}, u32[]{:S(2)}, u32[]{:S(2)}) %collective-permute-start.8) | collective-permute-done | bytes 65568 | tf_op jit(solution)/shard_map/ppermute | solution.py:117
  22.4 0.0 collective-permute-start.11
  22.4 1.6 %collective-permute-start.9 = (f32[64,128]{1,0:T(8,128)S(1)}, f32[64,128]{1,0:T(8,128)S(1)}, u32[]{:S(2)}, u32[]{:S(2)}) collective-permute-start(f32[64,128]{1,0:T(8,128)S(1)} %split.9), channel_id=1, source_target_pairs={{0,1},{1,0},{2,3},{3,2},{4,5},{5,4},{6,7},{7,6},{8,9},{9,8},{10,11... | collective-permute-start | bytes 98312 | tf_op jit(solution)/shard_map/ppermute | solution.py:117
  24.1 0.0 collective-permute-done.11
  24.1 1.5 %collective-permute-start.12 = (f32[64,512]{1,0:T(8,128)S(1)}, f32[64,512]{1,0:T(8,128)S(1)}, u32[]{:S(2)}, u32[]{:S(2)}) collective-permute-start(f32[64,512]{1,0:T(8,128)S(1)} %get-tuple-element.62), channel_id=1, source_target_pairs={{0,8},{1,9},{2,10},{3,11},{4,12},{5,13},{6,14},{7,15},{8,0},{9,1},... | collective-permute-start | bytes 393224 | tf_op jit(solution)/shard_map/ppermute | solution.py:117
  25.6 0.8 %collective-permute-done.9 = f32[64,128]{1,0:T(8,128)S(1)} collective-permute-done((f32[64,128]{1,0:T(8,128)S(1)}, f32[64,128]{1,0:T(8,128)S(1)}, u32[]{:S(2)}, u32[]{:S(2)}) %collective-permute-start.9) | collective-permute-done | bytes 32800 | tf_op jit(solution)/shard_map/ppermute | solution.py:117
  26.4 2.5 %collective-permute-start.10 = (f32[32,128]{1,0:T(8,128)S(1)}, f32[32,128]{1,0:T(8,128)S(1)}, u32[]{:S(2)}, u32[]{:S(2)}) collective-permute-start(f32[32,128]{1,0:T(8,128)S(1)} %slice.12), channel_id=1, source_target_pairs={{0,2},{1,3},{2,0},{3,1},{4,6},{5,7},{6,4},{7,5},{8,10},{9,11},{10,... | collective-permute-start | bytes 49160 | tf_op jit(solution)/shard_map/ppermute | solution.py:117
  29.6 0.2 collective-permute-done.12.got
  29.8 0.7 %shard_map.128 = f32[64,512]{1,0:T(8,128)} custom-call(f32[1,1]{1,0:T(1,128)} %bitcast.7.scale, f32[64,512]{1,0:T(8,128)S(1)} %get-tuple-element.63.own, f32[64,512]{1,0:T(8,128)S(1)} %collective-permute-done.12.got), custom_call_target="tpu_custom_call" | custom-call | flops 1000000 | bytes 1048576 | tf_op jit(solution)/shard_map/pallas_call | solution.py:73
  30.5 0.6 %collective-permute-done.10.got = f32[32,128]{1,0:T(8,128)S(1)} collective-permute-done((f32[32,128]{1,0:T(8,128)S(1)}, f32[32,128]{1,0:T(8,128)S(1)}, u32[]{:S(2)}, u32[]{:S(2)}) %collective-permute-start.10) | collective-permute-done | bytes 16416 | tf_op jit(solution)/shard_map/ppermute | solution.py:117
  31.1 0.8 %shard_map.129 = f32[64,64]{1,0:T(8,128)} custom-call(f32[1,1]{1,0:T(1,128)} %bitcast.8.scale, f32[64,128]{1,0:T(8,128)S(1)} %slice_add_fusion.2.own, f32[32,128]{1,0:T(8,128)S(1)} %collective-permute-done.10.got), custom_call_target="tpu_custom_call" | custom-call | flops 1000000 | bytes 1048576 | tf_op jit(solution)/shard_map/pallas_call | solution.py:73
  (17 shorter events, 0.1 us)
Async XLA Ops:
  1.4 6.2 %collective-permute-start = (bf16[64,128]{1,0:T(8,128)(2,1)S(1)}, bf16[64,128]{1,0:T(8,128)(2,1)S(1)}, u32[]{:S(2)}, u32[]{:S(2)}) collective-permute-start(bf16[64,128]{1,0:T(8,128)(2,1)S(1)} %pad_maximum_fusion.3), channel_id=1, source_target_pairs={{0,2},{1,3},{2,0},{3,1},{4,6},{5,7},{6,4},{7,5},{8,10},{9,11},{10,... | collective-permute-start | bytes 49160 | tf_op jit(solution)/shard_map/ppermute | solution.py:117
  5.5 7.9 %collective-permute-start.5 = (bf16[64,512]{1,0:T(8,128)(2,1)}, bf16[64,512]{1,0:T(8,128)(2,1)S(1)}, u32[]{:S(2)}, u32[]{:S(2)}) collective-permute-start(bf16[64,512]{1,0:T(8,128)(2,1)} %bitcast.9), channel_id=1, source_target_pairs={{0,8},{1,9},{2,10},{3,11},{4,12},{5,13},{6,14},{7,15},{8,0},{9,1},... | collective-permute-start | bytes 196616 | tf_op jit(solution)/shard_map/ppermute | solution.py:117
  7.0 6.9 %collective-permute-start.6 = (bf16[64,512]{1,0:T(8,128)(2,1)}, bf16[64,512]{1,0:T(8,128)(2,1)S(1)}, u32[]{:S(2)}, u32[]{:S(2)}) collective-permute-start(bf16[64,512]{1,0:T(8,128)(2,1)} %bitcast.10), channel_id=1, source_target_pairs={{0,4},{1,5},{2,6},{3,7},{4,0},{5,1},{6,2},{7,3},{8,12},{9,13},{10,... | collective-permute-start | bytes 196616 | tf_op jit(solution)/shard_map/ppermute | solution.py:117
  7.0 0.7 %copy-start.8 = (bf16[64,64]{1,0:T(8,128)(2,1)S(1)}, bf16[64,64]{1,0:T(8,128)(2,1)}, u32[]{:S(2)}) copy-start(bf16[64,64]{1,0:T(8,128)(2,1)} %param.13) | copy-start | bytes 24580
  7.0 0.7 %copy-start.9 = (bf16[64,64]{1,0:T(8,128)(2,1)S(1)}, bf16[64,64]{1,0:T(8,128)(2,1)}, u32[]{:S(2)}) copy-start(bf16[64,64]{1,0:T(8,128)(2,1)} %param.11) | copy-start | bytes 24580
  7.0 2.4 %copy-start = (bf16[512,512]{1,0:T(8,128)(2,1)S(1)}, bf16[512,512]{1,0:T(8,128)(2,1)}, u32[]{:S(2)}) copy-start(bf16[512,512]{1,0:T(8,128)(2,1)} %rest_11_.3) | copy-start | bytes 1572868
  7.0 2.4 %copy-start.1 = (bf16[512,256]{1,0:T(8,128)(2,1)S(1)}, bf16[512,256]{1,0:T(8,128)(2,1)}, u32[]{:S(2)}) copy-start(bf16[512,256]{1,0:T(8,128)(2,1)} %rest_13_.3) | copy-start | bytes 786436
  7.0 6.3 %collective-permute-start.3 = (bf16[64,512]{1,0:T(8,128)(2,1)}, bf16[64,512]{1,0:T(8,128)(2,1)S(1)}, u32[]{:S(2)}, u32[]{:S(2)}) collective-permute-start(bf16[64,512]{1,0:T(8,128)(2,1)} %bitcast.13), channel_id=1, source_target_pairs={{0,8},{1,9},{2,10},{3,11},{4,12},{5,13},{6,14},{7,15},{8,0},{9,1},... | collective-permute-start | bytes 196616 | tf_op jit(solution)/shard_map/ppermute | solution.py:117
  7.6 1.8 %copy-start.4 = (bf16[512,64]{0,1:T(8,128)(2,1)S(1)}, bf16[512,64]{0,1:T(8,128)(2,1)}, u32[]{:S(2)}) copy-start(bf16[512,64]{0,1:T(8,128)(2,1)} %param.12) | copy-start | bytes 196612
  7.6 1.8 %copy-start.6 = (f32[512]{0:T(512)S(1)}, f32[512]{0:T(512)}, u32[]{:S(2)}) copy-start(f32[512]{0:T(512)} %param.18) | copy-start | bytes 6148
  7.7 1.7 %copy-start.2 = (bf16[64,512]{1,0:T(8,128)(2,1)S(1)}, bf16[64,512]{1,0:T(8,128)(2,1)}, u32[]{:S(2)}) copy-start(bf16[64,512]{1,0:T(8,128)(2,1)} %rest_9_.3) | copy-start | bytes 196612
  7.8 3.9 %collective-permute-start.1 = (bf16[128,128]{1,0:T(8,128)(2,1)S(1)}, bf16[128,128]{1,0:T(8,128)(2,1)S(1)}, u32[]{:S(2)}, u32[]{:S(2)}) collective-permute-start(bf16[128,128]{1,0:T(8,128)(2,1)S(1)} %pad_maximum_fusion.2), channel_id=1, source_target_pairs={{0,1},{1,0},{2,3},{3,2},{4,5},{5,4},{6,7},{7,6},{8,9},{9,8},{10,11... | collective-permute-start | bytes 98312 | tf_op jit(solution)/shard_map/ppermute | solution.py:117
  9.4 0.7 %copy-start.5 = (f32[512]{0:T(512)S(1)}, f32[512]{0:T(512)}, u32[]{:S(2)}) copy-start(f32[512]{0:T(512)} %param.16) | copy-start | bytes 6148
  9.4 0.7 %copy-start.7 = (f32[256]{0:T(256)S(1)}, f32[256]{0:T(256)}, u32[]{:S(2)}) copy-start(f32[256]{0:T(256)} %param.20) | copy-start | bytes 3076
  11.8 4.6 %collective-permute-start.2 = (bf16[256,128]{1,0:T(8,128)(2,1)S(1)}, bf16[256,128]{1,0:T(8,128)(2,1)S(1)}, u32[]{:S(2)}, u32[]{:S(2)}) collective-permute-start(bf16[256,128]{1,0:T(8,128)(2,1)S(1)} %pad_maximum_fusion.1.rows), channel_id=1, source_target_pairs={{0,16},{1,17},{2,18},{3,19},{4,20},{5,21},{6,22},{7,23},{8,24},{9,... | collective-permute-start | bytes 196616 | tf_op jit(solution)/shard_map/ppermute | solution.py:117
  13.4 1.6 %collective-permute-start.4 = (bf16[64,1024]{1,0:T(8,128)(2,1)S(1)}, bf16[64,1024]{1,0:T(8,128)(2,1)S(1)}, u32[]{:S(2)}, u32[]{:S(2)}) collective-permute-start(bf16[64,1024]{1,0:T(8,128)(2,1)S(1)} %pad_maximum_fusion), channel_id=1, source_target_pairs={{0,4},{1,5},{2,6},{3,7},{4,0},{5,1},{6,2},{7,3},{8,12},{9,13},{10,... | collective-permute-start | bytes 393224 | tf_op jit(solution)/shard_map/ppermute | solution.py:117
  13.4 1.5 %collective-permute-start.7 = (bf16[64,512]{1,0:T(8,128)(2,1)S(1)}, bf16[64,512]{1,0:T(8,128)(2,1)S(1)}, u32[]{:S(2)}, u32[]{:S(2)}) collective-permute-start(bf16[64,512]{1,0:T(8,128)(2,1)S(1)} %collective-permute-done.5.rest_5_), channel_id=1, source_target_pairs={{0,4},{1,5},{2,6},{3,7},{4,0},{5,1},{6,2},{7,3},{8,12},{9,13},{10,... | collective-permute-start | bytes 196616 | tf_op jit(solution)/shard_map/ppermute | solution.py:117
  14.9 1.5 %copy-start.3 = (bf16[512,64]{0,1:T(8,128)(2,1)S(1)}, bf16[512,64]{0,1:T(8,128)(2,1)}, u32[]{:S(2)}) copy-start(bf16[512,64]{0,1:T(8,128)(2,1)} %param.14) | copy-start | bytes 196612
  18.1 4.3 %collective-permute-start.8 = (f32[128,128]{1,0:T(8,128)S(1)}, f32[128,128]{1,0:T(8,128)S(1)}, u32[]{:S(2)}, u32[]{:S(2)}) collective-permute-start(f32[128,128]{1,0:T(8,128)S(1)} %get-tuple-element.52), channel_id=1, source_target_pairs={{0,16},{1,17},{2,18},{3,19},{4,20},{5,21},{6,22},{7,23},{8,24},{9,... | collective-permute-start | bytes 196616 | tf_op jit(solution)/shard_map/ppermute | solution.py:117
  22.4 1.7 %collective-permute-start.11 = (f32[64,1024]{1,0:T(8,128)S(1)}, f32[64,1024]{1,0:T(8,128)S(1)}, u32[]{:S(2)}, u32[]{:S(2)}) collective-permute-start(f32[64,1024]{1,0:T(8,128)S(1)} %get-tuple-element.58), channel_id=1, source_target_pairs={{0,4},{1,5},{2,6},{3,7},{4,0},{5,1},{6,2},{7,3},{8,12},{9,13},{10,... | collective-permute-start | bytes 786440 | tf_op jit(solution)/shard_map/ppermute | solution.py:117
  22.4 4.0 %collective-permute-start.9 = (f32[64,128]{1,0:T(8,128)S(1)}, f32[64,128]{1,0:T(8,128)S(1)}, u32[]{:S(2)}, u32[]{:S(2)}) collective-permute-start(f32[64,128]{1,0:T(8,128)S(1)} %split.9), channel_id=1, source_target_pairs={{0,1},{1,0},{2,3},{3,2},{4,5},{5,4},{6,7},{7,6},{8,9},{9,8},{10,11... | collective-permute-start | bytes 98312 | tf_op jit(solution)/shard_map/ppermute | solution.py:117
  24.1 5.7 %collective-permute-start.12 = (f32[64,512]{1,0:T(8,128)S(1)}, f32[64,512]{1,0:T(8,128)S(1)}, u32[]{:S(2)}, u32[]{:S(2)}) collective-permute-start(f32[64,512]{1,0:T(8,128)S(1)} %get-tuple-element.62), channel_id=1, source_target_pairs={{0,8},{1,9},{2,10},{3,11},{4,12},{5,13},{6,14},{7,15},{8,0},{9,1},... | collective-permute-start | bytes 393224 | tf_op jit(solution)/shard_map/ppermute | solution.py:117
  26.4 4.7 %collective-permute-start.10 = (f32[32,128]{1,0:T(8,128)S(1)}, f32[32,128]{1,0:T(8,128)S(1)}, u32[]{:S(2)}, u32[]{:S(2)}) collective-permute-start(f32[32,128]{1,0:T(8,128)S(1)} %slice.12), channel_id=1, source_target_pairs={{0,2},{1,3},{2,0},{3,1},{4,6},{5,7},{6,4},{7,5},{8,10},{9,11},{10,... | collective-permute-start | bytes 49160 | tf_op jit(solution)/shard_map/ppermute | solution.py:117

commit v5 on v4

--- a/solution.py
+++ b/solution.py
@@ -1,4 +1,5 @@
 import functools
+import math
 
 import jax
 import jax.numpy as jnp
@@ -10,6 +11,7 @@
 AXES = ("row", "col")
 F32, BF16 = jnp.float32, jnp.bfloat16
 HOLD_FLOPS = 2 * 10**10
+CUT_MOST = 0.375 * 1.0625
 FINISH_FLOPS = 10**6
 
 
@@ -169,21 +171,34 @@
     args = (rows, *columns, *weights, far_rows, *far_panels)
     row_near, *col_sums = call(panel, [sums, *col_sums], args, flops)
 
-    got, col_sums = lax.optimization_barrier((swap(row_far, row_masks[-1]), col_sums))
+    top = math.ceil(math.log2(CUT_MOST * col_vectors.shape[0] * devices))
+    gain = 2.0 ** (math.floor(math.log2(float(jnp.finfo(jnp.float16).max))) - top)
+
+    def swap_sums(block, mask):
+        return swap((block * gain).astype(jnp.float16), mask)
+
+    def widen(block):
+        return block.astype(F32) * (1.0 / gain)
+
+    got, col_sums = lax.optimization_barrier((swap_sums(row_far, row_masks[-1]), col_sums))
+    got = widen(got)
     row_sum = row_near + got
     for number, mask in reversed(list(enumerate(col_masks))[1:]):
         got, start = swap(col_sums[number + 1], mask), 0
         for side in range(number + 1):
             col_sums[side] = col_sums[side] + got[:, start : start + sides[side]]
             start += sides[side]
-    got = swap(col_sums[1], col_masks[0])
-    (col_result,) = call(
-        finish_kernel, [jax.ShapeDtypeStruct(got.shape, F32)], (scale, col_sums[0], got), FINISH_FLOPS
-    )
+    got_cols = swap(col_sums[1], col_masks[0])
+    own_cols = col_sums[0]
     for mask in reversed(row_masks[1:-1]):
         keep, give = jnp.split(row_sum, 2, axis=0)
-        row_sum = keep + swap(give, mask)
-    got, col_result = lax.optimization_barrier((swap(row_sum[block // 2 :], row_masks[0]), col_result))
+        got, own_cols = lax.optimization_barrier((swap_sums(give, mask), own_cols))
+        row_sum = keep + widen(got)
+    (col_result,) = call(
+        finish_kernel, [jax.ShapeDtypeStruct(got_cols.shape, F32)], (scale, own_cols, got_cols), FINISH_FLOPS
+    )
+    got, col_result = lax.optimization_barrier((swap_sums(row_sum[block // 2 :], row_masks[0]), col_result))
+    got = widen(got)
     (row_result,) = call(
         finish_rows_kernel, [jax.ShapeDtypeStruct((block, nvec), F32)], (scale, row_sum, got), FINISH_FLOPS
     )

time: 32.3 us -> 31.7 us (0.981)
  waiting for transfers between devices: 3.61 us -> 3 us
    ppermute x13, waiting for transfers between devices: 3.61 us -> 3 us  [swap(): return lax.ppermute(block, AXES, [(i, i ^ mask) for i in range(devices)])]
where the time goes in v5:
time: 31.7 us; the launch traced here: 31.3 us
  starting transfers between devices  16.6 us (52%)
  Pallas kernels  8.34 us (26%)
  waiting for transfers between devices  3 us (9%)
  between operations  1.45 us (5%)
  other arithmetic  1.08 us (3%)
  local copies, waits for them, and re-layouts  0.8 us (3%)
    ppermute x13, starting transfers between devices, swap(): return lax.ppermute(block, AXES, [(i, i ^ mask) for i in range(devices)])  16.6 us
    pallas_call x8, Pallas kernels, call(): pl.pallas_call(kernel, out_shape=outs, in_specs=[pl.BlockSpec(memory_spac...  8.34 us
    ppermute x13, waiting for transfers between devices, swap(): return lax.ppermute(block, AXES, [(i, i ^ mask) for i in range(devices)])  3 us
    concatenate x1, other arithmetic, body(): rows = jnp.concatenate([row_points, row_vectors], axis=1)  0.82 us
    unnamed x21, local copies, waits for them, and re-layouts  0.79 us
  transfers between devices with their start and end apart: 13, of which 5 were waited for; matrix products, arithmetic and copies ran while one was open for 1% of the time, Pallas kernels for 19%

profile of v5, /device:TPU:0, one launch (start us, length us, event | category | flops | bytes accessed | tf_op | source)
XLA Modules:
  0.0 31.3 jit_solution(6048408565119460712)
XLA Ops:
  0.6 0.8 %pad_maximum_fusion.3 = bf16[64,128]{1,0:T(8,128)(2,1)S(1)} fusion(bf16[64,64]{1,0:T(8,128)(2,1)} %param.13, bf16[64,64]{1,0:T(8,128)(2,1)} %param.11), kind=kLoop, calls=%fused_computation.12 | loop fusion | flops 32768 | bytes 32768 | tf_op jit(solution)/shard_map/concatenate | solution.py:145
  1.4 4.1 %collective-permute-start = (bf16[64,128]{1,0:T(8,128)(2,1)S(1)}, bf16[64,128]{1,0:T(8,128)(2,1)S(1)}, u32[]{:S(2)}, u32[]{:S(2)}) collective-permute-start(bf16[64,128]{1,0:T(8,128)(2,1)S(1)} %pad_maximum_fusion.3), channel_id=1, source_target_pairs={{0,2},{1,3},{2,0},{3,1},{4,6},{5,7},{6,4},{7,5},{8,10},{9,11},{10,... | collective-permute-start | bytes 49160 | tf_op jit(solution)/shard_map/ppermute | solution.py:119
  5.5 1.5 %collective-permute-start.5 = (bf16[64,512]{1,0:T(8,128)(2,1)}, bf16[64,512]{1,0:T(8,128)(2,1)S(1)}, u32[]{:S(2)}, u32[]{:S(2)}) collective-permute-start(bf16[64,512]{1,0:T(8,128)(2,1)} %bitcast.9), channel_id=1, source_target_pairs={{0,8},{1,9},{2,10},{3,11},{4,12},{5,13},{6,14},{7,15},{8,0},{9,1},... | collective-permute-start | bytes 196616 | tf_op jit(solution)/shard_map/ppermute | solution.py:119
  7.0 0.0 collective-permute-start.6
  7.0 0.0 copy-start.1
  7.0 0.6 %collective-permute-start.3 = (bf16[64,512]{1,0:T(8,128)(2,1)}, bf16[64,512]{1,0:T(8,128)(2,1)S(1)}, u32[]{:S(2)}, u32[]{:S(2)}) collective-permute-start(bf16[64,512]{1,0:T(8,128)(2,1)} %bitcast.13), channel_id=1, source_target_pairs={{0,8},{1,9},{2,10},{3,11},{4,12},{5,13},{6,14},{7,15},{8,0},{9,1},... | collective-permute-start | bytes 196616 | tf_op jit(solution)/shard_map/ppermute | solution.py:119
  7.6 0.0 collective-permute-done.rows
  7.6 0.1 copy-done.8
  7.7 0.0 copy-done.9
  7.7 0.1 pad_maximum_fusion.2
  7.8 1.6 %collective-permute-start.1 = (bf16[128,128]{1,0:T(8,128)(2,1)S(1)}, bf16[128,128]{1,0:T(8,128)(2,1)S(1)}, u32[]{:S(2)}, u32[]{:S(2)}) collective-permute-start(bf16[128,128]{1,0:T(8,128)(2,1)S(1)} %pad_maximum_fusion.2), channel_id=1, source_target_pairs={{0,1},{1,0},{2,3},{3,2},{4,5},{5,4},{6,7},{7,6},{8,9},{9,8},{10,11... | collective-permute-start | bytes 98312 | tf_op jit(solution)/shard_map/ppermute | solution.py:119
  9.4 0.0 copy-done
  9.4 0.0 copy-done.1
  9.4 0.0 copy-done.4
  9.4 0.0 copy-done.6
  9.4 0.0 copy-done.2
  9.4 0.6 %copy-done.5 = f32[512]{0:T(512)S(1)} copy-done((f32[512]{0:T(512)S(1)}, f32[512]{0:T(512)}, u32[]{:S(2)}) %copy-start.5) | copy-done | bytes 2072
  10.1 0.0 copy-done.7
  10.1 0.9 %shard_map.123 = (bf16[256,512]{1,0:T(8,128)(2,1)S(1)}, f32[1,512]{1,0:T(1,128)S(1)}) custom-call(bf16[64,512]{1,0:T(8,128)(2,1)S(1)} %bitcast.14, bf16[64,512]{1,0:T(8,128)(2,1)S(1)} %copy-done.2, f32[1,512]{1,0:T(1,128)S(1)} %bitcast.16, bf16[512,512]{1,0:T(8,128)(2,1)S(1)} %copy-done, f32[1,512]{1,0:T(1,128)S(1)} %bitcast.21, ...), custom_call_target="tpu_custom_call" | custom-call | flops 436207616 | bytes 1048576 | tf_op jit(solution)/shard_map/pallas_call | solution.py:75
  11.0 0.7 %collective-permute-done.1 = bf16[128,128]{1,0:T(8,128)(2,1)S(1)} collective-permute-done((bf16[128,128]{1,0:T(8,128)(2,1)S(1)}, bf16[128,128]{1,0:T(8,128)(2,1)S(1)}, u32[]{:S(2)}, u32[]{:S(2)}) %collective-permute-start.1) | collective-permute-done | bytes 32800 | tf_op jit(solution)/shard_map/ppermute | solution.py:119
  11.7 0.1 pad_maximum_fusion.1.rows
  11.8 1.5 %collective-permute-start.2 = (bf16[256,128]{1,0:T(8,128)(2,1)S(1)}, bf16[256,128]{1,0:T(8,128)(2,1)S(1)}, u32[]{:S(2)}, u32[]{:S(2)}) collective-permute-start(bf16[256,128]{1,0:T(8,128)(2,1)S(1)} %pad_maximum_fusion.1.rows), channel_id=1, source_target_pairs={{0,16},{1,17},{2,18},{3,19},{4,20},{5,21},{6,22},{7,23},{8,24},{9,... | collective-permute-start | bytes 196616 | tf_op jit(solution)/shard_map/ppermute | solution.py:119
  13.3 0.0 collective-permute-done.3.points
  13.4 0.1 collective-permute-start.4
  13.4 0.0 collective-permute-done.5.rest_5_
  13.4 0.5 %collective-permute-start.7 = (bf16[64,512]{1,0:T(8,128)(2,1)S(1)}, bf16[64,512]{1,0:T(8,128)(2,1)S(1)}, u32[]{:S(2)}, u32[]{:S(2)}) collective-permute-start(bf16[64,512]{1,0:T(8,128)(2,1)S(1)} %collective-permute-done.5.rest_5_), channel_id=1, source_target_pairs={{0,4},{1,5},{2,6},{3,7},{4,0},{5,1},{6,2},{7,3},{8,12},{9,13},{10,... | collective-permute-start | bytes 196616 | tf_op jit(solution)/shard_map/ppermute | solution.py:119
  13.9 0.0 collective-permute-done.6
  13.9 0.9 %shard_map.124 = (bf16[256,512]{1,0:T(8,128)(2,1)S(1)}, f32[1,512]{1,0:T(1,128)S(1)}) custom-call(bf16[64,512]{1,0:T(8,128)(2,1)S(1)} %collective-permute-done.3.points, bf16[64,512]{1,0:T(8,128)(2,1)S(1)} %copy-done.2, f32[1,512]{1,0:T(1,128)S(1)} %bitcast.17, bf16[512,512]{1,0:T(8,128)(2,1)S(1)} %copy-done, f32[1,512]{1,0:T(1,128)S(1)} %bitcast.22, ...), custom_call_target="tpu_custom_call" | custom-call | flops 436207616 | bytes 1048576 | tf_op jit(solution)/shard_map/pallas_call | solution.py:75
  14.9 0.0 collective-permute-done.7
  14.9 0.0 copy-start.3
  14.9 0.0 collective-permute-done.4.points
  14.9 1.5 %shard_map.125 = (bf16[256,1024]{1,0:T(8,128)(2,1)S(1)}, f32[1,1024]{1,0:T(1,128)S(1)}) custom-call(bf16[64,1024]{1,0:T(8,128)(2,1)S(1)} %collective-permute-done.4.points, bf16[64,512]{1,0:T(8,128)(2,1)S(1)} %copy-done.2, f32[1,512]{1,0:T(1,128)S(1)} %bitcast.18, bf16[512,512]{1,0:T(8,128)(2,1)S(1)} %copy-done, f32[1,512]{1,0:T(1,128)S(1)} %bitcast.23, ...), custom_call_target="tpu_custom_call" | custom-call | flops 872415232 | bytes 1048576 | tf_op jit(solution)/shard_map/pallas_call | solution.py:75
  16.5 0.0 collective-permute-done.2.rows.rest_15_
  16.5 0.0 copy-done.3
  16.5 1.6 %shard_map.126 = (f32[128,128]{1,0:T(8,128)S(1)}, bf16[256,512]{1,0:T(8,128)(2,1)S(1)}, bf16[256,512]{1,0:T(8,128)(2,1)S(1)}, bf16[256,1024]{1,0:T(8,128)(2,1)S(1)}) custom-call(bf16[256,128]{1,0:T(8,128)(2,1)S(1)} %collective-permute-done.2.rows.rest_15_, bf16[256,512]{1,0:T(8,128)(2,1)S(1)} %get-tuple-element.43.rest_0_, ...), custom_call_target="tpu_custom_call" | custom-call | flops 754974720 | bytes 1048576 | tf_op jit(solution)/shard_map/pallas_call | solution.py:75
  18.1 1.2 %collective-permute-start.8 = (f16[128,128]{1,0:T(8,128)(2,1)S(1)}, f16[128,128]{1,0:T(8,128)(2,1)S(1)}, u32[]{:S(2)}, u32[]{:S(2)}) collective-permute-start(f16[128,128]{1,0:T(8,128)(2,1)S(1)} %multiply_convert_fusion), channel_id=1, source_target_pairs={{0,16},{1,17},{2,18},{3,19},{4,20},{5,21},{6,22},{7,23},{8,24},{9,... | collective-permute-start | bytes 98312 | tf_op jit(solution)/shard_map/ppermute | solution.py:119
  19.3 1.9 %shard_map.127 = (f32[128,128]{1,0:T(8,128)S(1)}, f32[64,512]{1,0:T(8,128)S(1)}, f32[64,512]{1,0:T(8,128)S(1)}, f32[64,1024]{1,0:T(8,128)S(1)}) custom-call(bf16[256,128]{1,0:T(8,128)(2,1)S(1)} %pad_maximum_fusion.1.rows, bf16[256,512]{1,0:T(8,128)(2,1)S(1)} %get-tuple-element.43.rest_0_, f32[1,512]{1,0:T(1,128)S(1)} %get-tuple-element.44.rest_1_, ...), custom_call_target="tpu_custom_call" | custom-call | flops 754974720 | bytes 1048576 | tf_op jit(solution)/shard_map/pallas_call | solution.py:75
  21.1 0.9 %collective-permute-done.8 = f16[128,128]{1,0:T(8,128)(2,1)S(1)} collective-permute-done((f16[128,128]{1,0:T(8,128)(2,1)S(1)}, f16[128,128]{1,0:T(8,128)(2,1)S(1)}, u32[]{:S(2)}, u32[]{:S(2)}) %collective-permute-start.8) | collective-permute-done | bytes 32800 | tf_op jit(solution)/shard_map/ppermute | solution.py:119
  22.1 0.0 collective-permute-start.10
  22.1 1.6 %collective-permute-start.9 = (f16[64,128]{1,0:T(8,128)(2,1)S(1)}, f16[64,128]{1,0:T(8,128)(2,1)S(1)}, u32[]{:S(2)}, u32[]{:S(2)}) collective-permute-start(f16[64,128]{1,0:T(8,128)(2,1)S(1)} %fusion), channel_id=1, source_target_pairs={{0,1},{1,0},{2,3},{3,2},{4,5},{5,4},{6,7},{7,6},{8,9},{9,8},{10,11... | collective-permute-start | bytes 49160 | tf_op jit(solution)/shard_map/ppermute | solution.py:119
  23.8 0.0 collective-permute-done.10
  23.8 1.5 %collective-permute-start.12 = (f32[64,512]{1,0:T(8,128)S(1)}, f32[64,512]{1,0:T(8,128)S(1)}, u32[]{:S(2)}, u32[]{:S(2)}) collective-permute-start(f32[64,512]{1,0:T(8,128)S(1)} %get-tuple-element.66), channel_id=1, source_target_pairs={{0,8},{1,9},{2,10},{3,11},{4,12},{5,13},{6,14},{7,15},{8,0},{9,1},... | collective-permute-start | bytes 393224 | tf_op jit(solution)/shard_map/ppermute | solution.py:119
  25.3 0.6 %collective-permute-done.9 = f16[64,128]{1,0:T(8,128)(2,1)S(1)} collective-permute-done((f16[64,128]{1,0:T(8,128)(2,1)S(1)}, f16[64,128]{1,0:T(8,128)(2,1)S(1)}, u32[]{:S(2)}, u32[]{:S(2)}) %collective-permute-start.9) | collective-permute-done | bytes 16416 | tf_op jit(solution)/shard_map/ppermute | solution.py:119
  25.9 2.5 %collective-permute-start.11 = (f16[32,128]{1,0:T(8,128)(2,1)S(1)}, f16[32,128]{1,0:T(8,128)(2,1)S(1)}, u32[]{:S(2)}, u32[]{:S(2)}) collective-permute-start(f16[32,128]{1,0:T(8,128)(2,1)S(1)} %fusion.1), channel_id=1, source_target_pairs={{0,2},{1,3},{2,0},{3,1},{4,6},{5,7},{6,4},{7,5},{8,10},{9,11},{10,... | collective-permute-start | bytes 24584 | tf_op jit(solution)/shard_map/ppermute | solution.py:119
  29.1 0.4 %collective-permute-done.12.got = f32[64,512]{1,0:T(8,128)S(1)} collective-permute-done((f32[64,512]{1,0:T(8,128)S(1)}, f32[64,512]{1,0:T(8,128)S(1)}, u32[]{:S(2)}, u32[]{:S(2)}) %collective-permute-start.12) | collective-permute-done | bytes 131104 | tf_op jit(solution)/shard_map/ppermute | solution.py:119
  29.5 0.7 %shard_map.128 = f32[64,512]{1,0:T(8,128)} custom-call(f32[1,1]{1,0:T(1,128)} %bitcast.7.scale, f32[64,512]{1,0:T(8,128)S(1)} %get-tuple-element.62.own, f32[64,512]{1,0:T(8,128)S(1)} %collective-permute-done.12.got), custom_call_target="tpu_custom_call" | custom-call | flops 1000000 | bytes 1048576 | tf_op jit(solution)/shard_map/pallas_call | solution.py:75
  30.2 0.3 %collective-permute-done.11 = f16[32,128]{1,0:T(8,128)(2,1)S(1)} collective-permute-done((f16[32,128]{1,0:T(8,128)(2,1)S(1)}, f16[32,128]{1,0:T(8,128)(2,1)S(1)}, u32[]{:S(2)}, u32[]{:S(2)}) %collective-permute-start.11) | collective-permute-done | bytes 8224 | tf_op jit(solution)/shard_map/ppermute | solution.py:119
  30.6 0.8 %shard_map.129 = f32[64,64]{1,0:T(8,128)} custom-call(f32[1,1]{1,0:T(1,128)} %bitcast.8.scale, f32[64,128]{1,0:T(8,128)S(1)} %slice_add_fusion.2.own, f32[32,128]{1,0:T(8,128)S(1)} %convert_multiply_fusion.got), custom_call_target="tpu_custom_call" | custom-call | flops 1000000 | bytes 1048576 | tf_op jit(solution)/shard_map/pallas_call | solution.py:75
  (19 shorter events, 0.1 us)
Async XLA Ops:
  1.4 6.2 %collective-permute-start = (bf16[64,128]{1,0:T(8,128)(2,1)S(1)}, bf16[64,128]{1,0:T(8,128)(2,1)S(1)}, u32[]{:S(2)}, u32[]{:S(2)}) collective-permute-start(bf16[64,128]{1,0:T(8,128)(2,1)S(1)} %pad_maximum_fusion.3), channel_id=1, source_target_pairs={{0,2},{1,3},{2,0},{3,1},{4,6},{5,7},{6,4},{7,5},{8,10},{9,11},{10,... | collective-permute-start | bytes 49160 | tf_op jit(solution)/shard_map/ppermute | solution.py:119
  5.5 7.9 %collective-permute-start.5 = (bf16[64,512]{1,0:T(8,128)(2,1)}, bf16[64,512]{1,0:T(8,128)(2,1)S(1)}, u32[]{:S(2)}, u32[]{:S(2)}) collective-permute-start(bf16[64,512]{1,0:T(8,128)(2,1)} %bitcast.9), channel_id=1, source_target_pairs={{0,8},{1,9},{2,10},{3,11},{4,12},{5,13},{6,14},{7,15},{8,0},{9,1},... | collective-permute-start | bytes 196616 | tf_op jit(solution)/shard_map/ppermute | solution.py:119
  7.0 6.9 %collective-permute-start.6 = (bf16[64,512]{1,0:T(8,128)(2,1)}, bf16[64,512]{1,0:T(8,128)(2,1)S(1)}, u32[]{:S(2)}, u32[]{:S(2)}) collective-permute-start(bf16[64,512]{1,0:T(8,128)(2,1)} %bitcast.10), channel_id=1, source_target_pairs={{0,4},{1,5},{2,6},{3,7},{4,0},{5,1},{6,2},{7,3},{8,12},{9,13},{10,... | collective-permute-start | bytes 196616 | tf_op jit(solution)/shard_map/ppermute | solution.py:119
  7.0 0.7 %copy-start.8 = (bf16[64,64]{1,0:T(8,128)(2,1)S(1)}, bf16[64,64]{1,0:T(8,128)(2,1)}, u32[]{:S(2)}) copy-start(bf16[64,64]{1,0:T(8,128)(2,1)} %param.13) | copy-start | bytes 24580
  7.0 0.7 %copy-start.9 = (bf16[64,64]{1,0:T(8,128)(2,1)S(1)}, bf16[64,64]{1,0:T(8,128)(2,1)}, u32[]{:S(2)}) copy-start(bf16[64,64]{1,0:T(8,128)(2,1)} %param.11) | copy-start | bytes 24580
  7.0 2.4 %copy-start = (bf16[512,512]{1,0:T(8,128)(2,1)S(1)}, bf16[512,512]{1,0:T(8,128)(2,1)}, u32[]{:S(2)}) copy-start(bf16[512,512]{1,0:T(8,128)(2,1)} %rest_11_.3) | copy-start | bytes 1572868
  7.0 2.4 %copy-start.1 = (bf16[512,256]{1,0:T(8,128)(2,1)S(1)}, bf16[512,256]{1,0:T(8,128)(2,1)}, u32[]{:S(2)}) copy-start(bf16[512,256]{1,0:T(8,128)(2,1)} %rest_13_.3) | copy-start | bytes 786436
  7.0 6.3 %collective-permute-start.3 = (bf16[64,512]{1,0:T(8,128)(2,1)}, bf16[64,512]{1,0:T(8,128)(2,1)S(1)}, u32[]{:S(2)}, u32[]{:S(2)}) collective-permute-start(bf16[64,512]{1,0:T(8,128)(2,1)} %bitcast.13), channel_id=1, source_target_pairs={{0,8},{1,9},{2,10},{3,11},{4,12},{5,13},{6,14},{7,15},{8,0},{9,1},... | collective-permute-start | bytes 196616 | tf_op jit(solution)/shard_map/ppermute | solution.py:119
  7.6 1.8 %copy-start.4 = (bf16[512,64]{0,1:T(8,128)(2,1)S(1)}, bf16[512,64]{0,1:T(8,128)(2,1)}, u32[]{:S(2)}) copy-start(bf16[512,64]{0,1:T(8,128)(2,1)} %param.12) | copy-start | bytes 196612
  7.6 1.8 %copy-start.6 = (f32[512]{0:T(512)S(1)}, f32[512]{0:T(512)}, u32[]{:S(2)}) copy-start(f32[512]{0:T(512)} %param.18) | copy-start | bytes 6148
  7.7 1.7 %copy-start.2 = (bf16[64,512]{1,0:T(8,128)(2,1)S(1)}, bf16[64,512]{1,0:T(8,128)(2,1)}, u32[]{:S(2)}) copy-start(bf16[64,512]{1,0:T(8,128)(2,1)} %rest_9_.3) | copy-start | bytes 196612
  7.8 3.9 %collective-permute-start.1 = (bf16[128,128]{1,0:T(8,128)(2,1)S(1)}, bf16[128,128]{1,0:T(8,128)(2,1)S(1)}, u32[]{:S(2)}, u32[]{:S(2)}) collective-permute-start(bf16[128,128]{1,0:T(8,128)(2,1)S(1)} %pad_maximum_fusion.2), channel_id=1, source_target_pairs={{0,1},{1,0},{2,3},{3,2},{4,5},{5,4},{6,7},{7,6},{8,9},{9,8},{10,11... | collective-permute-start | bytes 98312 | tf_op jit(solution)/shard_map/ppermute | solution.py:119
  9.4 0.7 %copy-start.5 = (f32[512]{0:T(512)S(1)}, f32[512]{0:T(512)}, u32[]{:S(2)}) copy-start(f32[512]{0:T(512)} %param.16) | copy-start | bytes 6148
  9.4 0.7 %copy-start.7 = (f32[256]{0:T(256)S(1)}, f32[256]{0:T(256)}, u32[]{:S(2)}) copy-start(f32[256]{0:T(256)} %param.20) | copy-start | bytes 3076
  11.8 4.6 %collective-permute-start.2 = (bf16[256,128]{1,0:T(8,128)(2,1)S(1)}, bf16[256,128]{1,0:T(8,128)(2,1)S(1)}, u32[]{:S(2)}, u32[]{:S(2)}) collective-permute-start(bf16[256,128]{1,0:T(8,128)(2,1)S(1)} %pad_maximum_fusion.1.rows), channel_id=1, source_target_pairs={{0,16},{1,17},{2,18},{3,19},{4,20},{5,21},{6,22},{7,23},{8,24},{9,... | collective-permute-start | bytes 196616 | tf_op jit(solution)/shard_map/ppermute | solution.py:119
  13.4 1.6 %collective-permute-start.4 = (bf16[64,1024]{1,0:T(8,128)(2,1)S(1)}, bf16[64,1024]{1,0:T(8,128)(2,1)S(1)}, u32[]{:S(2)}, u32[]{:S(2)}) collective-permute-start(bf16[64,1024]{1,0:T(8,128)(2,1)S(1)} %pad_maximum_fusion), channel_id=1, source_target_pairs={{0,4},{1,5},{2,6},{3,7},{4,0},{5,1},{6,2},{7,3},{8,12},{9,13},{10,... | collective-permute-start | bytes 393224 | tf_op jit(solution)/shard_map/ppermute | solution.py:119
  13.4 1.5 %collective-permute-start.7 = (bf16[64,512]{1,0:T(8,128)(2,1)S(1)}, bf16[64,512]{1,0:T(8,128)(2,1)S(1)}, u32[]{:S(2)}, u32[]{:S(2)}) collective-permute-start(bf16[64,512]{1,0:T(8,128)(2,1)S(1)} %collective-permute-done.5.rest_5_), channel_id=1, source_target_pairs={{0,4},{1,5},{2,6},{3,7},{4,0},{5,1},{6,2},{7,3},{8,12},{9,13},{10,... | collective-permute-start | bytes 196616 | tf_op jit(solution)/shard_map/ppermute | solution.py:119
  14.9 1.5 %copy-start.3 = (bf16[512,64]{0,1:T(8,128)(2,1)S(1)}, bf16[512,64]{0,1:T(8,128)(2,1)}, u32[]{:S(2)}) copy-start(bf16[512,64]{0,1:T(8,128)(2,1)} %param.14) | copy-start | bytes 196612
  18.1 4.0 %collective-permute-start.8 = (f16[128,128]{1,0:T(8,128)(2,1)S(1)}, f16[128,128]{1,0:T(8,128)(2,1)S(1)}, u32[]{:S(2)}, u32[]{:S(2)}) collective-permute-start(f16[128,128]{1,0:T(8,128)(2,1)S(1)} %multiply_convert_fusion), channel_id=1, source_target_pairs={{0,16},{1,17},{2,18},{3,19},{4,20},{5,21},{6,22},{7,23},{8,24},{9,... | collective-permute-start | bytes 98312 | tf_op jit(solution)/shard_map/ppermute | solution.py:119
  22.1 1.7 %collective-permute-start.10 = (f32[64,1024]{1,0:T(8,128)S(1)}, f32[64,1024]{1,0:T(8,128)S(1)}, u32[]{:S(2)}, u32[]{:S(2)}) collective-permute-start(f32[64,1024]{1,0:T(8,128)S(1)} %get-tuple-element.60), channel_id=1, source_target_pairs={{0,4},{1,5},{2,6},{3,7},{4,0},{5,1},{6,2},{7,3},{8,12},{9,13},{10,... | collective-permute-start | bytes 786440 | tf_op jit(solution)/shard_map/ppermute | solution.py:119
  22.1 3.8 %collective-permute-start.9 = (f16[64,128]{1,0:T(8,128)(2,1)S(1)}, f16[64,128]{1,0:T(8,128)(2,1)S(1)}, u32[]{:S(2)}, u32[]{:S(2)}) collective-permute-start(f16[64,128]{1,0:T(8,128)(2,1)S(1)} %fusion), channel_id=1, source_target_pairs={{0,1},{1,0},{2,3},{3,2},{4,5},{5,4},{6,7},{7,6},{8,9},{9,8},{10,11... | collective-permute-start | bytes 49160 | tf_op jit(solution)/shard_map/ppermute | solution.py:119
  23.8 5.7 %collective-permute-start.12 = (f32[64,512]{1,0:T(8,128)S(1)}, f32[64,512]{1,0:T(8,128)S(1)}, u32[]{:S(2)}, u32[]{:S(2)}) collective-permute-start(f32[64,512]{1,0:T(8,128)S(1)} %get-tuple-element.66), channel_id=1, source_target_pairs={{0,8},{1,9},{2,10},{3,11},{4,12},{5,13},{6,14},{7,15},{8,0},{9,1},... | collective-permute-start | bytes 393224 | tf_op jit(solution)/shard_map/ppermute | solution.py:119
  25.9 4.6 %collective-permute-start.11 = (f16[32,128]{1,0:T(8,128)(2,1)S(1)}, f16[32,128]{1,0:T(8,128)(2,1)S(1)}, u32[]{:S(2)}, u32[]{:S(2)}) collective-permute-start(f16[32,128]{1,0:T(8,128)(2,1)S(1)} %fusion.1), channel_id=1, source_target_pairs={{0,2},{1,3},{2,0},{3,1},{4,6},{5,7},{6,4},{7,5},{8,10},{9,11},{10,... | collective-permute-start | bytes 24584 | tf_op jit(solution)/shard_map/ppermute | solution.py:119

commit v6 on v5

--- a/solution.py
+++ b/solution.py
@@ -75,7 +75,7 @@
     return pl.pallas_call(
         kernel,
         out_shape=outs,
-        in_specs=[pl.BlockSpec(memory_space=pltpu.VMEM)] * len(args),
+        in_specs=[pl.BlockSpec(memory_space=pltpu.SMEM if a.shape == (1,) else pltpu.VMEM) for a in args],
         out_specs=[pl.BlockSpec(memory_space=pltpu.VMEM)] * len(outs),
         compiler_params=pltpu.CompilerParams(vmem_limit_bytes=20 * 2**20),
         cost_estimate=pl.CostEstimate(flops=flops, bytes_accessed=2**20, transcendentals=0),
@@ -87,12 +87,12 @@
 
 
 def finish_kernel(scale, own, got, result):
-    result[...] = (own[...] + got[...]) * scale[...]
+    result[...] = (own[...] + got[...]) * scale[0]
 
 
 def finish_rows_kernel(scale, own, got, result):
     tall, width = got.shape[0], result.shape[1]
-    total = (own[:tall, :] + got[...]) * scale[...]
+    total = (own[:tall, :] + got[...]) * scale[0]
     result[:tall, :] = total[:, :width]
     result[tall:, :] = total[:, width:]
 
@@ -112,8 +112,8 @@
 ):
     count_row, count_col = lax.axis_size("row"), lax.axis_size("col")
     devices = count_row * count_col
-    row_masks = [1 << b for b in reversed(range(count_col.bit_length() - 1))] + [devices // 2]
-    col_masks = [count_col << b for b in reversed(range(count_row.bit_length() - 2))]
+    row_masks = [(1 << b) | count_col for b in reversed(range(count_col.bit_length() - 1))] + [(devices // 2) | count_col]
+    col_masks = [(count_col << b) | count_col for b in reversed(range(count_row.bit_length() - 2))]
 
     def swap(block, mask):
         return lax.ppermute(block, AXES, [(i, i ^ mask) for i in range(devices)])
@@ -125,7 +125,6 @@
         bias_mid.reshape(1, -1),
         weight_out,
         ard_scales.reshape(1, -1),
-        signal_scale.reshape(1, 1),
     )
     block, nvec = row_vectors.shape
     emb = weight_out.shape[1]
@@ -141,8 +140,7 @@
             2 * count * layers,
         )
 
-    *weights, scale = weights
-    rows = jnp.concatenate([row_points, row_vectors], axis=1)
+    rows = lax.optimization_barrier(jnp.concatenate([row_points, row_vectors], axis=1))
     (got,) = call(hold_kernel, [jax.ShapeDtypeStruct(rows.shape, BF16)], (swap(rows, row_masks[0]),), HOLD_FLOPS)
     rows = jnp.concatenate([rows, got], axis=0)
     for mask in row_masks[1:-2]:
@@ -195,12 +193,12 @@
         got, own_cols = lax.optimization_barrier((swap_sums(give, mask), own_cols))
         row_sum = keep + widen(got)
     (col_result,) = call(
-        finish_kernel, [jax.ShapeDtypeStruct(got_cols.shape, F32)], (scale, own_cols, got_cols), FINISH_FLOPS
+        finish_kernel, [jax.ShapeDtypeStruct(got_cols.shape, F32)], (signal_scale, own_cols, got_cols), FINISH_FLOPS
     )
     got, col_result = lax.optimization_barrier((swap_sums(row_sum[block // 2 :], row_masks[0]), col_result))
     got = widen(got)
     (row_result,) = call(
-        finish_rows_kernel, [jax.ShapeDtypeStruct((block, nvec), F32)], (scale, row_sum, got), FINISH_FLOPS
+        finish_rows_kernel, [jax.ShapeDtypeStruct((block, nvec), F32)], (signal_scale, row_sum, got), FINISH_FLOPS
     )
     return (row_result, col_result.T)
 

time: 31.7 us -> 29.6 us (0.934)
  starting transfers between devices: 16.6 us -> 15.2 us
    ppermute x13, starting transfers between devices: 16.6 us -> 15.2 us  [swap(): return lax.ppermute(block, AXES, [(i, i ^ mask) for i in range(devices)])]
    unnamed x21 -> x17, local copies, waits for them, and re-layouts: 0.79 us -> 0.69 us
  transfers between devices with their start and end apart: 13 -> 13, of which waited for: 5 -> 5; matrix products, arithmetic and copies ran while one was open for 1% -> 0% of each run, Pallas kernels for 19% -> 20%
where the time goes in v6:
time: 29.6 us; the launch traced here: 29.3 us
  starting transfers between devices  15.2 us (51%)
  Pallas kernels  8.2 us (28%)
  waiting for transfers between devices  2.82 us (10%)
  between operations  1.42 us (5%)
  other arithmetic  0.93 us (3%)
  local copies, waits for them, and re-layouts  0.69 us (2%)
    ppermute x13, starting transfers between devices, swap(): return lax.ppermute(block, AXES, [(i, i ^ mask) for i in range(devices)])  15.2 us
    pallas_call x8, Pallas kernels, call(): pl.pallas_call(kernel, out_shape=outs, in_specs=[pl.BlockSpec(memory_spac...  8.2 us
    ppermute x13, waiting for transfers between devices, swap(): return lax.ppermute(block, AXES, [(i, i ^ mask) for i in range(devices)])  2.82 us
    concatenate x1, other arithmetic, body(): jnp.concatenate([row_points, row_vectors], axis=1)  0.82 us
    unnamed x17, local copies, waits for them, and re-layouts  0.69 us
  transfers between devices with their start and end apart: 13, of which 5 were waited for; matrix products, arithmetic and copies ran while one was open for 0% of the time, Pallas kernels for 20%

profile of v6, /device:TPU:0, one launch (start us, length us, event | category | flops | bytes accessed | tf_op | source)
XLA Modules:
  0.0 29.3 jit_solution(199492246418159180)
XLA Ops:
  0.6 0.8 %pad_maximum_fusion.3 = bf16[64,128]{1,0:T(8,128)(2,1)S(1)} fusion(bf16[64,64]{1,0:T(8,128)(2,1)} %param.13, bf16[64,64]{1,0:T(8,128)(2,1)} %param.11), kind=kLoop, calls=%fused_computation.12 | loop fusion | flops 32768 | bytes 32768 | tf_op jit(solution)/shard_map/concatenate | solution.py:143
  1.4 3.5 %collective-permute-start = (bf16[64,128]{1,0:T(8,128)(2,1)S(1)}, bf16[64,128]{1,0:T(8,128)(2,1)S(1)}, u32[]{:S(2)}, u32[]{:S(2)}) collective-permute-start(bf16[64,128]{1,0:T(8,128)(2,1)S(1)} %pad_maximum_fusion.3), channel_id=1, source_target_pairs={{0,6},{1,7},{2,4},{3,5},{4,2},{5,3},{6,0},{7,1},{8,14},{9,15},{10,... | collective-permute-start | bytes 49160 | tf_op jit(solution)/shard_map/ppermute | solution.py:119
  4.9 1.8 %collective-permute-start.5 = (bf16[64,512]{1,0:T(8,128)(2,1)}, bf16[64,512]{1,0:T(8,128)(2,1)S(1)}, u32[]{:S(2)}, u32[]{:S(2)}) collective-permute-start(bf16[64,512]{1,0:T(8,128)(2,1)} %bitcast.6), channel_id=1, source_target_pairs={{0,12},{1,13},{2,14},{3,15},{4,8},{5,9},{6,10},{7,11},{8,4},{9,5},... | collective-permute-start | bytes 196616 | tf_op jit(solution)/shard_map/ppermute | solution.py:119
  6.7 0.0 collective-permute-start.6
  6.7 0.0 copy-start
  6.7 0.0 copy-start.1
  6.7 0.6 %collective-permute-start.3 = (bf16[64,512]{1,0:T(8,128)(2,1)}, bf16[64,512]{1,0:T(8,128)(2,1)S(1)}, u32[]{:S(2)}, u32[]{:S(2)}) collective-permute-start(bf16[64,512]{1,0:T(8,128)(2,1)} %bitcast.10), channel_id=1, source_target_pairs={{0,12},{1,13},{2,14},{3,15},{4,8},{5,9},{6,10},{7,11},{8,4},{9,5},... | collective-permute-start | bytes 196616 | tf_op jit(solution)/shard_map/ppermute | solution.py:119
  7.4 0.0 collective-permute-done.rows
  7.4 0.0 copy-start.4
  7.4 0.0 copy-start.6
  7.4 0.0 copy-start.2
  7.4 1.2 %collective-permute-start.1 = (bf16[128,128]{1,0:T(8,128)(2,1)S(1)}, bf16[128,128]{1,0:T(8,128)(2,1)S(1)}, u32[]{:S(2)}, u32[]{:S(2)}) collective-permute-start(bf16[128,128]{1,0:T(8,128)(2,1)S(1)} %pad_maximum_fusion.2), channel_id=1, source_target_pairs={{0,5},{1,4},{2,7},{3,6},{4,1},{5,0},{6,3},{7,2},{8,13},{9,12},{10,... | collective-permute-start | bytes 98312 | tf_op jit(solution)/shard_map/ppermute | solution.py:119
  8.7 0.0 copy-start.5
  8.7 0.0 copy-done
  8.7 0.0 copy-done.1
  8.7 0.0 copy-done.4
  8.7 0.0 copy-done.6
  8.7 0.0 copy-done.2
  8.7 0.6 %copy-done.5 = f32[512]{0:T(512)S(1)} copy-done((f32[512]{0:T(512)S(1)}, f32[512]{0:T(512)}, u32[]{:S(2)}) %copy-start.5) | copy-done | bytes 2072
  9.3 0.0 copy-done.7
  9.3 0.9 %shard_map.123 = (bf16[256,512]{1,0:T(8,128)(2,1)S(1)}, f32[1,512]{1,0:T(1,128)S(1)}) custom-call(bf16[64,512]{1,0:T(8,128)(2,1)S(1)} %bitcast.11, bf16[64,512]{1,0:T(8,128)(2,1)S(1)} %copy-done.2, f32[1,512]{1,0:T(1,128)S(1)} %bitcast.13, bf16[512,512]{1,0:T(8,128)(2,1)S(1)} %copy-done, f32[1,512]{1,0:T(1,128)S(1)} %bitcast.18, ...), custom_call_target="tpu_custom_call" | custom-call | flops 436207616 | bytes 1048576 | tf_op jit(solution)/shard_map/pallas_call | solution.py:75
  10.3 0.7 %collective-permute-done.1 = bf16[128,128]{1,0:T(8,128)(2,1)S(1)} collective-permute-done((bf16[128,128]{1,0:T(8,128)(2,1)S(1)}, bf16[128,128]{1,0:T(8,128)(2,1)S(1)}, u32[]{:S(2)}, u32[]{:S(2)}) %collective-permute-start.1) | collective-permute-done | bytes 32800 | tf_op jit(solution)/shard_map/ppermute | solution.py:119
  11.0 1.2 %collective-permute-start.2 = (bf16[256,128]{1,0:T(8,128)(2,1)S(1)}, bf16[256,128]{1,0:T(8,128)(2,1)S(1)}, u32[]{:S(2)}, u32[]{:S(2)}) collective-permute-start(bf16[256,128]{1,0:T(8,128)(2,1)S(1)} %pad_maximum_fusion.1.rows), channel_id=1, source_target_pairs={{0,20},{1,21},{2,22},{3,23},{4,16},{5,17},{6,18},{7,19},{8,28},{9,... | collective-permute-start | bytes 196616 | tf_op jit(solution)/shard_map/ppermute | solution.py:119
  12.2 0.0 collective-permute-done.3.points
  12.2 0.5 %collective-permute-start.4 = (bf16[64,1024]{1,0:T(8,128)(2,1)S(1)}, bf16[64,1024]{1,0:T(8,128)(2,1)S(1)}, u32[]{:S(2)}, u32[]{:S(2)}) collective-permute-start(bf16[64,1024]{1,0:T(8,128)(2,1)S(1)} %pad_maximum_fusion), channel_id=1, source_target_pairs={{0,4},{1,5},{2,6},{3,7},{4,0},{5,1},{6,2},{7,3},{8,12},{9,13},{10,... | collective-permute-start | bytes 393224 | tf_op jit(solution)/shard_map/ppermute | solution.py:119
  12.7 0.0 collective-permute-done.5.rest_5_
  12.7 0.1 collective-permute-start.7
  12.8 0.0 collective-permute-done.6
  12.8 0.9 %shard_map.124 = (bf16[256,512]{1,0:T(8,128)(2,1)S(1)}, f32[1,512]{1,0:T(1,128)S(1)}) custom-call(bf16[64,512]{1,0:T(8,128)(2,1)S(1)} %collective-permute-done.3.points, bf16[64,512]{1,0:T(8,128)(2,1)S(1)} %copy-done.2, f32[1,512]{1,0:T(1,128)S(1)} %bitcast.14, bf16[512,512]{1,0:T(8,128)(2,1)S(1)} %copy-done, f32[1,512]{1,0:T(1,128)S(1)} %bitcast.19, ...), custom_call_target="tpu_custom_call" | custom-call | flops 436207616 | bytes 1048576 | tf_op jit(solution)/shard_map/pallas_call | solution.py:75
  13.8 0.2 collective-permute-done.7
  14.0 0.0 collective-permute-done.4.points
  14.0 1.5 %shard_map.125 = (bf16[256,1024]{1,0:T(8,128)(2,1)S(1)}, f32[1,1024]{1,0:T(1,128)S(1)}) custom-call(bf16[64,1024]{1,0:T(8,128)(2,1)S(1)} %collective-permute-done.4.points, bf16[64,512]{1,0:T(8,128)(2,1)S(1)} %copy-done.2, f32[1,512]{1,0:T(1,128)S(1)} %bitcast.15, bf16[512,512]{1,0:T(8,128)(2,1)S(1)} %copy-done, f32[1,512]{1,0:T(1,128)S(1)} %bitcast.20, ...), custom_call_target="tpu_custom_call" | custom-call | flops 872415232 | bytes 1048576 | tf_op jit(solution)/shard_map/pallas_call | solution.py:75
  15.5 0.0 collective-permute-done.2.rows.rest_15_
  15.5 0.0 copy-done.3
  15.5 1.6 %shard_map.126 = (f32[128,128]{1,0:T(8,128)S(1)}, bf16[256,512]{1,0:T(8,128)(2,1)S(1)}, bf16[256,512]{1,0:T(8,128)(2,1)S(1)}, bf16[256,1024]{1,0:T(8,128)(2,1)S(1)}) custom-call(bf16[256,128]{1,0:T(8,128)(2,1)S(1)} %collective-permute-done.2.rows.rest_15_, bf16[256,512]{1,0:T(8,128)(2,1)S(1)} %get-tuple-element.43.rest_0_, ...), custom_call_target="tpu_custom_call" | custom-call | flops 754974720 | bytes 1048576 | tf_op jit(solution)/shard_map/pallas_call | solution.py:75
  17.1 0.9 %collective-permute-start.8 = (f16[128,128]{1,0:T(8,128)(2,1)S(1)}, f16[128,128]{1,0:T(8,128)(2,1)S(1)}, u32[]{:S(2)}, u32[]{:S(2)}) collective-permute-start(f16[128,128]{1,0:T(8,128)(2,1)S(1)} %multiply_convert_fusion), channel_id=1, source_target_pairs={{0,20},{1,21},{2,22},{3,23},{4,16},{5,17},{6,18},{7,19},{8,28},{9,... | collective-permute-start | bytes 98312 | tf_op jit(solution)/shard_map/ppermute | solution.py:119
  18.0 1.9 %shard_map.127 = (f32[128,128]{1,0:T(8,128)S(1)}, f32[64,512]{1,0:T(8,128)S(1)}, f32[64,512]{1,0:T(8,128)S(1)}, f32[64,1024]{1,0:T(8,128)S(1)}) custom-call(bf16[256,128]{1,0:T(8,128)(2,1)S(1)} %pad_maximum_fusion.1.rows, bf16[256,512]{1,0:T(8,128)(2,1)S(1)} %get-tuple-element.43.rest_0_, f32[1,512]{1,0:T(1,128)S(1)} %get-tuple-element.44.rest_1_, ...), custom_call_target="tpu_custom_call" | custom-call | flops 754974720 | bytes 1048576 | tf_op jit(solution)/shard_map/pallas_call | solution.py:75
  19.8 0.7 %collective-permute-done.8 = f16[128,128]{1,0:T(8,128)(2,1)S(1)} collective-permute-done((f16[128,128]{1,0:T(8,128)(2,1)S(1)}, f16[128,128]{1,0:T(8,128)(2,1)S(1)}, u32[]{:S(2)}, u32[]{:S(2)}) %collective-permute-start.8) | collective-permute-done | bytes 32800 | tf_op jit(solution)/shard_map/ppermute | solution.py:119
  20.5 0.2 collective-permute-start.10
  20.8 1.5 %collective-permute-start.9 = (f16[64,128]{1,0:T(8,128)(2,1)S(1)}, f16[64,128]{1,0:T(8,128)(2,1)S(1)}, u32[]{:S(2)}, u32[]{:S(2)}) collective-permute-start(f16[64,128]{1,0:T(8,128)(2,1)S(1)} %fusion), channel_id=1, source_target_pairs={{0,5},{1,4},{2,7},{3,6},{4,1},{5,0},{6,3},{7,2},{8,13},{9,12},{10,... | collective-permute-start | bytes 49160 | tf_op jit(solution)/shard_map/ppermute | solution.py:119
  22.3 0.0 collective-permute-done.10
  22.4 1.4 %collective-permute-start.12 = (f32[64,512]{1,0:T(8,128)S(1)}, f32[64,512]{1,0:T(8,128)S(1)}, u32[]{:S(2)}, u32[]{:S(2)}) collective-permute-start(f32[64,512]{1,0:T(8,128)S(1)} %get-tuple-element.66), channel_id=1, source_target_pairs={{0,12},{1,13},{2,14},{3,15},{4,8},{5,9},{6,10},{7,11},{8,4},{9,5},... | collective-permute-start | bytes 393224 | tf_op jit(solution)/shard_map/ppermute | solution.py:119
  23.8 0.3 collective-permute-done.9
  24.1 2.2 %collective-permute-start.11 = (f16[32,128]{1,0:T(8,128)(2,1)S(1)}, f16[32,128]{1,0:T(8,128)(2,1)S(1)}, u32[]{:S(2)}, u32[]{:S(2)}) collective-permute-start(f16[32,128]{1,0:T(8,128)(2,1)S(1)} %fusion.1), channel_id=1, source_target_pairs={{0,6},{1,7},{2,4},{3,5},{4,2},{5,3},{6,0},{7,1},{8,14},{9,15},{10,... | collective-permute-start | bytes 24584 | tf_op jit(solution)/shard_map/ppermute | solution.py:119
  26.9 1.0 %collective-permute-done.12.got = f32[64,512]{1,0:T(8,128)S(1)} collective-permute-done((f32[64,512]{1,0:T(8,128)S(1)}, f32[64,512]{1,0:T(8,128)S(1)}, u32[]{:S(2)}, u32[]{:S(2)}) %collective-permute-start.12) | collective-permute-done | bytes 131104 | tf_op jit(solution)/shard_map/ppermute | solution.py:119
  27.9 0.7 %shard_map.128 = f32[64,512]{1,0:T(8,128)} custom-call(f32[1]{0:T(128)S(6)} %copy.14.scale, f32[64,512]{1,0:T(8,128)S(1)} %get-tuple-element.62.own, f32[64,512]{1,0:T(8,128)S(1)} %collective-permute-done.12.got), custom_call_target="tpu_custom_call" | custom-call | flops 1000000 | bytes 1048576 | tf_op jit(solution)/shard_map/pallas_call | solution.py:75
  28.6 0.0 collective-permute-done.11
  28.6 0.7 %shard_map.129 = f32[64,64]{1,0:T(8,128)} custom-call(f32[1]{0:T(128)S(6)} %copy.14.scale, f32[64,128]{1,0:T(8,128)S(1)} %slice_add_fusion.2.own, f32[32,128]{1,0:T(8,128)S(1)} %convert_multiply_fusion.got), custom_call_target="tpu_custom_call" | custom-call | flops 1000000 | bytes 1048576 | tf_op jit(solution)/shard_map/pallas_call | solution.py:75
  (15 shorter events, 0.1 us)
Async XLA Ops:
  1.4 5.9 %collective-permute-start = (bf16[64,128]{1,0:T(8,128)(2,1)S(1)}, bf16[64,128]{1,0:T(8,128)(2,1)S(1)}, u32[]{:S(2)}, u32[]{:S(2)}) collective-permute-start(bf16[64,128]{1,0:T(8,128)(2,1)S(1)} %pad_maximum_fusion.3), channel_id=1, source_target_pairs={{0,6},{1,7},{2,4},{3,5},{4,2},{5,3},{6,0},{7,1},{8,14},{9,15},{10,... | collective-permute-start | bytes 49160 | tf_op jit(solution)/shard_map/ppermute | solution.py:119
  4.9 7.8 %collective-permute-start.5 = (bf16[64,512]{1,0:T(8,128)(2,1)}, bf16[64,512]{1,0:T(8,128)(2,1)S(1)}, u32[]{:S(2)}, u32[]{:S(2)}) collective-permute-start(bf16[64,512]{1,0:T(8,128)(2,1)} %bitcast.6), channel_id=1, source_target_pairs={{0,12},{1,13},{2,14},{3,15},{4,8},{5,9},{6,10},{7,11},{8,4},{9,5},... | collective-permute-start | bytes 196616 | tf_op jit(solution)/shard_map/ppermute | solution.py:119
  6.7 6.1 %collective-permute-start.6 = (bf16[64,512]{1,0:T(8,128)(2,1)}, bf16[64,512]{1,0:T(8,128)(2,1)S(1)}, u32[]{:S(2)}, u32[]{:S(2)}) collective-permute-start(bf16[64,512]{1,0:T(8,128)(2,1)} %bitcast.7), channel_id=1, source_target_pairs={{0,4},{1,5},{2,6},{3,7},{4,0},{5,1},{6,2},{7,3},{8,12},{9,13},{10,... | collective-permute-start | bytes 196616 | tf_op jit(solution)/shard_map/ppermute | solution.py:119
  6.7 1.9 %copy-start = (bf16[512,512]{1,0:T(8,128)(2,1)S(1)}, bf16[512,512]{1,0:T(8,128)(2,1)}, u32[]{:S(2)}) copy-start(bf16[512,512]{1,0:T(8,128)(2,1)} %rest_11_.3) | copy-start | bytes 1572868
  6.7 1.9 %copy-start.1 = (bf16[512,256]{1,0:T(8,128)(2,1)S(1)}, bf16[512,256]{1,0:T(8,128)(2,1)}, u32[]{:S(2)}) copy-start(bf16[512,256]{1,0:T(8,128)(2,1)} %rest_13_.3) | copy-start | bytes 786436
  6.7 5.5 %collective-permute-start.3 = (bf16[64,512]{1,0:T(8,128)(2,1)}, bf16[64,512]{1,0:T(8,128)(2,1)S(1)}, u32[]{:S(2)}, u32[]{:S(2)}) collective-permute-start(bf16[64,512]{1,0:T(8,128)(2,1)} %bitcast.10), channel_id=1, source_target_pairs={{0,12},{1,13},{2,14},{3,15},{4,8},{5,9},{6,10},{7,11},{8,4},{9,5},... | collective-permute-start | bytes 196616 | tf_op jit(solution)/shard_map/ppermute | solution.py:119
  7.4 1.3 %copy-start.4 = (bf16[512,64]{0,1:T(8,128)(2,1)S(1)}, bf16[512,64]{0,1:T(8,128)(2,1)}, u32[]{:S(2)}) copy-start(bf16[512,64]{0,1:T(8,128)(2,1)} %param.12) | copy-start | bytes 196612
  7.4 1.3 %copy-start.6 = (f32[512]{0:T(512)S(1)}, f32[512]{0:T(512)}, u32[]{:S(2)}) copy-start(f32[512]{0:T(512)} %param.18) | copy-start | bytes 6148
  7.4 1.3 %copy-start.2 = (bf16[64,512]{1,0:T(8,128)(2,1)S(1)}, bf16[64,512]{1,0:T(8,128)(2,1)}, u32[]{:S(2)}) copy-start(bf16[64,512]{1,0:T(8,128)(2,1)} %rest_9_.3) | copy-start | bytes 196612
  7.4 3.6 %collective-permute-start.1 = (bf16[128,128]{1,0:T(8,128)(2,1)S(1)}, bf16[128,128]{1,0:T(8,128)(2,1)S(1)}, u32[]{:S(2)}, u32[]{:S(2)}) collective-permute-start(bf16[128,128]{1,0:T(8,128)(2,1)S(1)} %pad_maximum_fusion.2), channel_id=1, source_target_pairs={{0,5},{1,4},{2,7},{3,6},{4,1},{5,0},{6,3},{7,2},{8,13},{9,12},{10,... | collective-permute-start | bytes 98312 | tf_op jit(solution)/shard_map/ppermute | solution.py:119
  8.7 0.7 %copy-start.5 = (f32[512]{0:T(512)S(1)}, f32[512]{0:T(512)}, u32[]{:S(2)}) copy-start(f32[512]{0:T(512)} %param.16) | copy-start | bytes 6148
  8.7 0.7 %copy-start.7 = (f32[256]{0:T(256)S(1)}, f32[256]{0:T(256)}, u32[]{:S(2)}) copy-start(f32[256]{0:T(256)} %param.20) | copy-start | bytes 3076
  11.0 4.5 %collective-permute-start.2 = (bf16[256,128]{1,0:T(8,128)(2,1)S(1)}, bf16[256,128]{1,0:T(8,128)(2,1)S(1)}, u32[]{:S(2)}, u32[]{:S(2)}) collective-permute-start(bf16[256,128]{1,0:T(8,128)(2,1)S(1)} %pad_maximum_fusion.1.rows), channel_id=1, source_target_pairs={{0,20},{1,21},{2,22},{3,23},{4,16},{5,17},{6,18},{7,19},{8,28},{9,... | collective-permute-start | bytes 196616 | tf_op jit(solution)/shard_map/ppermute | solution.py:119
  12.2 1.7 %collective-permute-start.4 = (bf16[64,1024]{1,0:T(8,128)(2,1)S(1)}, bf16[64,1024]{1,0:T(8,128)(2,1)S(1)}, u32[]{:S(2)}, u32[]{:S(2)}) collective-permute-start(bf16[64,1024]{1,0:T(8,128)(2,1)S(1)} %pad_maximum_fusion), channel_id=1, source_target_pairs={{0,4},{1,5},{2,6},{3,7},{4,0},{5,1},{6,2},{7,3},{8,12},{9,13},{10,... | collective-permute-start | bytes 393224 | tf_op jit(solution)/shard_map/ppermute | solution.py:119
  12.7 1.3 %collective-permute-start.7 = (bf16[64,512]{1,0:T(8,128)(2,1)S(1)}, bf16[64,512]{1,0:T(8,128)(2,1)S(1)}, u32[]{:S(2)}, u32[]{:S(2)}) collective-permute-start(bf16[64,512]{1,0:T(8,128)(2,1)S(1)} %collective-permute-done.5.rest_5_), channel_id=1, source_target_pairs={{0,4},{1,5},{2,6},{3,7},{4,0},{5,1},{6,2},{7,3},{8,12},{9,13},{10,... | collective-permute-start | bytes 196616 | tf_op jit(solution)/shard_map/ppermute | solution.py:119
  14.0 1.5 %copy-start.3 = (bf16[512,64]{0,1:T(8,128)(2,1)S(1)}, bf16[512,64]{0,1:T(8,128)(2,1)}, u32[]{:S(2)}) copy-start(bf16[512,64]{0,1:T(8,128)(2,1)} %param.14) | copy-start | bytes 196612
  17.1 3.4 %collective-permute-start.8 = (f16[128,128]{1,0:T(8,128)(2,1)S(1)}, f16[128,128]{1,0:T(8,128)(2,1)S(1)}, u32[]{:S(2)}, u32[]{:S(2)}) collective-permute-start(f16[128,128]{1,0:T(8,128)(2,1)S(1)} %multiply_convert_fusion), channel_id=1, source_target_pairs={{0,20},{1,21},{2,22},{3,23},{4,16},{5,17},{6,18},{7,19},{8,28},{9,... | collective-permute-start | bytes 98312 | tf_op jit(solution)/shard_map/ppermute | solution.py:119
  20.5 1.8 %collective-permute-start.10 = (f32[64,1024]{1,0:T(8,128)S(1)}, f32[64,1024]{1,0:T(8,128)S(1)}, u32[]{:S(2)}, u32[]{:S(2)}) collective-permute-start(f32[64,1024]{1,0:T(8,128)S(1)} %get-tuple-element.60), channel_id=1, source_target_pairs={{0,4},{1,5},{2,6},{3,7},{4,0},{5,1},{6,2},{7,3},{8,12},{9,13},{10,... | collective-permute-start | bytes 786440 | tf_op jit(solution)/shard_map/ppermute | solution.py:119
  20.8 3.2 %collective-permute-start.9 = (f16[64,128]{1,0:T(8,128)(2,1)S(1)}, f16[64,128]{1,0:T(8,128)(2,1)S(1)}, u32[]{:S(2)}, u32[]{:S(2)}) collective-permute-start(f16[64,128]{1,0:T(8,128)(2,1)S(1)} %fusion), channel_id=1, source_target_pairs={{0,5},{1,4},{2,7},{3,6},{4,1},{5,0},{6,3},{7,2},{8,13},{9,12},{10,... | collective-permute-start | bytes 49160 | tf_op jit(solution)/shard_map/ppermute | solution.py:119
  22.4 5.5 %collective-permute-start.12 = (f32[64,512]{1,0:T(8,128)S(1)}, f32[64,512]{1,0:T(8,128)S(1)}, u32[]{:S(2)}, u32[]{:S(2)}) collective-permute-start(f32[64,512]{1,0:T(8,128)S(1)} %get-tuple-element.66), channel_id=1, source_target_pairs={{0,12},{1,13},{2,14},{3,15},{4,8},{5,9},{6,10},{7,11},{8,4},{9,5},... | collective-permute-start | bytes 393224 | tf_op jit(solution)/shard_map/ppermute | solution.py:119
  24.1 4.5 %collective-permute-start.11 = (f16[32,128]{1,0:T(8,128)(2,1)S(1)}, f16[32,128]{1,0:T(8,128)(2,1)S(1)}, u32[]{:S(2)}, u32[]{:S(2)}) collective-permute-start(f16[32,128]{1,0:T(8,128)(2,1)S(1)} %fusion.1), channel_id=1, source_target_pairs={{0,6},{1,7},{2,4},{3,5},{4,2},{5,3},{6,0},{7,1},{8,14},{9,15},{10,... | collective-permute-start | bytes 24584 | tf_op jit(solution)/shard_map/ppermute | solution.py:119

commit v7 on v6

--- a/solution.py
+++ b/solution.py
@@ -86,15 +86,12 @@
     out[...] = rows[...]
 
 
-def finish_kernel(scale, own, got, result):
-    result[...] = (own[...] + got[...]) * scale[0]
-
-
-def finish_rows_kernel(scale, own, got, result):
-    tall, width = got.shape[0], result.shape[1]
-    total = (own[:tall, :] + got[...]) * scale[0]
-    result[:tall, :] = total[:, :width]
-    result[tall:, :] = total[:, width:]
+def finish_kernel(scale, own_cols, got_cols, own_rows, got_rows, col_result, row_result):
+    col_result[...] = (own_cols[...] + got_cols[...]) * scale[0]
+    tall, width = got_rows.shape[0], row_result.shape[1]
+    total = (own_rows[:tall, :] + got_rows[...]) * scale[0]
+    row_result[:tall, :] = total[:, :width]
+    row_result[tall:, :] = total[:, width:]
 
 
 def body(
@@ -192,13 +189,13 @@
         keep, give = jnp.split(row_sum, 2, axis=0)
         got, own_cols = lax.optimization_barrier((swap_sums(give, mask), own_cols))
         row_sum = keep + widen(got)
-    (col_result,) = call(
-        finish_kernel, [jax.ShapeDtypeStruct(got_cols.shape, F32)], (signal_scale, own_cols, got_cols), FINISH_FLOPS
-    )
-    got, col_result = lax.optimization_barrier((swap_sums(row_sum[block // 2 :], row_masks[0]), col_result))
-    got = widen(got)
-    (row_result,) = call(
-        finish_rows_kernel, [jax.ShapeDtypeStruct((block, nvec), F32)], (signal_scale, row_sum, got), FINISH_FLOPS
+    got = swap_sums(row_sum[block // 2 :], row_masks[0])
+    got, got_cols = lax.optimization_barrier((got, got_cols))
+    col_result, row_result = call(
+        finish_kernel,
+        [jax.ShapeDtypeStruct(got_cols.shape, F32), jax.ShapeDtypeStruct((block, nvec), F32)],
+        (signal_scale, own_cols, got_cols, row_sum, widen(got)),
+        FINISH_FLOPS,
     )
     return (row_result, col_result.T)
 

time: 29.6 us -> 29.1 us (0.983)
  Pallas kernels: 8.2 us -> 7.53 us
    pallas_call x8 -> x7, Pallas kernels: 8.2 us -> 7.53 us  [call(): pl.pallas_call(kernel, out_shape=outs, in_specs=[pl.BlockSpec(memory_spac...]
  transfers between devices with their start and end apart: 13 -> 13, of which waited for: 5 -> 5; matrix products, arithmetic and copies ran while one was open for 0% -> 0% of each run, Pallas kernels for 20% -> 18%
where the time goes in v7:
time: 29.1 us; the launch traced here: 28.8 us
  starting transfers between devices  15.2 us (52%)
  Pallas kernels  7.53 us (26%)
  waiting for transfers between devices  3.03 us (10%)
  between operations  1.42 us (5%)
  other arithmetic  0.93 us (3%)
  local copies, waits for them, and re-layouts  0.69 us (2%)
    ppermute x13, starting transfers between devices, swap(): return lax.ppermute(block, AXES, [(i, i ^ mask) for i in range(devices)])  15.2 us
    pallas_call x7, Pallas kernels, call(): pl.pallas_call(kernel, out_shape=outs, in_specs=[pl.BlockSpec(memory_spac...  7.53 us
    ppermute x13, waiting for transfers between devices, swap(): return lax.ppermute(block, AXES, [(i, i ^ mask) for i in range(devices)])  3.03 us
    concatenate x1, other arithmetic, body(): jnp.concatenate([row_points, row_vectors], axis=1)  0.82 us
    unnamed x17, local copies, waits for them, and re-layouts  0.69 us
  transfers between devices with their start and end apart: 13, of which 5 were waited for; matrix products, arithmetic and copies ran while one was open for 0% of the time, Pallas kernels for 18%

profile of v7, /device:TPU:0, one launch (start us, length us, event | category | flops | bytes accessed | tf_op | source)
XLA Modules:
  0.0 28.8 jit_solution(11705913001665246374)
XLA Ops:
  0.6 0.8 %pad_maximum_fusion.3 = bf16[64,128]{1,0:T(8,128)(2,1)S(1)} fusion(bf16[64,64]{1,0:T(8,128)(2,1)} %param.13, bf16[64,64]{1,0:T(8,128)(2,1)} %param.11), kind=kLoop, calls=%fused_computation.12 | loop fusion | flops 32768 | bytes 32768 | tf_op jit(solution)/shard_map/concatenate | solution.py:140
  1.4 3.5 %collective-permute-start = (bf16[64,128]{1,0:T(8,128)(2,1)S(1)}, bf16[64,128]{1,0:T(8,128)(2,1)S(1)}, u32[]{:S(2)}, u32[]{:S(2)}) collective-permute-start(bf16[64,128]{1,0:T(8,128)(2,1)S(1)} %pad_maximum_fusion.3), channel_id=1, source_target_pairs={{0,6},{1,7},{2,4},{3,5},{4,2},{5,3},{6,0},{7,1},{8,14},{9,15},{10,... | collective-permute-start | bytes 49160 | tf_op jit(solution)/shard_map/ppermute | solution.py:116
  4.9 1.8 %collective-permute-start.5 = (bf16[64,512]{1,0:T(8,128)(2,1)}, bf16[64,512]{1,0:T(8,128)(2,1)S(1)}, u32[]{:S(2)}, u32[]{:S(2)}) collective-permute-start(bf16[64,512]{1,0:T(8,128)(2,1)} %bitcast.6), channel_id=1, source_target_pairs={{0,12},{1,13},{2,14},{3,15},{4,8},{5,9},{6,10},{7,11},{8,4},{9,5},... | collective-permute-start | bytes 196616 | tf_op jit(solution)/shard_map/ppermute | solution.py:116
  6.7 0.0 collective-permute-start.6
  6.7 0.0 copy-start
  6.7 0.0 copy-start.1
  6.7 0.6 %collective-permute-start.3 = (bf16[64,512]{1,0:T(8,128)(2,1)}, bf16[64,512]{1,0:T(8,128)(2,1)S(1)}, u32[]{:S(2)}, u32[]{:S(2)}) collective-permute-start(bf16[64,512]{1,0:T(8,128)(2,1)} %bitcast.10), channel_id=1, source_target_pairs={{0,12},{1,13},{2,14},{3,15},{4,8},{5,9},{6,10},{7,11},{8,4},{9,5},... | collective-permute-start | bytes 196616 | tf_op jit(solution)/shard_map/ppermute | solution.py:116
  7.4 0.0 collective-permute-done.rows
  7.4 0.0 copy-start.4
  7.4 0.0 copy-start.6
  7.4 0.0 copy-start.2
  7.4 1.2 %collective-permute-start.1 = (bf16[128,128]{1,0:T(8,128)(2,1)S(1)}, bf16[128,128]{1,0:T(8,128)(2,1)S(1)}, u32[]{:S(2)}, u32[]{:S(2)}) collective-permute-start(bf16[128,128]{1,0:T(8,128)(2,1)S(1)} %pad_maximum_fusion.2), channel_id=1, source_target_pairs={{0,5},{1,4},{2,7},{3,6},{4,1},{5,0},{6,3},{7,2},{8,13},{9,12},{10,... | collective-permute-start | bytes 98312 | tf_op jit(solution)/shard_map/ppermute | solution.py:116
  8.7 0.0 copy-start.5
  8.7 0.0 copy-start.7
  8.7 0.0 copy-done
  8.7 0.0 copy-done.1
  8.7 0.0 copy-done.4
  8.7 0.0 copy-done.6
  8.7 0.0 copy-done.2
  8.7 0.6 %copy-done.5 = f32[512]{0:T(512)S(1)} copy-done((f32[512]{0:T(512)S(1)}, f32[512]{0:T(512)}, u32[]{:S(2)}) %copy-start.5) | copy-done | bytes 2072
  9.3 0.0 copy-done.7
  9.3 0.9 %shard_map.123 = (bf16[256,512]{1,0:T(8,128)(2,1)S(1)}, f32[1,512]{1,0:T(1,128)S(1)}) custom-call(bf16[64,512]{1,0:T(8,128)(2,1)S(1)} %bitcast.11, bf16[64,512]{1,0:T(8,128)(2,1)S(1)} %copy-done.2, f32[1,512]{1,0:T(1,128)S(1)} %bitcast.13, bf16[512,512]{1,0:T(8,128)(2,1)S(1)} %copy-done, f32[1,512]{1,0:T(1,128)S(1)} %bitcast.18, ...), custom_call_target="tpu_custom_call" | custom-call | flops 436207616 | bytes 1048576 | tf_op jit(solution)/shard_map/pallas_call | solution.py:75
  10.3 0.7 %collective-permute-done.1 = bf16[128,128]{1,0:T(8,128)(2,1)S(1)} collective-permute-done((bf16[128,128]{1,0:T(8,128)(2,1)S(1)}, bf16[128,128]{1,0:T(8,128)(2,1)S(1)}, u32[]{:S(2)}, u32[]{:S(2)}) %collective-permute-start.1) | collective-permute-done | bytes 32800 | tf_op jit(solution)/shard_map/ppermute | solution.py:116
  11.0 1.2 %collective-permute-start.2 = (bf16[256,128]{1,0:T(8,128)(2,1)S(1)}, bf16[256,128]{1,0:T(8,128)(2,1)S(1)}, u32[]{:S(2)}, u32[]{:S(2)}) collective-permute-start(bf16[256,128]{1,0:T(8,128)(2,1)S(1)} %pad_maximum_fusion.1.rows), channel_id=1, source_target_pairs={{0,20},{1,21},{2,22},{3,23},{4,16},{5,17},{6,18},{7,19},{8,28},{9,... | collective-permute-start | bytes 196616 | tf_op jit(solution)/shard_map/ppermute | solution.py:116
  12.2 0.0 collective-permute-done.3.points
  12.2 0.5 %collective-permute-start.4 = (bf16[64,1024]{1,0:T(8,128)(2,1)S(1)}, bf16[64,1024]{1,0:T(8,128)(2,1)S(1)}, u32[]{:S(2)}, u32[]{:S(2)}) collective-permute-start(bf16[64,1024]{1,0:T(8,128)(2,1)S(1)} %pad_maximum_fusion), channel_id=1, source_target_pairs={{0,4},{1,5},{2,6},{3,7},{4,0},{5,1},{6,2},{7,3},{8,12},{9,13},{10,... | collective-permute-start | bytes 393224 | tf_op jit(solution)/shard_map/ppermute | solution.py:116
  12.7 0.0 collective-permute-done.5.rest_5_
  12.7 0.1 collective-permute-start.7
  12.8 0.0 collective-permute-done.6
  12.8 0.9 %shard_map.124 = (bf16[256,512]{1,0:T(8,128)(2,1)S(1)}, f32[1,512]{1,0:T(1,128)S(1)}) custom-call(bf16[64,512]{1,0:T(8,128)(2,1)S(1)} %collective-permute-done.3.points, bf16[64,512]{1,0:T(8,128)(2,1)S(1)} %copy-done.2, f32[1,512]{1,0:T(1,128)S(1)} %bitcast.14, bf16[512,512]{1,0:T(8,128)(2,1)S(1)} %copy-done, f32[1,512]{1,0:T(1,128)S(1)} %bitcast.19, ...), custom_call_target="tpu_custom_call" | custom-call | flops 436207616 | bytes 1048576 | tf_op jit(solution)/shard_map/pallas_call | solution.py:75
  13.8 0.2 collective-permute-done.7
  14.0 0.0 collective-permute-done.4.points
  14.0 1.5 %shard_map.125 = (bf16[256,1024]{1,0:T(8,128)(2,1)S(1)}, f32[1,1024]{1,0:T(1,128)S(1)}) custom-call(bf16[64,1024]{1,0:T(8,128)(2,1)S(1)} %collective-permute-done.4.points, bf16[64,512]{1,0:T(8,128)(2,1)S(1)} %copy-done.2, f32[1,512]{1,0:T(1,128)S(1)} %bitcast.15, bf16[512,512]{1,0:T(8,128)(2,1)S(1)} %copy-done, f32[1,512]{1,0:T(1,128)S(1)} %bitcast.20, ...), custom_call_target="tpu_custom_call" | custom-call | flops 872415232 | bytes 1048576 | tf_op jit(solution)/shard_map/pallas_call | solution.py:75
  15.5 0.0 collective-permute-done.2.rows.rest_15_
  15.5 0.0 copy-done.3
  15.5 1.6 %shard_map.126 = (f32[128,128]{1,0:T(8,128)S(1)}, bf16[256,512]{1,0:T(8,128)(2,1)S(1)}, bf16[256,512]{1,0:T(8,128)(2,1)S(1)}, bf16[256,1024]{1,0:T(8,128)(2,1)S(1)}) custom-call(bf16[256,128]{1,0:T(8,128)(2,1)S(1)} %collective-permute-done.2.rows.rest_15_, bf16[256,512]{1,0:T(8,128)(2,1)S(1)} %get-tuple-element.45.rest_0_, ...), custom_call_target="tpu_custom_call" | custom-call | flops 754974720 | bytes 1048576 | tf_op jit(solution)/shard_map/pallas_call | solution.py:75
  17.1 0.9 %collective-permute-start.8 = (f16[128,128]{1,0:T(8,128)(2,1)S(1)}, f16[128,128]{1,0:T(8,128)(2,1)S(1)}, u32[]{:S(2)}, u32[]{:S(2)}) collective-permute-start(f16[128,128]{1,0:T(8,128)(2,1)S(1)} %multiply_convert_fusion), channel_id=1, source_target_pairs={{0,20},{1,21},{2,22},{3,23},{4,16},{5,17},{6,18},{7,19},{8,28},{9,... | collective-permute-start | bytes 98312 | tf_op jit(solution)/shard_map/ppermute | solution.py:116
  18.0 1.9 %shard_map.127 = (f32[128,128]{1,0:T(8,128)S(1)}, f32[64,512]{1,0:T(8,128)S(1)}, f32[64,512]{1,0:T(8,128)S(1)}, f32[64,1024]{1,0:T(8,128)S(1)}) custom-call(bf16[256,128]{1,0:T(8,128)(2,1)S(1)} %pad_maximum_fusion.1.rows, bf16[256,512]{1,0:T(8,128)(2,1)S(1)} %get-tuple-element.45.rest_0_, f32[1,512]{1,0:T(1,128)S(1)} %get-tuple-element.46.rest_1_, ...), custom_call_target="tpu_custom_call" | custom-call | flops 754974720 | bytes 1048576 | tf_op jit(solution)/shard_map/pallas_call | solution.py:75
  19.8 0.7 %collective-permute-done.8 = f16[128,128]{1,0:T(8,128)(2,1)S(1)} collective-permute-done((f16[128,128]{1,0:T(8,128)(2,1)S(1)}, f16[128,128]{1,0:T(8,128)(2,1)S(1)}, u32[]{:S(2)}, u32[]{:S(2)}) %collective-permute-start.8) | collective-permute-done | bytes 32800 | tf_op jit(solution)/shard_map/ppermute | solution.py:116
  20.5 0.2 collective-permute-start.10
  20.8 1.5 %collective-permute-start.9 = (f16[64,128]{1,0:T(8,128)(2,1)S(1)}, f16[64,128]{1,0:T(8,128)(2,1)S(1)}, u32[]{:S(2)}, u32[]{:S(2)}) collective-permute-start(f16[64,128]{1,0:T(8,128)(2,1)S(1)} %fusion), channel_id=1, source_target_pairs={{0,5},{1,4},{2,7},{3,6},{4,1},{5,0},{6,3},{7,2},{8,13},{9,12},{10,... | collective-permute-start | bytes 49160 | tf_op jit(solution)/shard_map/ppermute | solution.py:116
  22.3 0.0 collective-permute-done.10
  22.4 1.4 %collective-permute-start.12 = (f32[64,512]{1,0:T(8,128)S(1)}, f32[64,512]{1,0:T(8,128)S(1)}, u32[]{:S(2)}, u32[]{:S(2)}) collective-permute-start(f32[64,512]{1,0:T(8,128)S(1)} %get-tuple-element.70), channel_id=1, source_target_pairs={{0,12},{1,13},{2,14},{3,15},{4,8},{5,9},{6,10},{7,11},{8,4},{9,5},... | collective-permute-start | bytes 393224 | tf_op jit(solution)/shard_map/ppermute | solution.py:116
  23.8 0.3 collective-permute-done.9
  24.1 2.2 %collective-permute-start.11 = (f16[32,128]{1,0:T(8,128)(2,1)S(1)}, f16[32,128]{1,0:T(8,128)(2,1)S(1)}, u32[]{:S(2)}, u32[]{:S(2)}) collective-permute-start(f16[32,128]{1,0:T(8,128)(2,1)S(1)} %fusion.1), channel_id=1, source_target_pairs={{0,6},{1,7},{2,4},{3,5},{4,2},{5,3},{6,0},{7,1},{8,14},{9,15},{10,... | collective-permute-start | bytes 24584 | tf_op jit(solution)/shard_map/ppermute | solution.py:116
  26.9 1.2 %collective-permute-done.11 = f16[32,128]{1,0:T(8,128)(2,1)S(1)} collective-permute-done((f16[32,128]{1,0:T(8,128)(2,1)S(1)}, f16[32,128]{1,0:T(8,128)(2,1)S(1)}, u32[]{:S(2)}, u32[]{:S(2)}) %collective-permute-start.11) | collective-permute-done | bytes 8224 | tf_op jit(solution)/shard_map/ppermute | solution.py:116
  28.1 0.0 collective-permute-done.12.got_cols
  28.1 0.7 %shard_map.128 = (f32[64,512]{1,0:T(8,128)}, f32[64,64]{1,0:T(8,128)}) custom-call(f32[1]{0:T(128)S(6)} %copy.14.scale, f32[64,512]{1,0:T(8,128)S(1)} %get-tuple-element.63.own_cols, f32[64,512]{1,0:T(8,128)S(1)} %collective-permute-done.12.got_cols, f32[64,128]{1,0:T(8,128)S(1)} %slice_add_fusion.2.own_rows, f32[32,128]{1,0:T(8,128)S(1)} %convert_multiply_fusion.got_rows), custom_call_target="tpu_custom_call" | custom-call | flops 1000000 | bytes 1048576 | tf_op jit(solution)/shard_map/pallas_call | solution.py:75
  (14 shorter events, 0.1 us)
Async XLA Ops:
  1.4 5.9 %collective-permute-start = (bf16[64,128]{1,0:T(8,128)(2,1)S(1)}, bf16[64,128]{1,0:T(8,128)(2,1)S(1)}, u32[]{:S(2)}, u32[]{:S(2)}) collective-permute-start(bf16[64,128]{1,0:T(8,128)(2,1)S(1)} %pad_maximum_fusion.3), channel_id=1, source_target_pairs={{0,6},{1,7},{2,4},{3,5},{4,2},{5,3},{6,0},{7,1},{8,14},{9,15},{10,... | collective-permute-start | bytes 49160 | tf_op jit(solution)/shard_map/ppermute | solution.py:116
  4.9 7.8 %collective-permute-start.5 = (bf16[64,512]{1,0:T(8,128)(2,1)}, bf16[64,512]{1,0:T(8,128)(2,1)S(1)}, u32[]{:S(2)}, u32[]{:S(2)}) collective-permute-start(bf16[64,512]{1,0:T(8,128)(2,1)} %bitcast.6), channel_id=1, source_target_pairs={{0,12},{1,13},{2,14},{3,15},{4,8},{5,9},{6,10},{7,11},{8,4},{9,5},... | collective-permute-start | bytes 196616 | tf_op jit(solution)/shard_map/ppermute | solution.py:116
  6.7 6.1 %collective-permute-start.6 = (bf16[64,512]{1,0:T(8,128)(2,1)}, bf16[64,512]{1,0:T(8,128)(2,1)S(1)}, u32[]{:S(2)}, u32[]{:S(2)}) collective-permute-start(bf16[64,512]{1,0:T(8,128)(2,1)} %bitcast.7), channel_id=1, source_target_pairs={{0,4},{1,5},{2,6},{3,7},{4,0},{5,1},{6,2},{7,3},{8,12},{9,13},{10,... | collective-permute-start | bytes 196616 | tf_op jit(solution)/shard_map/ppermute | solution.py:116
  6.7 1.9 %copy-start = (bf16[512,512]{1,0:T(8,128)(2,1)S(1)}, bf16[512,512]{1,0:T(8,128)(2,1)}, u32[]{:S(2)}) copy-start(bf16[512,512]{1,0:T(8,128)(2,1)} %rest_11_.3) | copy-start | bytes 1572868
  6.7 1.9 %copy-start.1 = (bf16[512,256]{1,0:T(8,128)(2,1)S(1)}, bf16[512,256]{1,0:T(8,128)(2,1)}, u32[]{:S(2)}) copy-start(bf16[512,256]{1,0:T(8,128)(2,1)} %rest_13_.3) | copy-start | bytes 786436
  6.7 5.5 %collective-permute-start.3 = (bf16[64,512]{1,0:T(8,128)(2,1)}, bf16[64,512]{1,0:T(8,128)(2,1)S(1)}, u32[]{:S(2)}, u32[]{:S(2)}) collective-permute-start(bf16[64,512]{1,0:T(8,128)(2,1)} %bitcast.10), channel_id=1, source_target_pairs={{0,12},{1,13},{2,14},{3,15},{4,8},{5,9},{6,10},{7,11},{8,4},{9,5},... | collective-permute-start | bytes 196616 | tf_op jit(solution)/shard_map/ppermute | solution.py:116
  7.4 1.3 %copy-start.4 = (bf16[512,64]{0,1:T(8,128)(2,1)S(1)}, bf16[512,64]{0,1:T(8,128)(2,1)}, u32[]{:S(2)}) copy-start(bf16[512,64]{0,1:T(8,128)(2,1)} %param.12) | copy-start | bytes 196612
  7.4 1.3 %copy-start.6 = (f32[512]{0:T(512)S(1)}, f32[512]{0:T(512)}, u32[]{:S(2)}) copy-start(f32[512]{0:T(512)} %param.18) | copy-start | bytes 6148
  7.4 1.3 %copy-start.2 = (bf16[64,512]{1,0:T(8,128)(2,1)S(1)}, bf16[64,512]{1,0:T(8,128)(2,1)}, u32[]{:S(2)}) copy-start(bf16[64,512]{1,0:T(8,128)(2,1)} %rest_9_.3) | copy-start | bytes 196612
  7.4 3.6 %collective-permute-start.1 = (bf16[128,128]{1,0:T(8,128)(2,1)S(1)}, bf16[128,128]{1,0:T(8,128)(2,1)S(1)}, u32[]{:S(2)}, u32[]{:S(2)}) collective-permute-start(bf16[128,128]{1,0:T(8,128)(2,1)S(1)} %pad_maximum_fusion.2), channel_id=1, source_target_pairs={{0,5},{1,4},{2,7},{3,6},{4,1},{5,0},{6,3},{7,2},{8,13},{9,12},{10,... | collective-permute-start | bytes 98312 | tf_op jit(solution)/shard_map/ppermute | solution.py:116
  8.7 0.7 %copy-start.5 = (f32[512]{0:T(512)S(1)}, f32[512]{0:T(512)}, u32[]{:S(2)}) copy-start(f32[512]{0:T(512)} %param.16) | copy-start | bytes 6148
  8.7 0.7 %copy-start.7 = (f32[256]{0:T(256)S(1)}, f32[256]{0:T(256)}, u32[]{:S(2)}) copy-start(f32[256]{0:T(256)} %param.20) | copy-start | bytes 3076
  11.0 4.5 %collective-permute-start.2 = (bf16[256,128]{1,0:T(8,128)(2,1)S(1)}, bf16[256,128]{1,0:T(8,128)(2,1)S(1)}, u32[]{:S(2)}, u32[]{:S(2)}) collective-permute-start(bf16[256,128]{1,0:T(8,128)(2,1)S(1)} %pad_maximum_fusion.1.rows), channel_id=1, source_target_pairs={{0,20},{1,21},{2,22},{3,23},{4,16},{5,17},{6,18},{7,19},{8,28},{9,... | collective-permute-start | bytes 196616 | tf_op jit(solution)/shard_map/ppermute | solution.py:116
  12.2 1.7 %collective-permute-start.4 = (bf16[64,1024]{1,0:T(8,128)(2,1)S(1)}, bf16[64,1024]{1,0:T(8,128)(2,1)S(1)}, u32[]{:S(2)}, u32[]{:S(2)}) collective-permute-start(bf16[64,1024]{1,0:T(8,128)(2,1)S(1)} %pad_maximum_fusion), channel_id=1, source_target_pairs={{0,4},{1,5},{2,6},{3,7},{4,0},{5,1},{6,2},{7,3},{8,12},{9,13},{10,... | collective-permute-start | bytes 393224 | tf_op jit(solution)/shard_map/ppermute | solution.py:116
  12.7 1.3 %collective-permute-start.7 = (bf16[64,512]{1,0:T(8,128)(2,1)S(1)}, bf16[64,512]{1,0:T(8,128)(2,1)S(1)}, u32[]{:S(2)}, u32[]{:S(2)}) collective-permute-start(bf16[64,512]{1,0:T(8,128)(2,1)S(1)} %collective-permute-done.5.rest_5_), channel_id=1, source_target_pairs={{0,4},{1,5},{2,6},{3,7},{4,0},{5,1},{6,2},{7,3},{8,12},{9,13},{10,... | collective-permute-start | bytes 196616 | tf_op jit(solution)/shard_map/ppermute | solution.py:116
  14.0 1.5 %copy-start.3 = (bf16[512,64]{0,1:T(8,128)(2,1)S(1)}, bf16[512,64]{0,1:T(8,128)(2,1)}, u32[]{:S(2)}) copy-start(bf16[512,64]{0,1:T(8,128)(2,1)} %param.14) | copy-start | bytes 196612
  17.1 3.4 %collective-permute-start.8 = (f16[128,128]{1,0:T(8,128)(2,1)S(1)}, f16[128,128]{1,0:T(8,128)(2,1)S(1)}, u32[]{:S(2)}, u32[]{:S(2)}) collective-permute-start(f16[128,128]{1,0:T(8,128)(2,1)S(1)} %multiply_convert_fusion), channel_id=1, source_target_pairs={{0,20},{1,21},{2,22},{3,23},{4,16},{5,17},{6,18},{7,19},{8,28},{9,... | collective-permute-start | bytes 98312 | tf_op jit(solution)/shard_map/ppermute | solution.py:116
  20.5 1.8 %collective-permute-start.10 = (f32[64,1024]{1,0:T(8,128)S(1)}, f32[64,1024]{1,0:T(8,128)S(1)}, u32[]{:S(2)}, u32[]{:S(2)}) collective-permute-start(f32[64,1024]{1,0:T(8,128)S(1)} %get-tuple-element.62), channel_id=1, source_target_pairs={{0,4},{1,5},{2,6},{3,7},{4,0},{5,1},{6,2},{7,3},{8,12},{9,13},{10,... | collective-permute-start | bytes 786440 | tf_op jit(solution)/shard_map/ppermute | solution.py:116
  20.8 3.2 %collective-permute-start.9 = (f16[64,128]{1,0:T(8,128)(2,1)S(1)}, f16[64,128]{1,0:T(8,128)(2,1)S(1)}, u32[]{:S(2)}, u32[]{:S(2)}) collective-permute-start(f16[64,128]{1,0:T(8,128)(2,1)S(1)} %fusion), channel_id=1, source_target_pairs={{0,5},{1,4},{2,7},{3,6},{4,1},{5,0},{6,3},{7,2},{8,13},{9,12},{10,... | collective-permute-start | bytes 49160 | tf_op jit(solution)/shard_map/ppermute | solution.py:116
  22.4 5.7 %collective-permute-start.12 = (f32[64,512]{1,0:T(8,128)S(1)}, f32[64,512]{1,0:T(8,128)S(1)}, u32[]{:S(2)}, u32[]{:S(2)}) collective-permute-start(f32[64,512]{1,0:T(8,128)S(1)} %get-tuple-element.70), channel_id=1, source_target_pairs={{0,12},{1,13},{2,14},{3,15},{4,8},{5,9},{6,10},{7,11},{8,4},{9,5},... | collective-permute-start | bytes 393224 | tf_op jit(solution)/shard_map/ppermute | solution.py:116
  24.1 4.0 %collective-permute-start.11 = (f16[32,128]{1,0:T(8,128)(2,1)S(1)}, f16[32,128]{1,0:T(8,128)(2,1)S(1)}, u32[]{:S(2)}, u32[]{:S(2)}) collective-permute-start(f16[32,128]{1,0:T(8,128)(2,1)S(1)} %fusion.1), channel_id=1, source_target_pairs={{0,6},{1,7},{2,4},{3,5},{4,2},{5,3},{6,0},{7,1},{8,14},{9,15},{10,... | collective-permute-start | bytes 24584 | tf_op jit(solution)/shard_map/ppermute | solution.py:116

commit v8 on v7

--- a/solution.py
+++ b/solution.py
@@ -51,8 +51,9 @@
         row_half = 0.5 * jnp.sum(jnp.square(row_feats.astype(F32)), axis=1, keepdims=True)
         row_acc = None
         for side, (feats, half_sq, col_vecs) in enumerate(columns):
-            for start in range(0, feats.shape[1], chunk_cols):
-                part = pl.ds(start, chunk_cols)
+            wide = min(2 * chunk_cols, feats.shape[1])
+            for start in range(0, feats.shape[1], wide):
+                part = pl.ds(start, wide)
                 inner = dot(row_feats, feats[:, part], ((1,), (0,)))
                 kernel = jnp.exp(inner - row_half - half_sq[:, part]).astype(BF16)
                 term = dot(kernel, col_vecs[:, part], ((1,), (1,)))

time: 29.1 us -> 29.1 us (level)
  no operation moved by 1% of the time
where the time goes in v8:
time: 29.1 us; the launch traced here: 28.8 us
  starting transfers between devices  15.2 us (52%)
  Pallas kernels  7.48 us (26%)
  waiting for transfers between devices  3.09 us (11%)
  between operations  1.42 us (5%)
  other arithmetic  0.93 us (3%)
  local copies, waits for them, and re-layouts  0.69 us (2%)
    ppermute x13, starting transfers between devices, swap(): return lax.ppermute(block, AXES, [(i, i ^ mask) for i in range(devices)])  15.2 us
    pallas_call x7, Pallas kernels, call(): pl.pallas_call(kernel, out_shape=outs, in_specs=[pl.BlockSpec(memory_spac...  7.48 us
    ppermute x13, waiting for transfers between devices, swap(): return lax.ppermute(block, AXES, [(i, i ^ mask) for i in range(devices)])  3.09 us
    concatenate x1, other arithmetic, body(): jnp.concatenate([row_points, row_vectors], axis=1)  0.82 us
    unnamed x17, local copies, waits for them, and re-layouts  0.69 us
  transfers between devices with their start and end apart: 13, of which 5 were waited for; matrix products, arithmetic and copies ran while one was open for 0% of the time, Pallas kernels for 18%

profile of v8, /device:TPU:0, one launch (start us, length us, event | category | flops | bytes accessed | tf_op | source)
XLA Modules:
  0.0 28.8 jit_solution(15369522916224763779)
XLA Ops:
  0.6 0.8 %pad_maximum_fusion.3 = bf16[64,128]{1,0:T(8,128)(2,1)S(1)} fusion(bf16[64,64]{1,0:T(8,128)(2,1)} %param.13, bf16[64,64]{1,0:T(8,128)(2,1)} %param.11), kind=kLoop, calls=%fused_computation.12 | loop fusion | flops 32768 | bytes 32768 | tf_op jit(solution)/shard_map/concatenate | solution.py:141
  1.4 3.5 %collective-permute-start = (bf16[64,128]{1,0:T(8,128)(2,1)S(1)}, bf16[64,128]{1,0:T(8,128)(2,1)S(1)}, u32[]{:S(2)}, u32[]{:S(2)}) collective-permute-start(bf16[64,128]{1,0:T(8,128)(2,1)S(1)} %pad_maximum_fusion.3), channel_id=1, source_target_pairs={{0,6},{1,7},{2,4},{3,5},{4,2},{5,3},{6,0},{7,1},{8,14},{9,15},{10,... | collective-permute-start | bytes 49160 | tf_op jit(solution)/shard_map/ppermute | solution.py:117
  4.9 1.8 %collective-permute-start.5 = (bf16[64,512]{1,0:T(8,128)(2,1)}, bf16[64,512]{1,0:T(8,128)(2,1)S(1)}, u32[]{:S(2)}, u32[]{:S(2)}) collective-permute-start(bf16[64,512]{1,0:T(8,128)(2,1)} %bitcast.6), channel_id=1, source_target_pairs={{0,12},{1,13},{2,14},{3,15},{4,8},{5,9},{6,10},{7,11},{8,4},{9,5},... | collective-permute-start | bytes 196616 | tf_op jit(solution)/shard_map/ppermute | solution.py:117
  6.7 0.0 collective-permute-start.6
  6.7 0.0 copy-start
  6.7 0.0 copy-start.1
  6.7 0.6 %collective-permute-start.3 = (bf16[64,512]{1,0:T(8,128)(2,1)}, bf16[64,512]{1,0:T(8,128)(2,1)S(1)}, u32[]{:S(2)}, u32[]{:S(2)}) collective-permute-start(bf16[64,512]{1,0:T(8,128)(2,1)} %bitcast.10), channel_id=1, source_target_pairs={{0,12},{1,13},{2,14},{3,15},{4,8},{5,9},{6,10},{7,11},{8,4},{9,5},... | collective-permute-start | bytes 196616 | tf_op jit(solution)/shard_map/ppermute | solution.py:117
  7.4 0.0 collective-permute-done.rows
  7.4 0.0 copy-start.4
  7.4 0.0 copy-start.6
  7.4 0.0 copy-start.2
  7.4 1.2 %collective-permute-start.1 = (bf16[128,128]{1,0:T(8,128)(2,1)S(1)}, bf16[128,128]{1,0:T(8,128)(2,1)S(1)}, u32[]{:S(2)}, u32[]{:S(2)}) collective-permute-start(bf16[128,128]{1,0:T(8,128)(2,1)S(1)} %pad_maximum_fusion.2), channel_id=1, source_target_pairs={{0,5},{1,4},{2,7},{3,6},{4,1},{5,0},{6,3},{7,2},{8,13},{9,12},{10,... | collective-permute-start | bytes 98312 | tf_op jit(solution)/shard_map/ppermute | solution.py:117
  8.7 0.0 copy-start.5
  8.7 0.0 copy-start.7
  8.7 0.0 copy-done
  8.7 0.0 copy-done.1
  8.7 0.0 copy-done.4
  8.7 0.0 copy-done.6
  8.7 0.0 copy-done.2
  8.7 0.6 %copy-done.5 = f32[512]{0:T(512)S(1)} copy-done((f32[512]{0:T(512)S(1)}, f32[512]{0:T(512)}, u32[]{:S(2)}) %copy-start.5) | copy-done | bytes 2072
  9.3 0.0 copy-done.7
  9.3 0.9 %shard_map.123 = (bf16[256,512]{1,0:T(8,128)(2,1)S(1)}, f32[1,512]{1,0:T(1,128)S(1)}) custom-call(bf16[64,512]{1,0:T(8,128)(2,1)S(1)} %bitcast.11, bf16[64,512]{1,0:T(8,128)(2,1)S(1)} %copy-done.2, f32[1,512]{1,0:T(1,128)S(1)} %bitcast.13, bf16[512,512]{1,0:T(8,128)(2,1)S(1)} %copy-done, f32[1,512]{1,0:T(1,128)S(1)} %bitcast.18, ...), custom_call_target="tpu_custom_call" | custom-call | flops 436207616 | bytes 1048576 | tf_op jit(solution)/shard_map/pallas_call | solution.py:76
  10.3 0.7 %collective-permute-done.1 = bf16[128,128]{1,0:T(8,128)(2,1)S(1)} collective-permute-done((bf16[128,128]{1,0:T(8,128)(2,1)S(1)}, bf16[128,128]{1,0:T(8,128)(2,1)S(1)}, u32[]{:S(2)}, u32[]{:S(2)}) %collective-permute-start.1) | collective-permute-done | bytes 32800 | tf_op jit(solution)/shard_map/ppermute | solution.py:117
  11.0 1.2 %collective-permute-start.2 = (bf16[256,128]{1,0:T(8,128)(2,1)S(1)}, bf16[256,128]{1,0:T(8,128)(2,1)S(1)}, u32[]{:S(2)}, u32[]{:S(2)}) collective-permute-start(bf16[256,128]{1,0:T(8,128)(2,1)S(1)} %pad_maximum_fusion.1.rows), channel_id=1, source_target_pairs={{0,20},{1,21},{2,22},{3,23},{4,16},{5,17},{6,18},{7,19},{8,28},{9,... | collective-permute-start | bytes 196616 | tf_op jit(solution)/shard_map/ppermute | solution.py:117
  12.2 0.0 collective-permute-done.3.points
  12.2 0.5 %collective-permute-start.4 = (bf16[64,1024]{1,0:T(8,128)(2,1)S(1)}, bf16[64,1024]{1,0:T(8,128)(2,1)S(1)}, u32[]{:S(2)}, u32[]{:S(2)}) collective-permute-start(bf16[64,1024]{1,0:T(8,128)(2,1)S(1)} %pad_maximum_fusion), channel_id=1, source_target_pairs={{0,4},{1,5},{2,6},{3,7},{4,0},{5,1},{6,2},{7,3},{8,12},{9,13},{10,... | collective-permute-start | bytes 393224 | tf_op jit(solution)/shard_map/ppermute | solution.py:117
  12.7 0.0 collective-permute-done.5.rest_5_
  12.7 0.1 collective-permute-start.7
  12.8 0.0 collective-permute-done.6
  12.8 0.9 %shard_map.124 = (bf16[256,512]{1,0:T(8,128)(2,1)S(1)}, f32[1,512]{1,0:T(1,128)S(1)}) custom-call(bf16[64,512]{1,0:T(8,128)(2,1)S(1)} %collective-permute-done.3.points, bf16[64,512]{1,0:T(8,128)(2,1)S(1)} %copy-done.2, f32[1,512]{1,0:T(1,128)S(1)} %bitcast.14, bf16[512,512]{1,0:T(8,128)(2,1)S(1)} %copy-done, f32[1,512]{1,0:T(1,128)S(1)} %bitcast.19, ...), custom_call_target="tpu_custom_call" | custom-call | flops 436207616 | bytes 1048576 | tf_op jit(solution)/shard_map/pallas_call | solution.py:76
  13.8 0.2 collective-permute-done.7
  14.0 0.0 collective-permute-done.4.points
  14.0 1.5 %shard_map.125 = (bf16[256,1024]{1,0:T(8,128)(2,1)S(1)}, f32[1,1024]{1,0:T(1,128)S(1)}) custom-call(bf16[64,1024]{1,0:T(8,128)(2,1)S(1)} %collective-permute-done.4.points, bf16[64,512]{1,0:T(8,128)(2,1)S(1)} %copy-done.2, f32[1,512]{1,0:T(1,128)S(1)} %bitcast.15, bf16[512,512]{1,0:T(8,128)(2,1)S(1)} %copy-done, f32[1,512]{1,0:T(1,128)S(1)} %bitcast.20, ...), custom_call_target="tpu_custom_call" | custom-call | flops 872415232 | bytes 1048576 | tf_op jit(solution)/shard_map/pallas_call | solution.py:76
  15.5 0.0 collective-permute-done.2.rows.rest_15_
  15.5 0.0 copy-done.3
  15.5 1.6 %shard_map.126 = (f32[128,128]{1,0:T(8,128)S(1)}, bf16[256,512]{1,0:T(8,128)(2,1)S(1)}, bf16[256,512]{1,0:T(8,128)(2,1)S(1)}, bf16[256,1024]{1,0:T(8,128)(2,1)S(1)}) custom-call(bf16[256,128]{1,0:T(8,128)(2,1)S(1)} %collective-permute-done.2.rows.rest_15_, bf16[256,512]{1,0:T(8,128)(2,1)S(1)} %get-tuple-element.45.rest_0_, ...), custom_call_target="tpu_custom_call" | custom-call | flops 754974720 | bytes 1048576 | tf_op jit(solution)/shard_map/pallas_call | solution.py:76
  17.1 0.9 %collective-permute-start.8 = (f16[128,128]{1,0:T(8,128)(2,1)S(1)}, f16[128,128]{1,0:T(8,128)(2,1)S(1)}, u32[]{:S(2)}, u32[]{:S(2)}) collective-permute-start(f16[128,128]{1,0:T(8,128)(2,1)S(1)} %multiply_convert_fusion), channel_id=1, source_target_pairs={{0,20},{1,21},{2,22},{3,23},{4,16},{5,17},{6,18},{7,19},{8,28},{9,... | collective-permute-start | bytes 98312 | tf_op jit(solution)/shard_map/ppermute | solution.py:117
  18.0 1.8 %shard_map.127 = (f32[128,128]{1,0:T(8,128)S(1)}, f32[64,512]{1,0:T(8,128)S(1)}, f32[64,512]{1,0:T(8,128)S(1)}, f32[64,1024]{1,0:T(8,128)S(1)}) custom-call(bf16[256,128]{1,0:T(8,128)(2,1)S(1)} %pad_maximum_fusion.1.rows, bf16[256,512]{1,0:T(8,128)(2,1)S(1)} %get-tuple-element.45.rest_0_, f32[1,512]{1,0:T(1,128)S(1)} %get-tuple-element.46.rest_1_, ...), custom_call_target="tpu_custom_call" | custom-call | flops 754974720 | bytes 1048576 | tf_op jit(solution)/shard_map/pallas_call | solution.py:76
  19.8 0.7 %collective-permute-done.8 = f16[128,128]{1,0:T(8,128)(2,1)S(1)} collective-permute-done((f16[128,128]{1,0:T(8,128)(2,1)S(1)}, f16[128,128]{1,0:T(8,128)(2,1)S(1)}, u32[]{:S(2)}, u32[]{:S(2)}) %collective-permute-start.8) | collective-permute-done | bytes 32800 | tf_op jit(solution)/shard_map/ppermute | solution.py:117
  20.5 0.2 collective-permute-start.10
  20.8 1.5 %collective-permute-start.9 = (f16[64,128]{1,0:T(8,128)(2,1)S(1)}, f16[64,128]{1,0:T(8,128)(2,1)S(1)}, u32[]{:S(2)}, u32[]{:S(2)}) collective-permute-start(f16[64,128]{1,0:T(8,128)(2,1)S(1)} %fusion), channel_id=1, source_target_pairs={{0,5},{1,4},{2,7},{3,6},{4,1},{5,0},{6,3},{7,2},{8,13},{9,12},{10,... | collective-permute-start | bytes 49160 | tf_op jit(solution)/shard_map/ppermute | solution.py:117
  22.3 0.0 collective-permute-done.10
  22.4 1.4 %collective-permute-start.12 = (f32[64,512]{1,0:T(8,128)S(1)}, f32[64,512]{1,0:T(8,128)S(1)}, u32[]{:S(2)}, u32[]{:S(2)}) collective-permute-start(f32[64,512]{1,0:T(8,128)S(1)} %get-tuple-element.70), channel_id=1, source_target_pairs={{0,12},{1,13},{2,14},{3,15},{4,8},{5,9},{6,10},{7,11},{8,4},{9,5},... | collective-permute-start | bytes 393224 | tf_op jit(solution)/shard_map/ppermute | solution.py:117
  23.8 0.3 collective-permute-done.9
  24.1 2.2 %collective-permute-start.11 = (f16[32,128]{1,0:T(8,128)(2,1)S(1)}, f16[32,128]{1,0:T(8,128)(2,1)S(1)}, u32[]{:S(2)}, u32[]{:S(2)}) collective-permute-start(f16[32,128]{1,0:T(8,128)(2,1)S(1)} %fusion.1), channel_id=1, source_target_pairs={{0,6},{1,7},{2,4},{3,5},{4,2},{5,3},{6,0},{7,1},{8,14},{9,15},{10,... | collective-permute-start | bytes 24584 | tf_op jit(solution)/shard_map/ppermute | solution.py:117
  26.9 1.2 %collective-permute-done.11 = f16[32,128]{1,0:T(8,128)(2,1)S(1)} collective-permute-done((f16[32,128]{1,0:T(8,128)(2,1)S(1)}, f16[32,128]{1,0:T(8,128)(2,1)S(1)}, u32[]{:S(2)}, u32[]{:S(2)}) %collective-permute-start.11) | collective-permute-done | bytes 8224 | tf_op jit(solution)/shard_map/ppermute | solution.py:117
  28.1 0.0 collective-permute-done.12.got_cols
  28.1 0.7 %shard_map.128 = (f32[64,512]{1,0:T(8,128)}, f32[64,64]{1,0:T(8,128)}) custom-call(f32[1]{0:T(128)S(6)} %copy.14.scale, f32[64,512]{1,0:T(8,128)S(1)} %get-tuple-element.63.own_cols, f32[64,512]{1,0:T(8,128)S(1)} %collective-permute-done.12.got_cols, f32[64,128]{1,0:T(8,128)S(1)} %slice_add_fusion.2.own_rows, f32[32,128]{1,0:T(8,128)S(1)} %convert_multiply_fusion.got_rows), custom_call_target="tpu_custom_call" | custom-call | flops 1000000 | bytes 1048576 | tf_op jit(solution)/shard_map/pallas_call | solution.py:76
  (14 shorter events, 0.1 us)
Async XLA Ops:
  1.4 5.9 %collective-permute-start = (bf16[64,128]{1,0:T(8,128)(2,1)S(1)}, bf16[64,128]{1,0:T(8,128)(2,1)S(1)}, u32[]{:S(2)}, u32[]{:S(2)}) collective-permute-start(bf16[64,128]{1,0:T(8,128)(2,1)S(1)} %pad_maximum_fusion.3), channel_id=1, source_target_pairs={{0,6},{1,7},{2,4},{3,5},{4,2},{5,3},{6,0},{7,1},{8,14},{9,15},{10,... | collective-permute-start | bytes 49160 | tf_op jit(solution)/shard_map/ppermute | solution.py:117
  4.9 7.8 %collective-permute-start.5 = (bf16[64,512]{1,0:T(8,128)(2,1)}, bf16[64,512]{1,0:T(8,128)(2,1)S(1)}, u32[]{:S(2)}, u32[]{:S(2)}) collective-permute-start(bf16[64,512]{1,0:T(8,128)(2,1)} %bitcast.6), channel_id=1, source_target_pairs={{0,12},{1,13},{2,14},{3,15},{4,8},{5,9},{6,10},{7,11},{8,4},{9,5},... | collective-permute-start | bytes 196616 | tf_op jit(solution)/shard_map/ppermute | solution.py:117
  6.7 6.1 %collective-permute-start.6 = (bf16[64,512]{1,0:T(8,128)(2,1)}, bf16[64,512]{1,0:T(8,128)(2,1)S(1)}, u32[]{:S(2)}, u32[]{:S(2)}) collective-permute-start(bf16[64,512]{1,0:T(8,128)(2,1)} %bitcast.7), channel_id=1, source_target_pairs={{0,4},{1,5},{2,6},{3,7},{4,0},{5,1},{6,2},{7,3},{8,12},{9,13},{10,... | collective-permute-start | bytes 196616 | tf_op jit(solution)/shard_map/ppermute | solution.py:117
  6.7 1.9 %copy-start = (bf16[512,512]{1,0:T(8,128)(2,1)S(1)}, bf16[512,512]{1,0:T(8,128)(2,1)}, u32[]{:S(2)}) copy-start(bf16[512,512]{1,0:T(8,128)(2,1)} %rest_11_.3) | copy-start | bytes 1572868
  6.7 1.9 %copy-start.1 = (bf16[512,256]{1,0:T(8,128)(2,1)S(1)}, bf16[512,256]{1,0:T(8,128)(2,1)}, u32[]{:S(2)}) copy-start(bf16[512,256]{1,0:T(8,128)(2,1)} %rest_13_.3) | copy-start | bytes 786436
  6.7 5.5 %collective-permute-start.3 = (bf16[64,512]{1,0:T(8,128)(2,1)}, bf16[64,512]{1,0:T(8,128)(2,1)S(1)}, u32[]{:S(2)}, u32[]{:S(2)}) collective-permute-start(bf16[64,512]{1,0:T(8,128)(2,1)} %bitcast.10), channel_id=1, source_target_pairs={{0,12},{1,13},{2,14},{3,15},{4,8},{5,9},{6,10},{7,11},{8,4},{9,5},... | collective-permute-start | bytes 196616 | tf_op jit(solution)/shard_map/ppermute | solution.py:117
  7.4 1.3 %copy-start.4 = (bf16[512,64]{0,1:T(8,128)(2,1)S(1)}, bf16[512,64]{0,1:T(8,128)(2,1)}, u32[]{:S(2)}) copy-start(bf16[512,64]{0,1:T(8,128)(2,1)} %param.12) | copy-start | bytes 196612
  7.4 1.3 %copy-start.6 = (f32[512]{0:T(512)S(1)}, f32[512]{0:T(512)}, u32[]{:S(2)}) copy-start(f32[512]{0:T(512)} %param.18) | copy-start | bytes 6148
  7.4 1.3 %copy-start.2 = (bf16[64,512]{1,0:T(8,128)(2,1)S(1)}, bf16[64,512]{1,0:T(8,128)(2,1)}, u32[]{:S(2)}) copy-start(bf16[64,512]{1,0:T(8,128)(2,1)} %rest_9_.3) | copy-start | bytes 196612
  7.4 3.6 %collective-permute-start.1 = (bf16[128,128]{1,0:T(8,128)(2,1)S(1)}, bf16[128,128]{1,0:T(8,128)(2,1)S(1)}, u32[]{:S(2)}, u32[]{:S(2)}) collective-permute-start(bf16[128,128]{1,0:T(8,128)(2,1)S(1)} %pad_maximum_fusion.2), channel_id=1, source_target_pairs={{0,5},{1,4},{2,7},{3,6},{4,1},{5,0},{6,3},{7,2},{8,13},{9,12},{10,... | collective-permute-start | bytes 98312 | tf_op jit(solution)/shard_map/ppermute | solution.py:117
  8.7 0.7 %copy-start.5 = (f32[512]{0:T(512)S(1)}, f32[512]{0:T(512)}, u32[]{:S(2)}) copy-start(f32[512]{0:T(512)} %param.16) | copy-start | bytes 6148
  8.7 0.7 %copy-start.7 = (f32[256]{0:T(256)S(1)}, f32[256]{0:T(256)}, u32[]{:S(2)}) copy-start(f32[256]{0:T(256)} %param.20) | copy-start | bytes 3076
  11.0 4.5 %collective-permute-start.2 = (bf16[256,128]{1,0:T(8,128)(2,1)S(1)}, bf16[256,128]{1,0:T(8,128)(2,1)S(1)}, u32[]{:S(2)}, u32[]{:S(2)}) collective-permute-start(bf16[256,128]{1,0:T(8,128)(2,1)S(1)} %pad_maximum_fusion.1.rows), channel_id=1, source_target_pairs={{0,20},{1,21},{2,22},{3,23},{4,16},{5,17},{6,18},{7,19},{8,28},{9,... | collective-permute-start | bytes 196616 | tf_op jit(solution)/shard_map/ppermute | solution.py:117
  12.2 1.7 %collective-permute-start.4 = (bf16[64,1024]{1,0:T(8,128)(2,1)S(1)}, bf16[64,1024]{1,0:T(8,128)(2,1)S(1)}, u32[]{:S(2)}, u32[]{:S(2)}) collective-permute-start(bf16[64,1024]{1,0:T(8,128)(2,1)S(1)} %pad_maximum_fusion), channel_id=1, source_target_pairs={{0,4},{1,5},{2,6},{3,7},{4,0},{5,1},{6,2},{7,3},{8,12},{9,13},{10,... | collective-permute-start | bytes 393224 | tf_op jit(solution)/shard_map/ppermute | solution.py:117
  12.7 1.3 %collective-permute-start.7 = (bf16[64,512]{1,0:T(8,128)(2,1)S(1)}, bf16[64,512]{1,0:T(8,128)(2,1)S(1)}, u32[]{:S(2)}, u32[]{:S(2)}) collective-permute-start(bf16[64,512]{1,0:T(8,128)(2,1)S(1)} %collective-permute-done.5.rest_5_), channel_id=1, source_target_pairs={{0,4},{1,5},{2,6},{3,7},{4,0},{5,1},{6,2},{7,3},{8,12},{9,13},{10,... | collective-permute-start | bytes 196616 | tf_op jit(solution)/shard_map/ppermute | solution.py:117
  14.0 1.5 %copy-start.3 = (bf16[512,64]{0,1:T(8,128)(2,1)S(1)}, bf16[512,64]{0,1:T(8,128)(2,1)}, u32[]{:S(2)}) copy-start(bf16[512,64]{0,1:T(8,128)(2,1)} %param.14) | copy-start | bytes 196612
  17.1 3.4 %collective-permute-start.8 = (f16[128,128]{1,0:T(8,128)(2,1)S(1)}, f16[128,128]{1,0:T(8,128)(2,1)S(1)}, u32[]{:S(2)}, u32[]{:S(2)}) collective-permute-start(f16[128,128]{1,0:T(8,128)(2,1)S(1)} %multiply_convert_fusion), channel_id=1, source_target_pairs={{0,20},{1,21},{2,22},{3,23},{4,16},{5,17},{6,18},{7,19},{8,28},{9,... | collective-permute-start | bytes 98312 | tf_op jit(solution)/shard_map/ppermute | solution.py:117
  20.5 1.8 %collective-permute-start.10 = (f32[64,1024]{1,0:T(8,128)S(1)}, f32[64,1024]{1,0:T(8,128)S(1)}, u32[]{:S(2)}, u32[]{:S(2)}) collective-permute-start(f32[64,1024]{1,0:T(8,128)S(1)} %get-tuple-element.62), channel_id=1, source_target_pairs={{0,4},{1,5},{2,6},{3,7},{4,0},{5,1},{6,2},{7,3},{8,12},{9,13},{10,... | collective-permute-start | bytes 786440 | tf_op jit(solution)/shard_map/ppermute | solution.py:117
  20.8 3.2 %collective-permute-start.9 = (f16[64,128]{1,0:T(8,128)(2,1)S(1)}, f16[64,128]{1,0:T(8,128)(2,1)S(1)}, u32[]{:S(2)}, u32[]{:S(2)}) collective-permute-start(f16[64,128]{1,0:T(8,128)(2,1)S(1)} %fusion), channel_id=1, source_target_pairs={{0,5},{1,4},{2,7},{3,6},{4,1},{5,0},{6,3},{7,2},{8,13},{9,12},{10,... | collective-permute-start | bytes 49160 | tf_op jit(solution)/shard_map/ppermute | solution.py:117
  22.4 5.7 %collective-permute-start.12 = (f32[64,512]{1,0:T(8,128)S(1)}, f32[64,512]{1,0:T(8,128)S(1)}, u32[]{:S(2)}, u32[]{:S(2)}) collective-permute-start(f32[64,512]{1,0:T(8,128)S(1)} %get-tuple-element.70), channel_id=1, source_target_pairs={{0,12},{1,13},{2,14},{3,15},{4,8},{5,9},{6,10},{7,11},{8,4},{9,5},... | collective-permute-start | bytes 393224 | tf_op jit(solution)/shard_map/ppermute | solution.py:117
  24.1 4.0 %collective-permute-start.11 = (f16[32,128]{1,0:T(8,128)(2,1)S(1)}, f16[32,128]{1,0:T(8,128)(2,1)S(1)}, u32[]{:S(2)}, u32[]{:S(2)}) collective-permute-start(f16[32,128]{1,0:T(8,128)(2,1)S(1)} %fusion.1), channel_id=1, source_target_pairs={{0,6},{1,7},{2,4},{3,5},{4,2},{5,3},{6,0},{7,1},{8,14},{9,15},{10,... | collective-permute-start | bytes 24584 | tf_op jit(solution)/shard_map/ppermute | solution.py:117
